TPU v7x, 32 devices: a whole 2x2x4 slice. The times are simulated.
32 devices in a mesh: scen: 8 (over y, x, core), arc: 4 (over z).
Axes of the slice: x: 2, y: 2, z: 4, core: 2. Of those that a mesh axis runs over, the one named last changes fastest.
Arguments:
- coupling: bfloat16 [512, 2048], P(None, 'arc'), may hold values from -0.125 to 0.125
- incidence: int32 [4, 16], P(None, 'arc'), may hold values 0 or 1
- arc_cost: float32 [2048], P('arc'), may hold values from -6 to 6
- capacity: float32 [2048], P('arc'), may hold values from 0.5 to 2
- demand: float32 [8, 512], P('scen'), may hold values from -4 to 4
- weights: int32 [8], P('scen'), may hold values from 8 to 1408, as said below
- fleet_slots: int32 [512], P('arc'), may hold values from 0 to 511, as said below
Outputs:
- flows: float32 [8, 2048], P('scen', 'arc')
- duals: float32 [8, 512], P('scen', 'arc')
- multipliers: float32 [8, 512], P('scen', 'arc')
- consensus: float32 [512], P('arc')
- spread: float32 [2], replicated
Inputs may be any that keep to these rules, and one draw needn't show every extreme that they name: `weights`: weight s is (8 + 2 s) times a power of two from 1 to 64. `fleet_slots`: within each aligned block of 128 entries (one arc block) the values are distinct positions inside that arc block.
All inputs are finite; a program needn't handle non-finite values. No bound on the sum of `incidence` on one device may be relied on, other than what follows from the above.
Results may differ from a plain program's by a relative error of at most 0.012.
Values may be sent and summed in bfloat16 or wider, within the bound.
No kernel may reach another device: no remote copies, remote signals or barrier semaphores. Data moves between devices by JAX's collectives and lax.ppermute only.
A program may use at most 64 MiB of HBM per device.

v0:
```python
import jax
import jax.numpy as jnp
from jax import lax
from jax.sharding import PartitionSpec as P

TILE = 128
ITERS = 4
ROUNDS = 2


primal_step = 0.9
dual_step = 0.9
penalty = 1.0


def weighted_total(value):
    return lax.psum(value, "scen")


def body(coupling, incidence, arc_cost, capacity, demand, weights, fleet_slots):
    total_rows, block_arcs = coupling.shape
    masked = (
        coupling.reshape(total_rows // TILE, TILE, block_arcs // TILE, TILE)
        * incidence.astype(jnp.bfloat16)[:, None, :, None]
    ).reshape(total_rows, block_arcs)
    blocks = lax.axis_size("arc")
    share_rows = total_rows // blocks
    first_row = lax.axis_index("arc") * share_rows
    demand_row = demand[0]
    own_demand = lax.dynamic_slice_in_dim(demand_row, first_row, share_rows, 0)
    shares = weights.astype(jnp.float32)[0]
    fleet_count = fleet_slots.shape[0] * blocks
    weight_sum = jnp.float32(1.0)
    weight_sum = lax.psum(shares, "scen")
    flows = jnp.zeros((block_arcs,), jnp.float32)
    duals = jnp.zeros((share_rows,), jnp.float32)
    multipliers = jnp.zeros(fleet_slots.shape, jnp.float32)
    consensus = jnp.zeros(fleet_slots.shape, jnp.float32)
    spreads = []
    for round_index in range(ROUNDS):
        for step_index in range(ITERS):
            dual_full = lax.all_gather(duals.astype(jnp.bfloat16), "arc", axis=0, tiled=True)
            dual_pull = jnp.dot(dual_full, masked, preferred_element_type=jnp.float32)
            fleet_push = multipliers + penalty * (flows[fleet_slots] - consensus)
            gradient = (arc_cost + dual_pull).at[fleet_slots].add(fleet_push)
            flows_next = jnp.clip(flows - primal_step * gradient, 0.0, capacity)
            flows_bar = (2.0 * flows_next - flows).astype(jnp.bfloat16)
            row_load = lax.psum_scatter(
                jnp.dot(masked, flows_bar, preferred_element_type=jnp.float32),
                "arc",
                scatter_dimension=0,
                tiled=True,
            )
            duals = jnp.maximum(duals + dual_step * (row_load - own_demand), 0.0)
            flows = flows_next
        fleet_flow = flows[fleet_slots]
        weighted = weighted_total(shares * fleet_flow)
        consensus = weighted / weight_sum
        deviation = fleet_flow - consensus
        local_square = shares * jnp.sum(deviation * deviation)
        square_sum = lax.psum(local_square, ("scen", "arc"))
        spreads.append(jnp.sqrt(square_sum / (weight_sum * fleet_count) + 1e-06))
        multipliers = multipliers + penalty * deviation
    return (flows[None, :], duals[None, :], multipliers[None, :], consensus, jnp.stack(spreads))


def solution(mesh):
    in_specs = (
        P(None, "arc"),
        P(None, "arc"),
        P("arc"),
        P("arc"),
        P("scen", None),
        P("scen"),
        P("arc"),
    )
    out_specs = (P("scen", "arc"), P("scen", "arc"), P("scen", "arc"), P("arc"), P())
    return jax.shard_map(body, mesh=mesh, in_specs=in_specs, out_specs=out_specs, check_vma=False)
```

profile of v0, /device:TPU:0, one launch (start us, length us, event | category | flops | bytes accessed | tf_op | source)
XLA Modules:
  0.0 242.4 jit_solution(13824858357344152260)
XLA Ops:
  0.6 0.7 convert_element_type.55
  1.9 0.5 copy-done.2
  2.5 0.6 copy-done.5
  3.1 1.3 gather_fusion
  4.4 1.4 scatter_fusion
  5.9 0.2 fusion.45
  6.1 13.4 %all-reduce = f32[512]{0:T(512)S(1)} all-reduce(f32[512]{0:T(512)S(1)} %bitcast.134), channel_id=2, replica_groups=mesh['scen'=8,'arc'=4] {'arc'}, use_global_device_ids=true, to_apply=%region_1.0.clone | all-reduce | flops 512 | bytes 4096
  19.5 0.7 copy-done.6
  20.2 0.6 dynamic-slice.1
  21.4 0.7 convert_bitcast_fusion.6
  22.2 7.5 %all-gather = bf16[4,1,128]{2,1,0:T(2,128)(2,1)S(1)} all-gather(bf16[1,1,128]{2,1,0:T(2,128)(2,1)S(1)} %get-tuple-element.40), channel_id=1, replica_groups=mesh['scen'=8,'arc'=4] {'arc'}, dimensions={0}, use_global_device_ids=true | all-gather | bytes 1280 | tf_op jit(solution)/shard_map/all_gather | solution.py:42
  29.9 1.3 gather_fusion.1
  31.1 1.4 scatter_fusion.1
  32.8 10.4 %all-reduce.1 = f32[512]{0:T(512)S(1)} all-reduce(f32[512]{0:T(512)S(1)} %bitcast.135), channel_id=3, replica_groups=mesh['scen'=8,'arc'=4] {'arc'}, use_global_device_ids=true, to_apply=%region_3.4.clone | all-reduce | flops 512 | bytes 4096
  43.3 7.5 %all-gather.1 = bf16[4,1,128]{2,1,0:T(2,128)(2,1)S(1)} all-gather(bf16[1,1,128]{2,1,0:T(2,128)(2,1)S(1)} %get-tuple-element.36), channel_id=1, replica_groups=mesh['scen'=8,'arc'=4] {'arc'}, dimensions={0}, use_global_device_ids=true | all-gather | bytes 1280 | tf_op jit(solution)/shard_map/all_gather | solution.py:42
  50.9 1.3 gather_fusion.2
  52.2 1.4 scatter_fusion.2
  53.9 10.4 %all-reduce.2 = f32[512]{0:T(512)S(1)} all-reduce(f32[512]{0:T(512)S(1)} %bitcast.136), channel_id=4, replica_groups=mesh['scen'=8,'arc'=4] {'arc'}, use_global_device_ids=true, to_apply=%region_5.6.clone | all-reduce | flops 512 | bytes 4096
  64.4 7.5 %all-gather.2 = bf16[4,1,128]{2,1,0:T(2,128)(2,1)S(1)} all-gather(bf16[1,1,128]{2,1,0:T(2,128)(2,1)S(1)} %get-tuple-element.32), channel_id=1, replica_groups=mesh['scen'=8,'arc'=4] {'arc'}, dimensions={0}, use_global_device_ids=true | all-gather | bytes 1280 | tf_op jit(solution)/shard_map/all_gather | solution.py:42
  72.0 1.3 gather_fusion.3
  73.3 1.4 scatter_fusion.3
  75.0 10.4 %all-reduce.3 = f32[512]{0:T(512)S(1)} all-reduce(f32[512]{0:T(512)S(1)} %bitcast.137), channel_id=5, replica_groups=mesh['scen'=8,'arc'=4] {'arc'}, use_global_device_ids=true, to_apply=%region_7.8.clone | all-reduce | flops 512 | bytes 4096
  85.5 7.5 %all-gather.3 = bf16[4,1,128]{2,1,0:T(2,128)(2,1)S(1)} all-gather(bf16[1,1,128]{2,1,0:T(2,128)(2,1)S(1)} %get-tuple-element.28), channel_id=1, replica_groups=mesh['scen'=8,'arc'=4] {'arc'}, dimensions={0}, use_global_device_ids=true | all-gather | bytes 1280 | tf_op jit(solution)/shard_map/all_gather | solution.py:42
  93.1 1.3 gather_fusion.4
  95.1 13.1 %all-reduce.9 = (f32[128]{0:T(128)S(1)}, f32[]{:T(128)}) all-reduce(f32[128]{0:T(128)S(1)} %broadcast_multiply_fusion.1, f32[]{:T(128)} %bitcast.14), channel_id=1, replica_groups=mesh['scen'=8,'arc'=4] {'scen'}, use_global_device_ids=true, to_apply=%region_8.9 | all-reduce | flops 129 | bytes 1032 | tf_op jit(solution)/shard_map/psum | solution.py:17
  108.2 1.3 multiply_reduce_fusion.1
  109.5 1.4 scatter_fusion.4
  111.2 10.4 %all-reduce.4 = f32[512]{0:T(512)S(1)} all-reduce(f32[512]{0:T(512)S(1)} %bitcast.138), channel_id=6, replica_groups=mesh['scen'=8,'arc'=4] {'arc'}, use_global_device_ids=true, to_apply=%region_11.12.clone | all-reduce | flops 512 | bytes 4096
  121.6 7.5 %all-gather.4 = bf16[4,1,128]{2,1,0:T(2,128)(2,1)S(1)} all-gather(bf16[1,1,128]{2,1,0:T(2,128)(2,1)S(1)} %get-tuple-element.24), channel_id=1, replica_groups=mesh['scen'=8,'arc'=4] {'arc'}, dimensions={0}, use_global_device_ids=true | all-gather | bytes 1280 | tf_op jit(solution)/shard_map/all_gather | solution.py:42
  129.3 1.3 gather_fusion.5
  130.6 1.4 scatter_fusion.5
  132.3 10.4 %all-reduce.5 = f32[512]{0:T(512)S(1)} all-reduce(f32[512]{0:T(512)S(1)} %bitcast.139), channel_id=7, replica_groups=mesh['scen'=8,'arc'=4] {'arc'}, use_global_device_ids=true, to_apply=%region_13.14.clone | all-reduce | flops 512 | bytes 4096
  142.7 7.5 %all-gather.5 = bf16[4,1,128]{2,1,0:T(2,128)(2,1)S(1)} all-gather(bf16[1,1,128]{2,1,0:T(2,128)(2,1)S(1)} %get-tuple-element.20), channel_id=1, replica_groups=mesh['scen'=8,'arc'=4] {'arc'}, dimensions={0}, use_global_device_ids=true | all-gather | bytes 1280 | tf_op jit(solution)/shard_map/all_gather | solution.py:42
  150.4 1.3 gather_fusion.6
  151.7 1.4 scatter_fusion.6
  153.4 10.4 %all-reduce.6 = f32[512]{0:T(512)S(1)} all-reduce(f32[512]{0:T(512)S(1)} %bitcast.140), channel_id=8, replica_groups=mesh['scen'=8,'arc'=4] {'arc'}, use_global_device_ids=true, to_apply=%region_15.16.clone | all-reduce | flops 512 | bytes 4096
  163.8 7.5 %all-gather.6 = bf16[4,1,128]{2,1,0:T(2,128)(2,1)S(1)} all-gather(bf16[1,1,128]{2,1,0:T(2,128)(2,1)S(1)} %get-tuple-element.16), channel_id=1, replica_groups=mesh['scen'=8,'arc'=4] {'arc'}, dimensions={0}, use_global_device_ids=true | all-gather | bytes 1280 | tf_op jit(solution)/shard_map/all_gather | solution.py:42
  171.5 1.3 gather_fusion.7
  172.8 1.4 scatter_fusion.7
  174.5 10.4 %all-reduce.7 = f32[512]{0:T(512)S(1)} all-reduce(f32[512]{0:T(512)S(1)} %bitcast.133), channel_id=9, replica_groups=mesh['scen'=8,'arc'=4] {'arc'}, use_global_device_ids=true, to_apply=%region_17.18.clone | all-reduce | flops 512 | bytes 4096
  184.9 0.6 maximum_bitcast_fusion
  185.5 1.3 gather_fusion.8
  186.7 11.8 %psum.37 = f32[128]{0:T(128)S(1)} all-reduce(f32[128]{0:T(128)S(1)} %broadcast_multiply_fusion), channel_id=1, replica_groups=mesh['scen'=8,'arc'=4] {'scen'}, use_global_device_ids=true, to_apply=%region_18.19 | all-reduce | flops 128 | bytes 1024 | tf_op jit(solution)/shard_map/psum | solution.py:17
  198.5 1.3 multiply_reduce_fusion
  199.9 0.5 copy-done.4
  200.4 0.5 add_bitcast_fusion
  202.1 37.7 %all-reduce.8 = (f32[]{:T(128)}, f32[]{:T(128)}) all-reduce(f32[]{:T(128)S(6)} %mul.147, f32[]{:T(128)S(6)} %mul.144), channel_id=1, replica_groups=mesh['scen'=8,'arc'=4] {'scen','arc'}, use_global_device_ids=true, to_apply=%region_22.23 | all-reduce | flops 2 | bytes 16 | tf_op jit(solution)/shard_map/psum | solution.py:61
  241.8 0.6 pad_maximum_fusion
  (66 shorter events, 4.1 us)
Async XLA Ops:
  0.6 1.1 copy-start.1
  1.8 0.7 copy-start.2
  2.4 0.7 copy-start.5
  4.4 1.4 copy-start.3
  19.5 0.7 copy-start.6
  174.2 11.2 %copy-start = (f32[512]{0:T(512)}, f32[512]{0:T(512)S(1)}, u32[]{:S(2)}) copy-start(f32[512]{0:T(512)S(1)} %get-tuple-element.15) | copy-start | bytes 6148
  199.9 0.5 copy-start.4
where the time goes:
time: 243 us; the launch traced here: 242 us
  blocking collectives  201 us (83%)
  other arithmetic  18 us (7%)
  local copies, waits for them, and re-layouts  14.8 us (6%)
  between operations  5.35 us (2%)
  matrix products  3.18 us (1%)
    unnamed x8, blocking collectives  86 us
    all_gather x7, blocking collectives, body(): lax.all_gather(duals.astype(jnp.bfloat16), 'arc', axis=0, tiled=True)  52.5 us
    psum x1, blocking collectives, body(): square_sum = lax.psum(local_square, ('scen', 'arc'))  37.7 us
    psum x2, blocking collectives, weighted_total(): return lax.psum(value, 'scen')  24.9 us
    scatter-add x8, other arithmetic, body(): gradient = (arc_cost + dual_pull).at[fleet_slots].add(fleet_push)  11.4 us
    gather x7, local copies, waits for them, and re-layouts, body(): fleet_push = multipliers + penalty * (flows[fleet_slots] - consensus)  8.94 us

commit v1 on v0

v1 whole, which is shorter than its diff:
```python
import functools

import jax
import jax.numpy as jnp
from jax import lax
from jax.experimental import pallas as pl
from jax.experimental.pallas import tpu as pltpu
from jax.sharding import PartitionSpec as P

TILE = 128
ITERS = 4
ROUNDS = 2
EXTRA = 16

primal_step = 0.9
dual_step = 0.9
penalty = 1.0

VMEM = pl.BlockSpec(memory_space=pltpu.VMEM)
SMEM = pl.BlockSpec(memory_space=pltpu.SMEM)
ANY = pl.BlockSpec(memory_space=pl.ANY)


def pieces(value):
    high = value.astype(jnp.bfloat16)
    rest = value - high.astype(jnp.float32)
    middle = rest.astype(jnp.bfloat16)
    low = (rest - middle.astype(jnp.float32)).astype(jnp.bfloat16)
    return high, middle, low


def one_hot(slots, block_arcs):
    arcs = lax.broadcasted_iota(jnp.int32, (block_arcs, slots.shape[1]), 0)
    return jnp.where(arcs == slots, 1.0, 0.0).astype(jnp.bfloat16)


def fleet_mask(slots, block_arcs):
    ones = jnp.ones((8, slots.shape[1]), jnp.bfloat16)
    hits = lax.dot_general(ones, one_hot(slots, block_arcs), (((1,), (1,)), ((), ())),
                           preferred_element_type=jnp.float32)
    return hits[:1]


def own_row(value, scen):
    rows = lax.broadcasted_iota(jnp.int32, value.shape, 0)
    return jnp.sum(jnp.where(rows == scen, value, 0.0), axis=0, keepdims=True)


def pack_kernel(coupling, incidence, arc_cost, capacity, demand, weights, slots,
                near, across, beyond, extra, rows_in, sems):
    total_rows, block_arcs = rows_in.shape
    half = TILE // 2
    scen = lax.axis_index("scen")
    chip, core = scen // 2, lax.rem(scen, 2)
    chips = total_rows // TILE
    copies = []
    for part in range(chips):
        first = pl.multiple_of(jnp.bitwise_xor(chip, part) * TILE, TILE)
        copies.append(pltpu.make_async_copy(
            coupling.at[pl.ds(first, TILE)], rows_in.at[pl.ds(part * TILE, TILE)], sems.at[part]))
    for copy in copies:
        copy.start()
    share = jnp.broadcast_to(weights[...].astype(jnp.float32), (1, 128))
    share = jnp.concatenate([*pieces(share), jnp.zeros((1, 128), jnp.bfloat16)], axis=1)
    mask = fleet_mask(slots[...], block_arcs)
    touch = []
    for part in range(chips):
        owner = jnp.bitwise_xor(chip, part)
        touch.append(jnp.concatenate(
            [jnp.full((1, TILE), incidence[owner, tile].astype(jnp.float32))
             for tile in range(block_arcs // TILE)], axis=1))
    lines = [*pieces(arc_cost[...]), *pieces(capacity[...]), mask, *pieces(demand[...]), share, *touch]
    lines = [line.astype(jnp.float32) for line in lines]
    lines += [jnp.zeros((1, block_arcs), jnp.float32)] * (EXTRA - len(lines))
    lines = jnp.concatenate(lines, axis=0).astype(jnp.bfloat16)
    extra[...] = lines
    across[TILE:, :] = lines
    beyond[half:, :] = lines
    for part in range(chips):
        copies[part].wait()
        rows = slice(part * TILE, (part + 1) * TILE)
        near[rows, :] = rows_in[rows, :] * touch[part].astype(jnp.bfloat16)
    across[:TILE, :] = near[(chips - 1) * TILE:, :]
    beyond[:half, :] = near[pl.ds(pl.multiple_of(core * half, half), half), :]


def rounds(masked, blocks, cost, cap, mask, demand, share, fleet_count, spread_out,
           flows, duals, prices, centre, shifted):
    scenarios, total_rows = demand.shape
    block_arcs = cost.shape[1] // blocks
    weight_sum = jnp.sum(share[:, :1])
    for round_index in range(ROUNDS):
        for step_index in range(ITERS):
            first = round_index == 0 and step_index == 0
            load = jnp.zeros((scenarios, total_rows), jnp.float32)
            if not first:
                duals_low = duals[...].astype(jnp.bfloat16)
            for block in range(blocks):
                cols = slice(block * block_arcs, (block + 1) * block_arcs)
                if first:
                    gradient = jnp.broadcast_to(cost[:, cols], (scenarios, block_arcs))
                    old = jnp.zeros((scenarios, block_arcs), jnp.float32)
                else:
                    old = flows[:, cols]
                    pull = jnp.dot(duals_low, masked(block), preferred_element_type=jnp.float32)
                    push = penalty * mask[:, cols] * old
                    if round_index > 0:
                        push = push + shifted[:, cols]
                    gradient = cost[:, cols] + pull + push
                new = jnp.clip(old - primal_step * gradient, 0.0, cap[:, cols])
                flows[:, cols] = new
                bar = (2.0 * new - old).astype(jnp.bfloat16)
                load = load + lax.dot_general(bar, masked(block), (((1,), (1,)), ((), ())),
                                              preferred_element_type=jnp.float32)
            step = dual_step * (load - demand[...])
            duals[...] = jnp.maximum(step if first else duals[...] + step, 0.0)
        squares = jnp.float32(0.0)
        for block in range(blocks):
            cols = slice(block * block_arcs, (block + 1) * block_arcs)
            fleet = flows[:, cols] * mask[:, cols]
            share_col = share[:, :1]
            mean = jnp.sum(share_col * fleet, axis=0, keepdims=True) / weight_sum
            gap = fleet - mean
            squares = squares + jnp.sum(share_col * gap * gap)
            total = penalty * gap if round_index == 0 else prices[:, cols] + penalty * gap
            prices[:, cols] = total
            centre[:, cols] = mean
            shifted[:, cols] = total - penalty * mean
        spread_out[round_index] = jnp.sqrt(squares / (weight_sum * fleet_count) + 1e-06)


def pick_fleet(price, mean, slots):
    picked = [line.astype(jnp.float32) for line in (*pieces(price), *pieces(mean))]
    picked += [jnp.zeros_like(price)] * 2
    picked = jnp.dot(jnp.concatenate(picked, axis=0).astype(jnp.bfloat16),
                     one_hot(slots, price.shape[1]), preferred_element_type=jnp.float32)
    return picked[0:1] + picked[1:2] + picked[2:3], picked[3:4] + picked[4:5] + picked[5:6]


def plain_kernel(masked, cost, cap, mask, demand, share, slots, flows_out, duals_out, mult_out, cons_out,
                 spread_out, flows, duals, prices, centre, shifted):
    blocks, total_rows, block_arcs = masked.shape
    rounds(lambda block: masked[block], blocks, cost, cap, mask, demand, share, slots.shape[1] * blocks,
           spread_out, flows, duals, prices, centre, shifted)
    scen, arc = lax.axis_index("scen"), lax.axis_index("arc")
    own = pl.ds(pl.multiple_of(arc * block_arcs, block_arcs), block_arcs)
    share_rows = total_rows // blocks
    own_rows = pl.ds(pl.multiple_of(arc * share_rows, share_rows), share_rows)
    flows_out[...] = own_row(flows[:, own], scen)
    duals_out[...] = own_row(duals[:, own_rows], scen)
    mult_out[...], cons_out[...] = pick_fleet(own_row(prices[:, own], scen), centre[:, own], slots[...])


def whole_kernel(near, *refs):
    lines, others = refs[:5], refs[5:10]
    (slots, flows_out, duals_out, mult_out, cons_out, spread_out,
     blocks_in, cost, cap, mask, demand_in, demand, share, flows, duals, prices, centre, shifted) = refs[10:]
    total_rows, block_arcs = near.shape
    scen, arc = lax.axis_index("scen"), lax.axis_index("arc")
    chip, core = scen // 2, lax.rem(scen, 2)
    chips = total_rows // TILE
    half = TILE // 2
    tails = [lines[0][TILE + half:, :], lines[3][TILE:, :], others[3][TILE:, :], lines[4][half:, :]]
    touch = []
    for block, tail in enumerate(tails):
        cols = slice(block * block_arcs, (block + 1) * block_arcs)
        tail = tail.astype(jnp.float32)
        cost[:, cols] = tail[0:1] + tail[1:2] + tail[2:3]
        cap[:, cols] = tail[3:4] + tail[4:5] + tail[5:6]
        mask[:, cols] = tail[6:7]
        touch.append(tail[11:11 + chips].astype(jnp.bfloat16))
    for row in range(2 * chips):
        part, source = row // 2, others if row % 2 else lines
        tail = source[part][TILE + half:, :] if part < chips - 1 else source[chips][half:, :]
        tail = tail.astype(jnp.float32)
        demand_in[row:row + 1, :] = tail[7:8] + tail[8:9] + tail[9:10]
        share[row:row + 1, :] = tail[10:11, :128] + tail[10:11, 128:256] + tail[10:11, 256:384]
    for part in range(chips):
        owner = jnp.bitwise_xor(chip, part)
        rows = slice(part * TILE, (part + 1) * TILE)
        demand[:, rows] = demand_in[:, pl.ds(pl.multiple_of(owner * TILE, TILE), TILE)]
        for side, source in enumerate((lines, others)):
            place = jnp.where(core == side, 0, half)
            place = pl.ds(pl.multiple_of(part * TILE + place, half), half)
            if part < chips - 1:
                blocks_in[side, rows, :] = source[part][:TILE, :] * touch[1 + side][part:part + 1]
                on = touch[3][chips - 1 - part:chips - part]
                blocks_in[2, place, :] = source[part][TILE:TILE + half, :] * on
            else:
                blocks_in[side, rows, :] = source[chips - 1][:TILE, :]
                blocks_in[2, place, :] = source[chips][:half, :]

    def masked(block):
        return near[...] if block == 0 else blocks_in[block - 1]

    rounds(masked, len(tails), cost, cap, mask, demand, share, slots.shape[1] * len(tails),
           spread_out, flows, duals, prices, centre, shifted)
    flows_out[...] = flows[0:1, :block_arcs]
    first = pl.multiple_of(jnp.bitwise_xor(chip, arc) * TILE, TILE)
    duals_out[...] = duals[:, pl.ds(first, TILE)][0:1]
    mult_out[...], cons_out[...] = pick_fleet(prices[0:1, :block_arcs], centre[:, :block_arcs], slots[...])


def swap(value, partner):
    scenarios, blocks = lax.axis_size("scen"), lax.axis_size("arc")
    pairs = []
    for scen in range(scenarios):
        for arc in range(blocks):
            other_scen, other_arc = partner(scen, arc)
            pairs.append((scen * blocks + arc, other_scen * blocks + other_arc))
    return lax.ppermute(value, ("scen", "arc"), pairs)


def bring(coupling, across, beyond, extra):
    scen = lax.axis_index("scen")
    half = TILE // 2
    wide = lax.dynamic_slice_in_dim(coupling, lax.shift_right_logical(scen, 1) * TILE, TILE, 0)
    wide = lax.optimization_barrier(wide)
    narrow = lax.dynamic_slice_in_dim(wide, (scen & 1) * half, half, 0)
    wide = swap(wide, lambda scen, arc: (scen, arc ^ (1 + scen % 2)))
    narrow = swap(narrow, lambda scen, arc: (scen, arc ^ 3))
    beyond = swap(beyond, lambda scen, arc: (scen ^ 6, arc ^ 3))
    line = jnp.concatenate([wide, narrow, extra], axis=0)
    line, across = lax.optimization_barrier((line, across))
    side = swap(line, lambda scen, arc: (scen ^ 2, arc))
    front = swap(line, lambda scen, arc: (scen ^ 4, arc))
    across = swap(across, lambda scen, arc: (scen, arc ^ (1 + scen % 2)))
    brought = [line, side, front, across, beyond]
    return brought + [swap(value, lambda scen, arc: (scen ^ 1, arc)) for value in brought]


def body(coupling, incidence, arc_cost, capacity, demand, weights, fleet_slots):
    total_rows, block_arcs = coupling.shape
    scenarios, blocks = lax.axis_size("scen"), lax.axis_size("arc")
    arcs = blocks * block_arcs
    fleet_block = fleet_slots.shape[0]
    row = lambda value: value.reshape(1, -1)
    slots = row(fleet_slots)
    out_shape = (
        jax.ShapeDtypeStruct((1, block_arcs), jnp.float32),
        jax.ShapeDtypeStruct((1, total_rows // blocks), jnp.float32),
        jax.ShapeDtypeStruct((1, fleet_block), jnp.float32),
        jax.ShapeDtypeStruct((1, fleet_block), jnp.float32),
        jax.ShapeDtypeStruct((ROUNDS,), jnp.float32),
    )
    out_specs = (VMEM, VMEM, VMEM, VMEM, SMEM)
    state = [
        pltpu.VMEM((scenarios, arcs), jnp.float32),
        pltpu.VMEM((scenarios, total_rows), jnp.float32),
        pltpu.VMEM((scenarios, arcs), jnp.float32),
        pltpu.VMEM((1, arcs), jnp.float32),
        pltpu.VMEM((scenarios, arcs), jnp.float32),
    ]
    limit = lambda mib: pltpu.CompilerParams(vmem_limit_bytes=mib * 1024 * 1024)
    cost = pl.CostEstimate(
        flops=4 * ROUNDS * ITERS * scenarios * total_rows * arcs,
        bytes_accessed=2 * total_rows * arcs,
        transcendentals=0,
    )
    fits = (scenarios, blocks) == (8, 4)
    if fits and total_rows == TILE * 4:
        like = lambda rows: jax.ShapeDtypeStruct((rows, block_arcs), jnp.bfloat16)
        near, across, beyond, extra = pl.pallas_call(
            pack_kernel,
            out_shape=(like(total_rows), like(TILE + EXTRA), like(TILE // 2 + EXTRA), like(EXTRA)),
            in_specs=[ANY, SMEM, VMEM, VMEM, VMEM, VMEM, VMEM],
            out_specs=(VMEM,) * 4,
            scratch_shapes=[
                pltpu.VMEM((total_rows, block_arcs), jnp.bfloat16),
                pltpu.SemaphoreType.DMA((total_rows // TILE,)),
            ],
            compiler_params=limit(8),
            name="pack",
        )(coupling, incidence, row(arc_cost), row(capacity), demand, weights.reshape(1, 1), slots)
        brought = bring(coupling, across, beyond, extra)
        outs = pl.pallas_call(
            whole_kernel,
            out_shape=out_shape,
            in_specs=[VMEM] * (len(brought) + 2),
            out_specs=out_specs,
            scratch_shapes=[
                pltpu.VMEM((blocks - 1, total_rows, block_arcs), jnp.bfloat16),
                pltpu.VMEM((1, arcs), jnp.float32),
                pltpu.VMEM((1, arcs), jnp.float32),
                pltpu.VMEM((1, arcs), jnp.float32),
                pltpu.VMEM((scenarios, total_rows), jnp.float32),
                pltpu.VMEM((scenarios, total_rows), jnp.float32),
                pltpu.VMEM((scenarios, 128), jnp.float32),
                *state,
            ],
            compiler_params=limit(16),
            cost_estimate=cost,
            name="whole",
        )(near, *brought, slots)
    else:
        masked = (
            coupling.reshape(total_rows // TILE, TILE, block_arcs // TILE, TILE)
            * incidence.astype(jnp.bfloat16)[:, None, :, None]
        ).reshape(total_rows, block_arcs)
        masked = lax.all_gather(masked, "arc")
        own_mask = jnp.zeros((block_arcs,), jnp.float32).at[fleet_slots].set(1.0)
        per_arc = lax.all_gather(jnp.stack([arc_cost, capacity, own_mask]), "arc", axis=1, tiled=True)
        shares = jnp.broadcast_to(weights.astype(jnp.float32)[:, None], (1, 128))
        per_scen = lax.all_gather(jnp.concatenate([demand, shares], axis=1), "scen", tiled=True)
        outs = pl.pallas_call(
            plain_kernel,
            out_shape=out_shape,
            in_specs=[VMEM] * 7,
            out_specs=out_specs,
            scratch_shapes=state,
            compiler_params=limit(48),
            cost_estimate=cost,
            name="whole",
        )(masked, per_arc[0:1], per_arc[1:2], per_arc[2:3], per_scen[:, :total_rows],
          per_scen[:, total_rows:], slots)
    flows, duals, multipliers, consensus, spread = outs
    return flows, duals, multipliers, consensus.reshape(-1), spread


def solution(mesh):
    in_specs = (
        P(None, "arc"),
        P(None, "arc"),
        P("arc"),
        P("arc"),
        P("scen", None),
        P("scen"),
        P("arc"),
    )
    out_specs = (P("scen", "arc"), P("scen", "arc"), P("scen", "arc"), P("arc"), P())
    return jax.shard_map(body, mesh=mesh, in_specs=in_specs, out_specs=out_specs, check_vma=False)
```

time: 243 us -> 37.8 us (0.16)
  blocking collectives: 201 us -> 0 us
  other arithmetic: 18 us -> 0.02 us
  starting transfers between devices: 0 us -> 14.8 us
  local copies, waits for them, and re-layouts: 14.8 us -> 2.63 us
  Pallas kernels: 0 us -> 9.6 us
  waiting for transfers between devices: 0 us -> 9.16 us
  between operations: 5.35 us -> 1.37 us
  matrix products: 3.18 us -> 0 us
    unnamed x8 -> x0, blocking collectives: 86 us -> none
    psum x3 -> x0, blocking collectives: 62.6 us -> none  [the longest x1 37.7 us: body(): square_sum = lax.psum(local_square, ('scen', 'arc'))]
    all_gather x7 -> x0, blocking collectives: 52.5 us -> none  [body(): lax.all_gather(duals.astype(jnp.bfloat16), 'arc', axis=0, tiled=True)]
    ppermute x0 -> x11, starting transfers between devices: none -> 14.8 us  [swap(): return lax.ppermute(value, ('scen', 'arc'), pairs)]
    gather x9 -> x0, local copies, waits for them, and re-layouts: 11.5 us -> none  [the longest x7 8.94 us: body(): fleet_push = multipliers + penalty * (flows[fleet_slots] - consensus)]
    scatter-add x8 -> x0, other arithmetic: 11.4 us -> none  [body(): gradient = (arc_cost + dual_pull).at[fleet_slots].add(fleet_push)]
    pallas_call x0 -> x2, Pallas kernels: none -> 9.6 us  [the longest x1 8.07 us: body(): pl.pallas_call(whole_kernel, out_shape=out_shape, in_specs=[VMEM] * (len(...]
    ppermute x0 -> x11, waiting for transfers between devices: none -> 9.16 us  [swap(): return lax.ppermute(value, ('scen', 'arc'), pairs)]
  transfers between devices with their start and end apart: 0 -> 11, of which waited for: 0 -> 5; matrix products, arithmetic and copies ran while one was open for 0% -> 0% of each run, Pallas kernels for 0% -> 4%
where the time goes in v1:
time: 37.8 us; the launch traced here: 37.6 us
  starting transfers between devices  14.8 us (39%)
  Pallas kernels  9.6 us (25%)
  waiting for transfers between devices  9.16 us (24%)
  local copies, waits for them, and re-layouts  2.63 us (7%)
  between operations  1.37 us (4%)
    ppermute x11, starting transfers between devices, swap(): return lax.ppermute(value, ('scen', 'arc'), pairs)  14.8 us
    ppermute x11, waiting for transfers between devices, swap(): return lax.ppermute(value, ('scen', 'arc'), pairs)  9.16 us
    pallas_call x1, Pallas kernels, body(): pl.pallas_call(whole_kernel, out_shape=out_shape, in_specs=[VMEM] * (len(...  8.07 us
    unnamed x12, local copies, waits for them, and re-layouts  1.71 us
    pallas_call x1, Pallas kernels, body(): pl.pallas_call(pack_kernel, out_shape=(like(total_rows), like(TILE + EXTR...  1.53 us
    dynamic_slice x1, local copies, waits for them, and re-layouts, bring(): lax.dynamic_slice_in_dim(coupling, lax.shift_right_logical(scen, 1) * TIL...  0.92 us
  transfers between devices with their start and end apart: 11, of which 5 were waited for; matrix products, arithmetic and copies ran while one was open for 0% of the time, Pallas kernels for 4%

profile of v1, /device:TPU:0, one launch (start us, length us, event | category | flops | bytes accessed | tf_op | source)
XLA Modules:
  0.0 37.6 jit_solution(15984267641511057440)
XLA Ops:
  0.6 0.9 %constant_dynamic-slice_fusion.1 = bf16[128,512]{1,0:T(8,128)(2,1)S(1)} fusion(bf16[512,512]{1,0:T(8,128)(2,1)} %coupling.1, s32[]{:T(128)S(6)} %select_n.6), kind=kLoop, calls=%fused_computation.2 | loop fusion | bytes 262148 | tf_op jit(solution)/shard_map/dynamic_slice | solution.py:217
  1.6 3.1 %collective-permute-start = (bf16[128,512]{1,0:T(8,128)(2,1)S(1)}, bf16[128,512]{1,0:T(8,128)(2,1)S(1)}, u32[]{:S(2)}, u32[]{:S(2)}) collective-permute-start(bf16[128,512]{1,0:T(8,128)(2,1)S(1)} %constant_dynamic-slice_fusion.1), channel_id=1, source_target_pairs={{0,1},{1,0},{2,3},{3,2},{4,6},{5,7},{6,4},{7,5},{8,9},{9,8},{10,11... | collective-permute-start | bytes 393224 | tf_op jit(solution)/shard_map/ppermute | solution.py:211
  4.6 0.0 copy-start.3
  4.6 0.0 copy-start.4
  4.7 2.5 %collective-permute-start.1 = (bf16[64,512]{1,0:T(8,128)(2,1)S(1)}, bf16[64,512]{1,0:T(8,128)(2,1)S(1)}, u32[]{:S(2)}, u32[]{:S(2)}) collective-permute-start(bf16[64,512]{1,0:T(8,128)(2,1)S(1)} %constant_dynamic-slice_fusion), channel_id=1, source_target_pairs={{0,3},{1,2},{2,1},{3,0},{4,7},{5,6},{6,5},{7,4},{8,11},{9,10},{10,... | collective-permute-start | bytes 196616 | tf_op jit(solution)/shard_map/ppermute | solution.py:211
  7.9 0.0 copy-start.2
  7.9 0.0 copy-start.1
  7.9 0.0 copy-start.5
  7.9 0.0 copy-done.3
  7.9 0.0 copy-done.4
  7.9 0.6 %copy-done.2 = f32[512]{0:T(512)S(1)} copy-done((f32[512]{0:T(512)S(1)}, f32[512]{0:T(512)}, u32[]{:S(2)}) %copy-start.2) | copy-done | bytes 2072
  8.5 0.0 copy-done.1
  8.6 0.0 copy-done.5
  8.6 0.0 copy-start
  8.6 1.0 %copy-done = bf16[512,512]{1,0:T(8,128)(2,1)S(1)} copy-done((bf16[512,512]{1,0:T(8,128)(2,1)S(1)}, bf16[512,512]{1,0:T(8,128)(2,1)}, u32[]{:S(2)}) %copy-start) | copy-done | bytes 524312
  9.6 1.5 %pack.1 = (bf16[512,512]{1,0:T(8,128)(2,1)S(1)}, bf16[144,512]{1,0:T(8,128)(2,1)S(1)}, bf16[80,512]{1,0:T(8,128)(2,1)S(1)}, bf16[16,512]{1,0:T(8,128)(2,1)S(1)}) custom-call(bf16[512,512]{1,0:T(8,128)(2,1)S(1)} %copy-done, s32[4,4]{1,0:T(4,128)S(1)} %copy-done.1, f32[1,512]{1,0:T(1,128)S(1)} %bitcast.6, f32[1,512]{1,0:T(1,128)S(1)} %bitcast.7, ...), custom_call_target="tpu_custom_call" | custom-call | tf_op jit(solution)/shard_map/pack/pallas_call | solution.py:263
  11.1 0.6 %collective-permute-done.1 = bf16[64,512]{1,0:T(8,128)(2,1)S(1)} collective-permute-done((bf16[64,512]{1,0:T(8,128)(2,1)S(1)}, bf16[64,512]{1,0:T(8,128)(2,1)S(1)}, u32[]{:S(2)}, u32[]{:S(2)}) %collective-permute-start.1) | collective-permute-done | bytes 65568 | tf_op jit(solution)/shard_map/ppermute | solution.py:211
  11.8 0.0 collective-permute-done
  11.8 1.6 %collective-permute-start.3 = (bf16[208,512]{1,0:T(8,128)(2,1)S(1)}, bf16[208,512]{1,0:T(8,128)(2,1)S(1)}, u32[]{:S(2)}, u32[]{:S(2)}) collective-permute-start(bf16[208,512]{1,0:T(8,128)(2,1)S(1)} %pad_maximum_fusion.refs_0_), channel_id=1, source_target_pairs={{0,16},{1,17},{2,18},{3,19},{4,20},{5,21},{6,22},{7,23},{8,24},{9,... | collective-permute-start | bytes 638984 | tf_op jit(solution)/shard_map/ppermute | solution.py:211
  13.4 1.5 %collective-permute-start.2 = (bf16[208,512]{1,0:T(8,128)(2,1)S(1)}, bf16[208,512]{1,0:T(8,128)(2,1)S(1)}, u32[]{:S(2)}, u32[]{:S(2)}) collective-permute-start(bf16[208,512]{1,0:T(8,128)(2,1)S(1)} %pad_maximum_fusion.refs_0_), channel_id=1, source_target_pairs={{0,8},{1,9},{2,10},{3,11},{4,12},{5,13},{6,14},{7,15},{8,0},{9,1},... | collective-permute-start | bytes 638984 | tf_op jit(solution)/shard_map/ppermute | solution.py:211
  14.9 0.6 %collective-permute-start.4 = (bf16[144,512]{1,0:T(8,128)(2,1)S(1)}, bf16[144,512]{1,0:T(8,128)(2,1)S(1)}, u32[]{:S(2)}, u32[]{:S(2)}) collective-permute-start(bf16[144,512]{1,0:T(8,128)(2,1)S(1)} %get-tuple-element.20), channel_id=1, source_target_pairs={{0,1},{1,0},{2,3},{3,2},{4,6},{5,7},{6,4},{7,5},{8,9},{9,8},{10,11... | collective-permute-start | bytes 442376 | tf_op jit(solution)/shard_map/ppermute | solution.py:211
  15.5 1.2 %collective-permute-start.6 = (bf16[208,512]{1,0:T(8,128)(2,1)S(1)}, bf16[208,512]{1,0:T(8,128)(2,1)S(1)}, u32[]{:S(2)}, u32[]{:S(2)}) collective-permute-start(bf16[208,512]{1,0:T(8,128)(2,1)S(1)} %pad_maximum_fusion.refs_0_), channel_id=1, source_target_pairs={{0,4},{1,5},{2,6},{3,7},{4,0},{5,1},{6,2},{7,3},{8,12},{9,13},{10,... | collective-permute-start | bytes 638984 | tf_op jit(solution)/shard_map/ppermute | solution.py:211
  16.7 1.8 %collective-permute-done.3.refs_2_ = bf16[208,512]{1,0:T(8,128)(2,1)S(1)} collective-permute-done((bf16[208,512]{1,0:T(8,128)(2,1)S(1)}, bf16[208,512]{1,0:T(8,128)(2,1)S(1)}, u32[]{:S(2)}, u32[]{:S(2)}) %collective-permute-start.3) | collective-permute-done | bytes 213024 | tf_op jit(solution)/shard_map/ppermute | solution.py:211
  18.4 0.0 collective-permute-start.8
  18.5 1.2 %collective-permute-done.2.refs_1_ = bf16[208,512]{1,0:T(8,128)(2,1)S(1)} collective-permute-done((bf16[208,512]{1,0:T(8,128)(2,1)S(1)}, bf16[208,512]{1,0:T(8,128)(2,1)S(1)}, u32[]{:S(2)}, u32[]{:S(2)}) %collective-permute-start.2) | collective-permute-done | bytes 213024 | tf_op jit(solution)/shard_map/ppermute | solution.py:211
  19.7 0.0 collective-permute-start.7
  19.7 4.3 %collective-permute-start.5 = (bf16[80,512]{1,0:T(8,128)(2,1)S(1)}, bf16[80,512]{1,0:T(8,128)(2,1)S(1)}, u32[]{:S(2)}, u32[]{:S(2)}) collective-permute-start(bf16[80,512]{1,0:T(8,128)(2,1)S(1)} %get-tuple-element.21), channel_id=1, source_target_pairs={{0,27},{1,26},{2,25},{3,24},{4,31},{5,30},{6,29},{7,28},{8,19},{9,... | collective-permute-start | bytes 245768 | tf_op jit(solution)/shard_map/ppermute | solution.py:211
  24.0 0.0 collective-permute-done.4.refs_3_
  24.0 0.0 collective-permute-start.9
  24.0 4.2 %collective-permute-done.5.refs_4_ = bf16[80,512]{1,0:T(8,128)(2,1)S(1)} collective-permute-done((bf16[80,512]{1,0:T(8,128)(2,1)S(1)}, bf16[80,512]{1,0:T(8,128)(2,1)S(1)}, u32[]{:S(2)}, u32[]{:S(2)}) %collective-permute-start.5) | collective-permute-done | bytes 81952 | tf_op jit(solution)/shard_map/ppermute | solution.py:211
  28.2 0.0 collective-permute-start.10
  28.3 1.3 %collective-permute-done.10.refs_9_ = bf16[80,512]{1,0:T(8,128)(2,1)S(1)} collective-permute-done((bf16[80,512]{1,0:T(8,128)(2,1)S(1)}, bf16[80,512]{1,0:T(8,128)(2,1)S(1)}, u32[]{:S(2)}, u32[]{:S(2)}) %collective-permute-start.10) | collective-permute-done | bytes 81952 | tf_op jit(solution)/shard_map/ppermute | solution.py:211
  29.5 0.0 collective-permute-done.6.refs_5_
  29.5 0.0 collective-permute-done.9.refs_8_
  29.5 0.0 collective-permute-done.8.refs_7_
  29.5 0.0 collective-permute-done.7.refs_6_
  29.6 8.1 %whole.1 = (f32[1,512]{1,0:T(1,128)}, f32[1,128]{1,0:T(1,128)}, f32[1,128]{1,0:T(1,128)}, f32[1,128]{1,0:T(1,128)}, f32[2]{0:T(128)}) custom-call(bf16[512,512]{1,0:T(8,128)(2,1)S(1)} %get-tuple-element.16.near, bf16[208,512]{1,0:T(8,128)(2,1)S(1)} %pad_maximum_fusion.refs_0_, bf16[208,512]{1,0:T(8,128)(2,1)S(1)} %collective-permute-done.2.refs_1_, ...), custom_call_target="tpu_custom_call" | custom-call | flops 268435456 | bytes 2097152 | tf_op jit(solution)/shard_map/whole/pallas_call | solution.py:276
  (2 shorter events, 0.0 us)
Async XLA Ops:
  1.6 10.2 %collective-permute-start = (bf16[128,512]{1,0:T(8,128)(2,1)S(1)}, bf16[128,512]{1,0:T(8,128)(2,1)S(1)}, u32[]{:S(2)}, u32[]{:S(2)}) collective-permute-start(bf16[128,512]{1,0:T(8,128)(2,1)S(1)} %constant_dynamic-slice_fusion.1), channel_id=1, source_target_pairs={{0,1},{1,0},{2,3},{3,2},{4,6},{5,7},{6,4},{7,5},{8,9},{9,8},{10,11... | collective-permute-start | bytes 393224 | tf_op jit(solution)/shard_map/ppermute | solution.py:211
  4.6 3.2 %copy-start.3 = (f32[512]{0:T(512)S(1)}, f32[512]{0:T(512)}, u32[]{:S(2)}) copy-start(f32[512]{0:T(512)} %param.10) | copy-start | bytes 6148
  4.6 3.3 %copy-start.4 = (f32[1,512]{1,0:T(1,128)S(1)}, f32[1,512]{1,0:T(1,128)}, u32[]{:S(2)}) copy-start(f32[1,512]{1,0:T(1,128)} %demand.1) | copy-start | bytes 6148
  4.7 7.1 %collective-permute-start.1 = (bf16[64,512]{1,0:T(8,128)(2,1)S(1)}, bf16[64,512]{1,0:T(8,128)(2,1)S(1)}, u32[]{:S(2)}, u32[]{:S(2)}) collective-permute-start(bf16[64,512]{1,0:T(8,128)(2,1)S(1)} %constant_dynamic-slice_fusion), channel_id=1, source_target_pairs={{0,3},{1,2},{2,1},{3,0},{4,7},{5,6},{6,5},{7,4},{8,11},{9,10},{10,... | collective-permute-start | bytes 196616 | tf_op jit(solution)/shard_map/ppermute | solution.py:211
  7.9 0.7 %copy-start.2 = (f32[512]{0:T(512)S(1)}, f32[512]{0:T(512)}, u32[]{:S(2)}) copy-start(f32[512]{0:T(512)} %param.9) | copy-start | bytes 6148
  7.9 0.7 %copy-start.1 = (s32[4,4]{1,0:T(4,128)S(1)}, s32[4,4]{1,0:T(4,128)}, u32[]{:S(2)}) copy-start(s32[4,4]{1,0:T(4,128)} %incidence.1) | copy-start | bytes 196
  7.9 0.7 %copy-start.5 = (s32[128]{0:T(128)S(1)}, s32[128]{0:T(128)}, u32[]{:S(2)}) copy-start(s32[128]{0:T(128)} %param.13) | copy-start | bytes 1540
  8.6 1.0 %copy-start = (bf16[512,512]{1,0:T(8,128)(2,1)S(1)}, bf16[512,512]{1,0:T(8,128)(2,1)}, u32[]{:S(2)}) copy-start(bf16[512,512]{1,0:T(8,128)(2,1)} %coupling.1) | copy-start | bytes 1572868
  11.8 6.7 %collective-permute-start.3 = (bf16[208,512]{1,0:T(8,128)(2,1)S(1)}, bf16[208,512]{1,0:T(8,128)(2,1)S(1)}, u32[]{:S(2)}, u32[]{:S(2)}) collective-permute-start(bf16[208,512]{1,0:T(8,128)(2,1)S(1)} %pad_maximum_fusion.refs_0_), channel_id=1, source_target_pairs={{0,16},{1,17},{2,18},{3,19},{4,20},{5,21},{6,22},{7,23},{8,24},{9,... | collective-permute-start | bytes 638984 | tf_op jit(solution)/shard_map/ppermute | solution.py:211
  13.4 6.3 %collective-permute-start.2 = (bf16[208,512]{1,0:T(8,128)(2,1)S(1)}, bf16[208,512]{1,0:T(8,128)(2,1)S(1)}, u32[]{:S(2)}, u32[]{:S(2)}) collective-permute-start(bf16[208,512]{1,0:T(8,128)(2,1)S(1)} %pad_maximum_fusion.refs_0_), channel_id=1, source_target_pairs={{0,8},{1,9},{2,10},{3,11},{4,12},{5,13},{6,14},{7,15},{8,0},{9,1},... | collective-permute-start | bytes 638984 | tf_op jit(solution)/shard_map/ppermute | solution.py:211
  14.9 9.1 %collective-permute-start.4 = (bf16[144,512]{1,0:T(8,128)(2,1)S(1)}, bf16[144,512]{1,0:T(8,128)(2,1)S(1)}, u32[]{:S(2)}, u32[]{:S(2)}) collective-permute-start(bf16[144,512]{1,0:T(8,128)(2,1)S(1)} %get-tuple-element.20), channel_id=1, source_target_pairs={{0,1},{1,0},{2,3},{3,2},{4,6},{5,7},{6,4},{7,5},{8,9},{9,8},{10,11... | collective-permute-start | bytes 442376 | tf_op jit(solution)/shard_map/ppermute | solution.py:211
  15.5 14.1 %collective-permute-start.6 = (bf16[208,512]{1,0:T(8,128)(2,1)S(1)}, bf16[208,512]{1,0:T(8,128)(2,1)S(1)}, u32[]{:S(2)}, u32[]{:S(2)}) collective-permute-start(bf16[208,512]{1,0:T(8,128)(2,1)S(1)} %pad_maximum_fusion.refs_0_), channel_id=1, source_target_pairs={{0,4},{1,5},{2,6},{3,7},{4,0},{5,1},{6,2},{7,3},{8,12},{9,13},{10,... | collective-permute-start | bytes 638984 | tf_op jit(solution)/shard_map/ppermute | solution.py:211
  18.4 11.1 %collective-permute-start.8 = (bf16[208,512]{1,0:T(8,128)(2,1)S(1)}, bf16[208,512]{1,0:T(8,128)(2,1)S(1)}, u32[]{:S(2)}, u32[]{:S(2)}) collective-permute-start(bf16[208,512]{1,0:T(8,128)(2,1)S(1)} %collective-permute-done.3.refs_2_), channel_id=1, source_target_pairs={{0,4},{1,5},{2,6},{3,7},{4,0},{5,1},{6,2},{7,3},{8,12},{9,13},{10,... | collective-permute-start | bytes 638984 | tf_op jit(solution)/shard_map/ppermute | solution.py:211
  19.7 9.9 %collective-permute-start.7 = (bf16[208,512]{1,0:T(8,128)(2,1)S(1)}, bf16[208,512]{1,0:T(8,128)(2,1)S(1)}, u32[]{:S(2)}, u32[]{:S(2)}) collective-permute-start(bf16[208,512]{1,0:T(8,128)(2,1)S(1)} %collective-permute-done.2.refs_1_), channel_id=1, source_target_pairs={{0,4},{1,5},{2,6},{3,7},{4,0},{5,1},{6,2},{7,3},{8,12},{9,13},{10,... | collective-permute-start | bytes 638984 | tf_op jit(solution)/shard_map/ppermute | solution.py:211
  19.7 8.6 %collective-permute-start.5 = (bf16[80,512]{1,0:T(8,128)(2,1)S(1)}, bf16[80,512]{1,0:T(8,128)(2,1)S(1)}, u32[]{:S(2)}, u32[]{:S(2)}) collective-permute-start(bf16[80,512]{1,0:T(8,128)(2,1)S(1)} %get-tuple-element.21), channel_id=1, source_target_pairs={{0,27},{1,26},{2,25},{3,24},{4,31},{5,30},{6,29},{7,28},{8,19},{9,... | collective-permute-start | bytes 245768 | tf_op jit(solution)/shard_map/ppermute | solution.py:211
  24.0 5.5 %collective-permute-start.9 = (bf16[144,512]{1,0:T(8,128)(2,1)S(1)}, bf16[144,512]{1,0:T(8,128)(2,1)S(1)}, u32[]{:S(2)}, u32[]{:S(2)}) collective-permute-start(bf16[144,512]{1,0:T(8,128)(2,1)S(1)} %collective-permute-done.4.refs_3_), channel_id=1, source_target_pairs={{0,4},{1,5},{2,6},{3,7},{4,0},{5,1},{6,2},{7,3},{8,12},{9,13},{10,... | collective-permute-start | bytes 442376 | tf_op jit(solution)/shard_map/ppermute | solution.py:211
  28.2 1.3 %collective-permute-start.10 = (bf16[80,512]{1,0:T(8,128)(2,1)S(1)}, bf16[80,512]{1,0:T(8,128)(2,1)S(1)}, u32[]{:S(2)}, u32[]{:S(2)}) collective-permute-start(bf16[80,512]{1,0:T(8,128)(2,1)S(1)} %collective-permute-done.5.refs_4_), channel_id=1, source_target_pairs={{0,4},{1,5},{2,6},{3,7},{4,0},{5,1},{6,2},{7,3},{8,12},{9,13},{10,... | collective-permute-start | bytes 245768 | tf_op jit(solution)/shard_map/ppermute | solution.py:211

commit v2 on v1

--- a/solution.py
+++ b/solution.py
@@ -152,9 +152,14 @@
 
 
 def whole_kernel(near, *refs):
-    lines, others = refs[:5], refs[5:10]
+    lines, (early, late) = refs[:5], refs[5:7]
+    others, first = [None] * 5, {id(early): 0, id(late): 0}
+    for index, packed in ((0, early), (1, early), (4, early), (2, late), (3, late)):
+        size = lines[index].shape[0]
+        others[index] = packed.at[pl.ds(first[id(packed)], size)]
+        first[id(packed)] += size
     (slots, flows_out, duals_out, mult_out, cons_out, spread_out,
-     blocks_in, cost, cap, mask, demand_in, demand, share, flows, duals, prices, centre, shifted) = refs[10:]
+     blocks_in, cost, cap, mask, demand_in, demand, share, flows, duals, prices, centre, shifted) = refs[7:]
     total_rows, block_arcs = near.shape
     scen, arc = lax.axis_index("scen"), lax.axis_index("arc")
     chip, core = scen // 2, lax.rem(scen, 2)
@@ -225,8 +230,10 @@
     side = swap(line, lambda scen, arc: (scen ^ 2, arc))
     front = swap(line, lambda scen, arc: (scen ^ 4, arc))
     across = swap(across, lambda scen, arc: (scen, arc ^ (1 + scen % 2)))
-    brought = [line, side, front, across, beyond]
-    return brought + [swap(value, lambda scen, arc: (scen ^ 1, arc)) for value in brought]
+    early = jnp.concatenate([line, side, beyond], axis=0)
+    late = jnp.concatenate([front, across], axis=0)
+    other = lambda scen, arc: (scen ^ 1, arc)
+    return [line, side, front, across, beyond, swap(early, other), swap(late, other)]
 
 
 def body(coupling, incidence, arc_cost, capacity, demand, weights, fleet_slots):

time: 37.8 us -> 35.2 us (0.931)
  starting transfers between devices: 14.8 us -> 11.7 us
  waiting for transfers between devices: 9.16 us -> 9.59 us
    ppermute x11 -> x8, starting transfers between devices: 14.8 us -> 11.7 us  [swap(): return lax.ppermute(value, ('scen', 'arc'), pairs)]
    ppermute x11 -> x8, waiting for transfers between devices: 9.16 us -> 9.59 us  [swap(): return lax.ppermute(value, ('scen', 'arc'), pairs)]
  transfers between devices with their start and end apart: 11 -> 8, of which waited for: 5 -> 5; matrix products, arithmetic and copies ran while one was open for 0% -> 0% of each run, Pallas kernels for 4% -> 4%
where the time goes in v2:
time: 35.2 us; the launch traced here: 35 us
  starting transfers between devices  11.7 us (33%)
  Pallas kernels  9.59 us (27%)
  waiting for transfers between devices  9.59 us (27%)
  local copies, waits for them, and re-layouts  2.63 us (7%)
  between operations  1.38 us (4%)
    ppermute x8, starting transfers between devices, swap(): return lax.ppermute(value, ('scen', 'arc'), pairs)  11.7 us
    ppermute x8, waiting for transfers between devices, swap(): return lax.ppermute(value, ('scen', 'arc'), pairs)  9.59 us
    pallas_call x1, Pallas kernels, body(): pl.pallas_call(whole_kernel, out_shape=out_shape, in_specs=[VMEM] * (len(...  8.06 us
    unnamed x12, local copies, waits for them, and re-layouts  1.71 us
    pallas_call x1, Pallas kernels, body(): pl.pallas_call(pack_kernel, out_shape=(like(total_rows), like(TILE + EXTR...  1.53 us
    dynamic_slice x1, local copies, waits for them, and re-layouts, bring(): lax.dynamic_slice_in_dim(coupling, lax.shift_right_logical(scen, 1) * TIL...  0.92 us
  transfers between devices with their start and end apart: 8, of which 5 were waited for; matrix products, arithmetic and copies ran while one was open for 0% of the time, Pallas kernels for 4%

profile of v2, /device:TPU:0, one launch (start us, length us, event | category | flops | bytes accessed | tf_op | source)
XLA Modules:
  0.0 35.0 jit_solution(9072628027155916132)
XLA Ops:
  0.6 0.9 %constant_dynamic-slice_fusion.1 = bf16[128,512]{1,0:T(8,128)(2,1)S(1)} fusion(bf16[512,512]{1,0:T(8,128)(2,1)} %coupling.1, s32[]{:T(128)S(6)} %select_n.6), kind=kLoop, calls=%fused_computation.4 | loop fusion | bytes 262148 | tf_op jit(solution)/shard_map/dynamic_slice | solution.py:222
  1.6 3.1 %collective-permute-start = (bf16[128,512]{1,0:T(8,128)(2,1)S(1)}, bf16[128,512]{1,0:T(8,128)(2,1)S(1)}, u32[]{:S(2)}, u32[]{:S(2)}) collective-permute-start(bf16[128,512]{1,0:T(8,128)(2,1)S(1)} %constant_dynamic-slice_fusion.1), channel_id=1, source_target_pairs={{0,1},{1,0},{2,3},{3,2},{4,6},{5,7},{6,4},{7,5},{8,9},{9,8},{10,11... | collective-permute-start | bytes 393224 | tf_op jit(solution)/shard_map/ppermute | solution.py:216
  4.6 0.0 copy-start.3
  4.6 0.0 copy-start.4
  4.7 2.5 %collective-permute-start.1 = (bf16[64,512]{1,0:T(8,128)(2,1)S(1)}, bf16[64,512]{1,0:T(8,128)(2,1)S(1)}, u32[]{:S(2)}, u32[]{:S(2)}) collective-permute-start(bf16[64,512]{1,0:T(8,128)(2,1)S(1)} %constant_dynamic-slice_fusion), channel_id=1, source_target_pairs={{0,3},{1,2},{2,1},{3,0},{4,7},{5,6},{6,5},{7,4},{8,11},{9,10},{10,... | collective-permute-start | bytes 196616 | tf_op jit(solution)/shard_map/ppermute | solution.py:216
  7.9 0.0 copy-start.2
  7.9 0.0 copy-start.1
  7.9 0.0 copy-start.5
  7.9 0.0 copy-done.3
  7.9 0.0 copy-done.4
  7.9 0.6 %copy-done.2 = f32[512]{0:T(512)S(1)} copy-done((f32[512]{0:T(512)S(1)}, f32[512]{0:T(512)}, u32[]{:S(2)}) %copy-start.2) | copy-done | bytes 2072
  8.5 0.0 copy-done.1
  8.6 0.0 copy-done.5
  8.6 0.0 copy-start
  8.6 1.0 %copy-done = bf16[512,512]{1,0:T(8,128)(2,1)S(1)} copy-done((bf16[512,512]{1,0:T(8,128)(2,1)S(1)}, bf16[512,512]{1,0:T(8,128)(2,1)}, u32[]{:S(2)}) %copy-start) | copy-done | bytes 524312
  9.6 1.5 %pack.1 = (bf16[512,512]{1,0:T(8,128)(2,1)S(1)}, bf16[144,512]{1,0:T(8,128)(2,1)S(1)}, bf16[80,512]{1,0:T(8,128)(2,1)S(1)}, bf16[16,512]{1,0:T(8,128)(2,1)S(1)}) custom-call(bf16[512,512]{1,0:T(8,128)(2,1)S(1)} %copy-done, s32[4,4]{1,0:T(4,128)S(1)} %copy-done.1, f32[1,512]{1,0:T(1,128)S(1)} %bitcast.6, f32[1,512]{1,0:T(1,128)S(1)} %bitcast.7, ...), custom_call_target="tpu_custom_call" | custom-call | tf_op jit(solution)/shard_map/pack/pallas_call | solution.py:270
  11.1 0.6 %collective-permute-done.1 = bf16[64,512]{1,0:T(8,128)(2,1)S(1)} collective-permute-done((bf16[64,512]{1,0:T(8,128)(2,1)S(1)}, bf16[64,512]{1,0:T(8,128)(2,1)S(1)}, u32[]{:S(2)}, u32[]{:S(2)}) %collective-permute-start.1) | collective-permute-done | bytes 65568 | tf_op jit(solution)/shard_map/ppermute | solution.py:216
  11.8 0.0 collective-permute-done
  11.8 1.6 %collective-permute-start.2 = (bf16[208,512]{1,0:T(8,128)(2,1)S(1)}, bf16[208,512]{1,0:T(8,128)(2,1)S(1)}, u32[]{:S(2)}, u32[]{:S(2)}) collective-permute-start(bf16[208,512]{1,0:T(8,128)(2,1)S(1)} %pad_maximum_fusion.2.refs_0_), channel_id=1, source_target_pairs={{0,8},{1,9},{2,10},{3,11},{4,12},{5,13},{6,14},{7,15},{8,0},{9,1},... | collective-permute-start | bytes 638984 | tf_op jit(solution)/shard_map/ppermute | solution.py:216
  13.4 3.3 %collective-permute-start.5 = (bf16[80,512]{1,0:T(8,128)(2,1)S(1)}, bf16[80,512]{1,0:T(8,128)(2,1)S(1)}, u32[]{:S(2)}, u32[]{:S(2)}) collective-permute-start(bf16[80,512]{1,0:T(8,128)(2,1)S(1)} %get-tuple-element.21), channel_id=1, source_target_pairs={{0,27},{1,26},{2,25},{3,24},{4,31},{5,30},{6,29},{7,28},{8,19},{9,... | collective-permute-start | bytes 245768 | tf_op jit(solution)/shard_map/ppermute | solution.py:216
  16.6 0.5 %collective-permute-start.3 = (bf16[208,512]{1,0:T(8,128)(2,1)S(1)}, bf16[208,512]{1,0:T(8,128)(2,1)S(1)}, u32[]{:S(2)}, u32[]{:S(2)}) collective-permute-start(bf16[208,512]{1,0:T(8,128)(2,1)S(1)} %pad_maximum_fusion.2.refs_0_), channel_id=1, source_target_pairs={{0,16},{1,17},{2,18},{3,19},{4,20},{5,21},{6,22},{7,23},{8,24},{9,... | collective-permute-start | bytes 638984 | tf_op jit(solution)/shard_map/ppermute | solution.py:216
  17.1 0.6 %collective-permute-start.4 = (bf16[144,512]{1,0:T(8,128)(2,1)S(1)}, bf16[144,512]{1,0:T(8,128)(2,1)S(1)}, u32[]{:S(2)}, u32[]{:S(2)}) collective-permute-start(bf16[144,512]{1,0:T(8,128)(2,1)S(1)} %get-tuple-element.20), channel_id=1, source_target_pairs={{0,1},{1,0},{2,3},{3,2},{4,6},{5,7},{6,4},{7,5},{8,9},{9,8},{10,11... | collective-permute-start | bytes 442376 | tf_op jit(solution)/shard_map/ppermute | solution.py:216
  17.7 3.8 %collective-permute-done.5.refs_4_ = bf16[80,512]{1,0:T(8,128)(2,1)S(1)} collective-permute-done((bf16[80,512]{1,0:T(8,128)(2,1)S(1)}, bf16[80,512]{1,0:T(8,128)(2,1)S(1)}, u32[]{:S(2)}, u32[]{:S(2)}) %collective-permute-start.5) | collective-permute-done | bytes 81952 | tf_op jit(solution)/shard_map/ppermute | solution.py:216
  21.5 0.0 collective-permute-done.2.refs_1_
  21.6 0.1 collective-permute-start.6
  21.6 2.4 %collective-permute-done.4.refs_3_ = bf16[144,512]{1,0:T(8,128)(2,1)S(1)} collective-permute-done((bf16[144,512]{1,0:T(8,128)(2,1)S(1)}, bf16[144,512]{1,0:T(8,128)(2,1)S(1)}, u32[]{:S(2)}, u32[]{:S(2)}) %collective-permute-start.4) | collective-permute-done | bytes 147488 | tf_op jit(solution)/shard_map/ppermute | solution.py:216
  24.0 1.1 %collective-permute-done.3.refs_2_ = bf16[208,512]{1,0:T(8,128)(2,1)S(1)} collective-permute-done((bf16[208,512]{1,0:T(8,128)(2,1)S(1)}, bf16[208,512]{1,0:T(8,128)(2,1)S(1)}, u32[]{:S(2)}, u32[]{:S(2)}) %collective-permute-start.3) | collective-permute-done | bytes 213024 | tf_op jit(solution)/shard_map/ppermute | solution.py:216
  25.2 0.1 collective-permute-start.7
  25.2 1.7 %collective-permute-done.7.refs_6_ = bf16[352,512]{1,0:T(8,128)(2,1)S(1)} collective-permute-done((bf16[352,512]{1,0:T(8,128)(2,1)S(1)}, bf16[352,512]{1,0:T(8,128)(2,1)S(1)}, u32[]{:S(2)}, u32[]{:S(2)}) %collective-permute-start.7) | collective-permute-done | bytes 360480 | tf_op jit(solution)/shard_map/ppermute | solution.py:216
  26.9 0.0 collective-permute-done.6.refs_5_
  26.9 8.1 %whole.1 = (f32[1,512]{1,0:T(1,128)}, f32[1,128]{1,0:T(1,128)}, f32[1,128]{1,0:T(1,128)}, f32[1,128]{1,0:T(1,128)}, f32[2]{0:T(128)}) custom-call(bf16[512,512]{1,0:T(8,128)(2,1)S(1)} %get-tuple-element.16.near, bf16[208,512]{1,0:T(8,128)(2,1)S(1)} %pad_maximum_fusion.2.refs_0_, bf16[208,512]{1,0:T(8,128)(2,1)S(1)} %collective-permute-done.2.refs_1_, ...), custom_call_target="tpu_custom_call" | custom-call | flops 268435456 | bytes 2097152 | tf_op jit(solution)/shard_map/whole/pallas_call | solution.py:283
  (4 shorter events, 0.1 us)
Async XLA Ops:
  1.6 10.2 %collective-permute-start = (bf16[128,512]{1,0:T(8,128)(2,1)S(1)}, bf16[128,512]{1,0:T(8,128)(2,1)S(1)}, u32[]{:S(2)}, u32[]{:S(2)}) collective-permute-start(bf16[128,512]{1,0:T(8,128)(2,1)S(1)} %constant_dynamic-slice_fusion.1), channel_id=1, source_target_pairs={{0,1},{1,0},{2,3},{3,2},{4,6},{5,7},{6,4},{7,5},{8,9},{9,8},{10,11... | collective-permute-start | bytes 393224 | tf_op jit(solution)/shard_map/ppermute | solution.py:216
  4.6 3.2 %copy-start.3 = (f32[512]{0:T(512)S(1)}, f32[512]{0:T(512)}, u32[]{:S(2)}) copy-start(f32[512]{0:T(512)} %param.10) | copy-start | bytes 6148
  4.6 3.3 %copy-start.4 = (f32[1,512]{1,0:T(1,128)S(1)}, f32[1,512]{1,0:T(1,128)}, u32[]{:S(2)}) copy-start(f32[1,512]{1,0:T(1,128)} %demand.1) | copy-start | bytes 6148
  4.7 7.1 %collective-permute-start.1 = (bf16[64,512]{1,0:T(8,128)(2,1)S(1)}, bf16[64,512]{1,0:T(8,128)(2,1)S(1)}, u32[]{:S(2)}, u32[]{:S(2)}) collective-permute-start(bf16[64,512]{1,0:T(8,128)(2,1)S(1)} %constant_dynamic-slice_fusion), channel_id=1, source_target_pairs={{0,3},{1,2},{2,1},{3,0},{4,7},{5,6},{6,5},{7,4},{8,11},{9,10},{10,... | collective-permute-start | bytes 196616 | tf_op jit(solution)/shard_map/ppermute | solution.py:216
  7.9 0.7 %copy-start.2 = (f32[512]{0:T(512)S(1)}, f32[512]{0:T(512)}, u32[]{:S(2)}) copy-start(f32[512]{0:T(512)} %param.9) | copy-start | bytes 6148
  7.9 0.7 %copy-start.1 = (s32[4,4]{1,0:T(4,128)S(1)}, s32[4,4]{1,0:T(4,128)}, u32[]{:S(2)}) copy-start(s32[4,4]{1,0:T(4,128)} %incidence.1) | copy-start | bytes 196
  7.9 0.7 %copy-start.5 = (s32[128]{0:T(128)S(1)}, s32[128]{0:T(128)}, u32[]{:S(2)}) copy-start(s32[128]{0:T(128)} %param.13) | copy-start | bytes 1540
  8.6 1.0 %copy-start = (bf16[512,512]{1,0:T(8,128)(2,1)S(1)}, bf16[512,512]{1,0:T(8,128)(2,1)}, u32[]{:S(2)}) copy-start(bf16[512,512]{1,0:T(8,128)(2,1)} %coupling.1) | copy-start | bytes 1572868
  11.8 9.7 %collective-permute-start.2 = (bf16[208,512]{1,0:T(8,128)(2,1)S(1)}, bf16[208,512]{1,0:T(8,128)(2,1)S(1)}, u32[]{:S(2)}, u32[]{:S(2)}) collective-permute-start(bf16[208,512]{1,0:T(8,128)(2,1)S(1)} %pad_maximum_fusion.2.refs_0_), channel_id=1, source_target_pairs={{0,8},{1,9},{2,10},{3,11},{4,12},{5,13},{6,14},{7,15},{8,0},{9,1},... | collective-permute-start | bytes 638984 | tf_op jit(solution)/shard_map/ppermute | solution.py:216
  13.4 8.2 %collective-permute-start.5 = (bf16[80,512]{1,0:T(8,128)(2,1)S(1)}, bf16[80,512]{1,0:T(8,128)(2,1)S(1)}, u32[]{:S(2)}, u32[]{:S(2)}) collective-permute-start(bf16[80,512]{1,0:T(8,128)(2,1)S(1)} %get-tuple-element.21), channel_id=1, source_target_pairs={{0,27},{1,26},{2,25},{3,24},{4,31},{5,30},{6,29},{7,28},{8,19},{9,... | collective-permute-start | bytes 245768 | tf_op jit(solution)/shard_map/ppermute | solution.py:216
  16.6 8.5 %collective-permute-start.3 = (bf16[208,512]{1,0:T(8,128)(2,1)S(1)}, bf16[208,512]{1,0:T(8,128)(2,1)S(1)}, u32[]{:S(2)}, u32[]{:S(2)}) collective-permute-start(bf16[208,512]{1,0:T(8,128)(2,1)S(1)} %pad_maximum_fusion.2.refs_0_), channel_id=1, source_target_pairs={{0,16},{1,17},{2,18},{3,19},{4,20},{5,21},{6,22},{7,23},{8,24},{9,... | collective-permute-start | bytes 638984 | tf_op jit(solution)/shard_map/ppermute | solution.py:216
  17.1 6.9 %collective-permute-start.4 = (bf16[144,512]{1,0:T(8,128)(2,1)S(1)}, bf16[144,512]{1,0:T(8,128)(2,1)S(1)}, u32[]{:S(2)}, u32[]{:S(2)}) collective-permute-start(bf16[144,512]{1,0:T(8,128)(2,1)S(1)} %get-tuple-element.20), channel_id=1, source_target_pairs={{0,1},{1,0},{2,3},{3,2},{4,6},{5,7},{6,4},{7,5},{8,9},{9,8},{10,11... | collective-permute-start | bytes 442376 | tf_op jit(solution)/shard_map/ppermute | solution.py:216
  21.6 5.3 %collective-permute-start.6 = (bf16[496,512]{1,0:T(8,128)(2,1)S(1)}, bf16[496,512]{1,0:T(8,128)(2,1)S(1)}, u32[]{:S(2)}, u32[]{:S(2)}) collective-permute-start(bf16[496,512]{1,0:T(8,128)(2,1)S(1)} %pad_maximum_fusion), channel_id=1, source_target_pairs={{0,4},{1,5},{2,6},{3,7},{4,0},{5,1},{6,2},{7,3},{8,12},{9,13},{10,... | collective-permute-start | bytes 1523720 | tf_op jit(solution)/shard_map/ppermute | solution.py:216
  25.2 1.7 %collective-permute-start.7 = (bf16[352,512]{1,0:T(8,128)(2,1)S(1)}, bf16[352,512]{1,0:T(8,128)(2,1)S(1)}, u32[]{:S(2)}, u32[]{:S(2)}) collective-permute-start(bf16[352,512]{1,0:T(8,128)(2,1)S(1)} %pad_maximum_fusion.1), channel_id=1, source_target_pairs={{0,4},{1,5},{2,6},{3,7},{4,0},{5,1},{6,2},{7,3},{8,12},{9,13},{10,... | collective-permute-start | bytes 1081352 | tf_op jit(solution)/shard_map/ppermute | solution.py:216

commit v3 on v1

--- a/solution.py
+++ b/solution.py
@@ -47,11 +47,9 @@
 
 
 def pack_kernel(coupling, incidence, arc_cost, capacity, demand, weights, slots,
-                near, across, beyond, extra, rows_in, sems):
+                near, across, extra, rows_in, sems):
     total_rows, block_arcs = rows_in.shape
-    half = TILE // 2
-    scen = lax.axis_index("scen")
-    chip, core = scen // 2, lax.rem(scen, 2)
+    chip = lax.axis_index("scen") // 2
     chips = total_rows // TILE
     copies = []
     for part in range(chips):
@@ -75,13 +73,11 @@
     lines = jnp.concatenate(lines, axis=0).astype(jnp.bfloat16)
     extra[...] = lines
     across[TILE:, :] = lines
-    beyond[half:, :] = lines
     for part in range(chips):
         copies[part].wait()
         rows = slice(part * TILE, (part + 1) * TILE)
         near[rows, :] = rows_in[rows, :] * touch[part].astype(jnp.bfloat16)
     across[:TILE, :] = near[(chips - 1) * TILE:, :]
-    beyond[:half, :] = near[pl.ds(pl.multiple_of(core * half, half), half), :]
 
 
 def rounds(masked, blocks, cost, cap, mask, demand, share, fleet_count, spread_out,
@@ -152,15 +148,21 @@
 
 
 def whole_kernel(near, *refs):
-    lines, others = refs[:5], refs[5:10]
+    lines, others = refs[:6], [None] * 6
+    for packed, parts in ((refs[6], (0, 1, 4)), (refs[7], (2, 3, 5))):
+        first = 0
+        for part in parts:
+            rows = lines[part].shape[0]
+            others[part] = packed.at[pl.ds(first, rows)]
+            first += rows
     (slots, flows_out, duals_out, mult_out, cons_out, spread_out,
-     blocks_in, cost, cap, mask, demand_in, demand, share, flows, duals, prices, centre, shifted) = refs[10:]
+     blocks_in, cost, cap, mask, demand_in, demand, share, flows, duals, prices, centre, shifted) = refs[8:]
     total_rows, block_arcs = near.shape
     scen, arc = lax.axis_index("scen"), lax.axis_index("arc")
     chip, core = scen // 2, lax.rem(scen, 2)
     chips = total_rows // TILE
     half = TILE // 2
-    tails = [lines[0][TILE + half:, :], lines[3][TILE:, :], others[3][TILE:, :], lines[4][half:, :]]
+    tails = [lines[0][TILE + half:, :], lines[3][TILE:, :], others[3][TILE:, :], lines[5][...]]
     touch = []
     for block, tail in enumerate(tails):
         cols = slice(block * block_arcs, (block + 1) * block_arcs)
@@ -171,7 +173,7 @@
         touch.append(tail[11:11 + chips].astype(jnp.bfloat16))
     for row in range(2 * chips):
         part, source = row // 2, others if row % 2 else lines
-        tail = source[part][TILE + half:, :] if part < chips - 1 else source[chips][half:, :]
+        tail = source[part][TILE + half:, :] if part < chips - 1 else source[5][...]
         tail = tail.astype(jnp.float32)
         demand_in[row:row + 1, :] = tail[7:8] + tail[8:9] + tail[9:10]
         share[row:row + 1, :] = tail[10:11, :128] + tail[10:11, 128:256] + tail[10:11, 256:384]
@@ -182,13 +184,13 @@
         for side, source in enumerate((lines, others)):
             place = jnp.where(core == side, 0, half)
             place = pl.ds(pl.multiple_of(part * TILE + place, half), half)
+            on = touch[3][chips - 1 - part:chips - part]
             if part < chips - 1:
                 blocks_in[side, rows, :] = source[part][:TILE, :] * touch[1 + side][part:part + 1]
-                on = touch[3][chips - 1 - part:chips - part]
                 blocks_in[2, place, :] = source[part][TILE:TILE + half, :] * on
             else:
-                blocks_in[side, rows, :] = source[chips - 1][:TILE, :]
-                blocks_in[2, place, :] = source[chips][:half, :]
+                blocks_in[side, rows, :] = source[3][:TILE, :]
+                blocks_in[2, place, :] = source[4][...] * on
 
     def masked(block):
         return near[...] if block == 0 else blocks_in[block - 1]
@@ -211,7 +213,7 @@
     return lax.ppermute(value, ("scen", "arc"), pairs)
 
 
-def bring(coupling, across, beyond, extra):
+def bring(coupling, across, extra):
     scen = lax.axis_index("scen")
     half = TILE // 2
     wide = lax.dynamic_slice_in_dim(coupling, lax.shift_right_logical(scen, 1) * TILE, TILE, 0)
@@ -219,14 +221,17 @@
     narrow = lax.dynamic_slice_in_dim(wide, (scen & 1) * half, half, 0)
     wide = swap(wide, lambda scen, arc: (scen, arc ^ (1 + scen % 2)))
     narrow = swap(narrow, lambda scen, arc: (scen, arc ^ 3))
-    beyond = swap(beyond, lambda scen, arc: (scen ^ 6, arc ^ 3))
     line = jnp.concatenate([wide, narrow, extra], axis=0)
     line, across = lax.optimization_barrier((line, across))
     side = swap(line, lambda scen, arc: (scen ^ 2, arc))
     front = swap(line, lambda scen, arc: (scen ^ 4, arc))
     across = swap(across, lambda scen, arc: (scen, arc ^ (1 + scen % 2)))
-    brought = [line, side, front, across, beyond]
-    return brought + [swap(value, lambda scen, arc: (scen ^ 1, arc)) for value in brought]
+    beyond = swap(narrow, lambda scen, arc: (scen ^ 6, arc))
+    extra = swap(extra, lambda scen, arc: (scen ^ 6, arc ^ 3))
+    early = jnp.concatenate([line, side, beyond], axis=0)
+    late = jnp.concatenate([front, across, extra], axis=0)
+    other = lambda scen, arc: (scen ^ 1, arc)
+    return [line, side, front, across, beyond, extra, swap(early, other), swap(late, other)]
 
 
 def body(coupling, incidence, arc_cost, capacity, demand, weights, fleet_slots):
@@ -260,11 +265,11 @@
     fits = (scenarios, blocks) == (8, 4)
     if fits and total_rows == TILE * 4:
         like = lambda rows: jax.ShapeDtypeStruct((rows, block_arcs), jnp.bfloat16)
-        near, across, beyond, extra = pl.pallas_call(
+        near, across, extra = pl.pallas_call(
             pack_kernel,
-            out_shape=(like(total_rows), like(TILE + EXTRA), like(TILE // 2 + EXTRA), like(EXTRA)),
+            out_shape=(like(total_rows), like(TILE + EXTRA), like(EXTRA)),
             in_specs=[ANY, SMEM, VMEM, VMEM, VMEM, VMEM, VMEM],
-            out_specs=(VMEM,) * 4,
+            out_specs=(VMEM,) * 3,
             scratch_shapes=[
                 pltpu.VMEM((total_rows, block_arcs), jnp.bfloat16),
                 pltpu.SemaphoreType.DMA((total_rows // TILE,)),
@@ -272,7 +277,7 @@
             compiler_params=limit(8),
             name="pack",
         )(coupling, incidence, row(arc_cost), row(capacity), demand, weights.reshape(1, 1), slots)
-        brought = bring(coupling, across, beyond, extra)
+        brought = bring(coupling, across, extra)
         outs = pl.pallas_call(
             whole_kernel,
             out_shape=out_shape,

time: 37.8 us -> 34.6 us (0.915)
  waiting for transfers between devices: 9.16 us -> 5.7 us
    ppermute x11 -> x9, waiting for transfers between devices: 9.16 us -> 5.7 us  [swap(): return lax.ppermute(value, ('scen', 'arc'), pairs)]
    ppermute x11 -> x9, starting transfers between devices: 14.8 us -> 15 us  [swap(): return lax.ppermute(value, ('scen', 'arc'), pairs)]
  transfers between devices with their start and end apart: 11 -> 9, of which waited for: 5 -> 3; matrix products, arithmetic and copies ran while one was open for 0% -> 0% of each run, Pallas kernels for 4% -> 4%
where the time goes in v3:
time: 34.6 us; the launch traced here: 34.4 us
  starting transfers between devices  15 us (43%)
  Pallas kernels  9.58 us (28%)
  waiting for transfers between devices  5.7 us (16%)
  local copies, waits for them, and re-layouts  2.63 us (8%)
  between operations  1.38 us (4%)
    ppermute x9, starting transfers between devices, swap(): return lax.ppermute(value, ('scen', 'arc'), pairs)  15 us
    pallas_call x1, Pallas kernels, body(): pl.pallas_call(whole_kernel, out_shape=out_shape, in_specs=[VMEM] * (len(...  8.06 us
    ppermute x9, waiting for transfers between devices, swap(): return lax.ppermute(value, ('scen', 'arc'), pairs)  5.7 us
    unnamed x12, local copies, waits for them, and re-layouts  1.71 us
    pallas_call x1, Pallas kernels, body(): pl.pallas_call(pack_kernel, out_shape=(like(total_rows), like(TILE + EXTR...  1.52 us
    dynamic_slice x1, local copies, waits for them, and re-layouts, bring(): lax.dynamic_slice_in_dim(coupling, lax.shift_right_logical(scen, 1) * TIL...  0.92 us
  transfers between devices with their start and end apart: 9, of which 3 were waited for; matrix products, arithmetic and copies ran while one was open for 0% of the time, Pallas kernels for 4%

profile of v3, /device:TPU:0, one launch (start us, length us, event | category | flops | bytes accessed | tf_op | source)
XLA Modules:
  0.0 34.4 jit_solution(12922437446314152132)
XLA Ops:
  0.6 0.9 %constant_dynamic-slice_fusion.1 = bf16[128,512]{1,0:T(8,128)(2,1)S(1)} fusion(bf16[512,512]{1,0:T(8,128)(2,1)} %coupling.1, s32[]{:T(128)S(6)} %select_n.6), kind=kLoop, calls=%fused_computation.4 | loop fusion | bytes 262148 | tf_op jit(solution)/shard_map/dynamic_slice | solution.py:219
  1.6 3.1 %collective-permute-start = (bf16[128,512]{1,0:T(8,128)(2,1)S(1)}, bf16[128,512]{1,0:T(8,128)(2,1)S(1)}, u32[]{:S(2)}, u32[]{:S(2)}) collective-permute-start(bf16[128,512]{1,0:T(8,128)(2,1)S(1)} %constant_dynamic-slice_fusion.1), channel_id=1, source_target_pairs={{0,1},{1,0},{2,3},{3,2},{4,6},{5,7},{6,4},{7,5},{8,9},{9,8},{10,11... | collective-permute-start | bytes 393224 | tf_op jit(solution)/shard_map/ppermute | solution.py:213
  4.6 0.0 copy-start.3
  4.6 0.0 copy-start.4
  4.7 2.5 %collective-permute-start.1 = (bf16[64,512]{1,0:T(8,128)(2,1)S(1)}, bf16[64,512]{1,0:T(8,128)(2,1)S(1)}, u32[]{:S(2)}, u32[]{:S(2)}) collective-permute-start(bf16[64,512]{1,0:T(8,128)(2,1)S(1)} %constant_dynamic-slice_fusion), channel_id=1, source_target_pairs={{0,3},{1,2},{2,1},{3,0},{4,7},{5,6},{6,5},{7,4},{8,11},{9,10},{10,... | collective-permute-start | bytes 196616 | tf_op jit(solution)/shard_map/ppermute | solution.py:213
  7.9 0.0 copy-start.2
  7.9 0.0 copy-start.1
  7.9 0.0 copy-start.5
  7.9 0.0 copy-done.3
  7.9 0.0 copy-done.4
  7.9 0.6 %copy-done.2 = f32[512]{0:T(512)S(1)} copy-done((f32[512]{0:T(512)S(1)}, f32[512]{0:T(512)}, u32[]{:S(2)}) %copy-start.2) | copy-done | bytes 2072
  8.5 0.0 copy-done.1
  8.6 0.0 copy-done.5
  8.6 0.0 copy-start
  8.6 1.0 %copy-done = bf16[512,512]{1,0:T(8,128)(2,1)S(1)} copy-done((bf16[512,512]{1,0:T(8,128)(2,1)S(1)}, bf16[512,512]{1,0:T(8,128)(2,1)}, u32[]{:S(2)}) %copy-start) | copy-done | bytes 524312
  9.6 1.5 %pack.1 = (bf16[512,512]{1,0:T(8,128)(2,1)S(1)}, bf16[144,512]{1,0:T(8,128)(2,1)S(1)}, bf16[16,512]{1,0:T(8,128)(2,1)S(1)}) custom-call(bf16[512,512]{1,0:T(8,128)(2,1)S(1)} %copy-done, s32[4,4]{1,0:T(4,128)S(1)} %copy-done.1, f32[1,512]{1,0:T(1,128)S(1)} %bitcast.6, f32[1,512]{1,0:T(1,128)S(1)} %bitcast.7, f32[1,512]{1,0:T(1,128)S(1)} %copy-done.4, ...), custom_call_target="tpu_custom_call" | custom-call | tf_op jit(solution)/shard_map/pack/pallas_call | solution.py:268
  11.1 0.6 %collective-permute-done.1 = bf16[64,512]{1,0:T(8,128)(2,1)S(1)} collective-permute-done((bf16[64,512]{1,0:T(8,128)(2,1)S(1)}, bf16[64,512]{1,0:T(8,128)(2,1)S(1)}, u32[]{:S(2)}, u32[]{:S(2)}) %collective-permute-start.1) | collective-permute-done | bytes 65568 | tf_op jit(solution)/shard_map/ppermute | solution.py:213
  11.8 0.0 collective-permute-done
  11.8 1.6 %collective-permute-start.2 = (bf16[208,512]{1,0:T(8,128)(2,1)S(1)}, bf16[208,512]{1,0:T(8,128)(2,1)S(1)}, u32[]{:S(2)}, u32[]{:S(2)}) collective-permute-start(bf16[208,512]{1,0:T(8,128)(2,1)S(1)} %pad_maximum_fusion.2.refs_0_), channel_id=1, source_target_pairs={{0,8},{1,9},{2,10},{3,11},{4,12},{5,13},{6,14},{7,15},{8,0},{9,1},... | collective-permute-start | bytes 638984 | tf_op jit(solution)/shard_map/ppermute | solution.py:213
  13.4 1.5 %collective-permute-start.3 = (bf16[208,512]{1,0:T(8,128)(2,1)S(1)}, bf16[208,512]{1,0:T(8,128)(2,1)S(1)}, u32[]{:S(2)}, u32[]{:S(2)}) collective-permute-start(bf16[208,512]{1,0:T(8,128)(2,1)S(1)} %pad_maximum_fusion.2.refs_0_), channel_id=1, source_target_pairs={{0,16},{1,17},{2,18},{3,19},{4,20},{5,21},{6,22},{7,23},{8,24},{9,... | collective-permute-start | bytes 638984 | tf_op jit(solution)/shard_map/ppermute | solution.py:213
  14.9 0.5 %collective-permute-start.5 = (bf16[64,512]{1,0:T(8,128)(2,1)S(1)}, bf16[64,512]{1,0:T(8,128)(2,1)S(1)}, u32[]{:S(2)}, u32[]{:S(2)}) collective-permute-start(bf16[64,512]{1,0:T(8,128)(2,1)S(1)} %collective-permute-done.1), channel_id=1, source_target_pairs={{0,24},{1,25},{2,26},{3,27},{4,28},{5,29},{6,30},{7,31},{8,16},{9,... | collective-permute-start | bytes 196616 | tf_op jit(solution)/shard_map/ppermute | solution.py:213
  15.4 0.6 %collective-permute-start.4 = (bf16[144,512]{1,0:T(8,128)(2,1)S(1)}, bf16[144,512]{1,0:T(8,128)(2,1)S(1)}, u32[]{:S(2)}, u32[]{:S(2)}) collective-permute-start(bf16[144,512]{1,0:T(8,128)(2,1)S(1)} %get-tuple-element.19), channel_id=1, source_target_pairs={{0,1},{1,0},{2,3},{3,2},{4,6},{5,7},{6,4},{7,5},{8,9},{9,8},{10,11... | collective-permute-start | bytes 442376 | tf_op jit(solution)/shard_map/ppermute | solution.py:213
  16.0 5.1 %collective-permute-start.6 = (bf16[16,512]{1,0:T(8,128)(2,1)S(1)}, bf16[16,512]{1,0:T(8,128)(2,1)S(1)}, u32[]{:S(2)}, u32[]{:S(2)}) collective-permute-start(bf16[16,512]{1,0:T(8,128)(2,1)S(1)} %get-tuple-element.16), channel_id=1, source_target_pairs={{0,27},{1,26},{2,25},{3,24},{4,31},{5,30},{6,29},{7,28},{8,19},{9,... | collective-permute-start | bytes 49160 | tf_op jit(solution)/shard_map/ppermute | solution.py:213
  21.1 0.0 collective-permute-done.5.refs_4_
  21.1 0.0 collective-permute-done.2.refs_1_
  21.1 0.1 collective-permute-start.7
  21.2 3.3 %collective-permute-done.6.refs_5_ = bf16[16,512]{1,0:T(8,128)(2,1)S(1)} collective-permute-done((bf16[16,512]{1,0:T(8,128)(2,1)S(1)}, bf16[16,512]{1,0:T(8,128)(2,1)S(1)}, u32[]{:S(2)}, u32[]{:S(2)}) %collective-permute-start.6) | collective-permute-done | bytes 16416 | tf_op jit(solution)/shard_map/ppermute | solution.py:213
  24.5 0.0 collective-permute-done.4.refs_3_
  24.5 0.0 collective-permute-done.3.refs_2_
  24.6 0.1 collective-permute-start.8
  24.7 1.7 %collective-permute-done.8.refs_7_ = bf16[368,512]{1,0:T(8,128)(2,1)S(1)} collective-permute-done((bf16[368,512]{1,0:T(8,128)(2,1)S(1)}, bf16[368,512]{1,0:T(8,128)(2,1)S(1)}, u32[]{:S(2)}, u32[]{:S(2)}) %collective-permute-start.8) | collective-permute-done | bytes 376864 | tf_op jit(solution)/shard_map/ppermute | solution.py:213
  26.3 0.0 collective-permute-done.7.refs_6_
  26.3 8.1 %whole.1 = (f32[1,512]{1,0:T(1,128)}, f32[1,128]{1,0:T(1,128)}, f32[1,128]{1,0:T(1,128)}, f32[1,128]{1,0:T(1,128)}, f32[2]{0:T(128)}) custom-call(bf16[512,512]{1,0:T(8,128)(2,1)S(1)} %get-tuple-element.15.near, bf16[208,512]{1,0:T(8,128)(2,1)S(1)} %pad_maximum_fusion.2.refs_0_, bf16[208,512]{1,0:T(8,128)(2,1)S(1)} %collective-permute-done.2.refs_1_, ...), custom_call_target="tpu_custom_call" | custom-call | flops 268435456 | bytes 2097152 | tf_op jit(solution)/shard_map/whole/pallas_call | solution.py:281
  (4 shorter events, 0.1 us)
Async XLA Ops:
  1.6 10.2 %collective-permute-start = (bf16[128,512]{1,0:T(8,128)(2,1)S(1)}, bf16[128,512]{1,0:T(8,128)(2,1)S(1)}, u32[]{:S(2)}, u32[]{:S(2)}) collective-permute-start(bf16[128,512]{1,0:T(8,128)(2,1)S(1)} %constant_dynamic-slice_fusion.1), channel_id=1, source_target_pairs={{0,1},{1,0},{2,3},{3,2},{4,6},{5,7},{6,4},{7,5},{8,9},{9,8},{10,11... | collective-permute-start | bytes 393224 | tf_op jit(solution)/shard_map/ppermute | solution.py:213
  4.6 3.2 %copy-start.3 = (f32[512]{0:T(512)S(1)}, f32[512]{0:T(512)}, u32[]{:S(2)}) copy-start(f32[512]{0:T(512)} %param.10) | copy-start | bytes 6148
  4.6 3.3 %copy-start.4 = (f32[1,512]{1,0:T(1,128)S(1)}, f32[1,512]{1,0:T(1,128)}, u32[]{:S(2)}) copy-start(f32[1,512]{1,0:T(1,128)} %demand.1) | copy-start | bytes 6148
  4.7 7.1 %collective-permute-start.1 = (bf16[64,512]{1,0:T(8,128)(2,1)S(1)}, bf16[64,512]{1,0:T(8,128)(2,1)S(1)}, u32[]{:S(2)}, u32[]{:S(2)}) collective-permute-start(bf16[64,512]{1,0:T(8,128)(2,1)S(1)} %constant_dynamic-slice_fusion), channel_id=1, source_target_pairs={{0,3},{1,2},{2,1},{3,0},{4,7},{5,6},{6,5},{7,4},{8,11},{9,10},{10,... | collective-permute-start | bytes 196616 | tf_op jit(solution)/shard_map/ppermute | solution.py:213
  7.9 0.7 %copy-start.2 = (f32[512]{0:T(512)S(1)}, f32[512]{0:T(512)}, u32[]{:S(2)}) copy-start(f32[512]{0:T(512)} %param.9) | copy-start | bytes 6148
  7.9 0.7 %copy-start.1 = (s32[4,4]{1,0:T(4,128)S(1)}, s32[4,4]{1,0:T(4,128)}, u32[]{:S(2)}) copy-start(s32[4,4]{1,0:T(4,128)} %incidence.1) | copy-start | bytes 196
  7.9 0.7 %copy-start.5 = (s32[128]{0:T(128)S(1)}, s32[128]{0:T(128)}, u32[]{:S(2)}) copy-start(s32[128]{0:T(128)} %param.13) | copy-start | bytes 1540
  8.6 1.0 %copy-start = (bf16[512,512]{1,0:T(8,128)(2,1)S(1)}, bf16[512,512]{1,0:T(8,128)(2,1)}, u32[]{:S(2)}) copy-start(bf16[512,512]{1,0:T(8,128)(2,1)} %coupling.1) | copy-start | bytes 1572868
  11.8 9.3 %collective-permute-start.2 = (bf16[208,512]{1,0:T(8,128)(2,1)S(1)}, bf16[208,512]{1,0:T(8,128)(2,1)S(1)}, u32[]{:S(2)}, u32[]{:S(2)}) collective-permute-start(bf16[208,512]{1,0:T(8,128)(2,1)S(1)} %pad_maximum_fusion.2.refs_0_), channel_id=1, source_target_pairs={{0,8},{1,9},{2,10},{3,11},{4,12},{5,13},{6,14},{7,15},{8,0},{9,1},... | collective-permute-start | bytes 638984 | tf_op jit(solution)/shard_map/ppermute | solution.py:213
  13.4 11.2 %collective-permute-start.3 = (bf16[208,512]{1,0:T(8,128)(2,1)S(1)}, bf16[208,512]{1,0:T(8,128)(2,1)S(1)}, u32[]{:S(2)}, u32[]{:S(2)}) collective-permute-start(bf16[208,512]{1,0:T(8,128)(2,1)S(1)} %pad_maximum_fusion.2.refs_0_), channel_id=1, source_target_pairs={{0,16},{1,17},{2,18},{3,19},{4,20},{5,21},{6,22},{7,23},{8,24},{9,... | collective-permute-start | bytes 638984 | tf_op jit(solution)/shard_map/ppermute | solution.py:213
  14.9 6.2 %collective-permute-start.5 = (bf16[64,512]{1,0:T(8,128)(2,1)S(1)}, bf16[64,512]{1,0:T(8,128)(2,1)S(1)}, u32[]{:S(2)}, u32[]{:S(2)}) collective-permute-start(bf16[64,512]{1,0:T(8,128)(2,1)S(1)} %collective-permute-done.1), channel_id=1, source_target_pairs={{0,24},{1,25},{2,26},{3,27},{4,28},{5,29},{6,30},{7,31},{8,16},{9,... | collective-permute-start | bytes 196616 | tf_op jit(solution)/shard_map/ppermute | solution.py:213
  15.4 9.2 %collective-permute-start.4 = (bf16[144,512]{1,0:T(8,128)(2,1)S(1)}, bf16[144,512]{1,0:T(8,128)(2,1)S(1)}, u32[]{:S(2)}, u32[]{:S(2)}) collective-permute-start(bf16[144,512]{1,0:T(8,128)(2,1)S(1)} %get-tuple-element.19), channel_id=1, source_target_pairs={{0,1},{1,0},{2,3},{3,2},{4,6},{5,7},{6,4},{7,5},{8,9},{9,8},{10,11... | collective-permute-start | bytes 442376 | tf_op jit(solution)/shard_map/ppermute | solution.py:213
  16.0 8.6 %collective-permute-start.6 = (bf16[16,512]{1,0:T(8,128)(2,1)S(1)}, bf16[16,512]{1,0:T(8,128)(2,1)S(1)}, u32[]{:S(2)}, u32[]{:S(2)}) collective-permute-start(bf16[16,512]{1,0:T(8,128)(2,1)S(1)} %get-tuple-element.16), channel_id=1, source_target_pairs={{0,27},{1,26},{2,25},{3,24},{4,31},{5,30},{6,29},{7,28},{8,19},{9,... | collective-permute-start | bytes 49160 | tf_op jit(solution)/shard_map/ppermute | solution.py:213
  21.1 5.2 %collective-permute-start.7 = (bf16[480,512]{1,0:T(8,128)(2,1)S(1)}, bf16[480,512]{1,0:T(8,128)(2,1)S(1)}, u32[]{:S(2)}, u32[]{:S(2)}) collective-permute-start(bf16[480,512]{1,0:T(8,128)(2,1)S(1)} %pad_maximum_fusion), channel_id=1, source_target_pairs={{0,4},{1,5},{2,6},{3,7},{4,0},{5,1},{6,2},{7,3},{8,12},{9,13},{10,... | collective-permute-start | bytes 1474568 | tf_op jit(solution)/shard_map/ppermute | solution.py:213
  24.6 1.8 %collective-permute-start.8 = (bf16[368,512]{1,0:T(8,128)(2,1)S(1)}, bf16[368,512]{1,0:T(8,128)(2,1)S(1)}, u32[]{:S(2)}, u32[]{:S(2)}) collective-permute-start(bf16[368,512]{1,0:T(8,128)(2,1)S(1)} %pad_maximum_fusion.1), channel_id=1, source_target_pairs={{0,4},{1,5},{2,6},{3,7},{4,0},{5,1},{6,2},{7,3},{8,12},{9,13},{10,... | collective-permute-start | bytes 1130504 | tf_op jit(solution)/shard_map/ppermute | solution.py:213

commit v4 on v3

--- a/solution.py
+++ b/solution.py
@@ -80,7 +80,7 @@
     across[:TILE, :] = near[(chips - 1) * TILE:, :]
 
 
-def rounds(masked, blocks, cost, cap, mask, demand, share, fleet_count, spread_out,
+def rounds(masked, turned, blocks, cost, cap, mask, demand, share, fleet_count, spread_out,
            flows, duals, prices, centre, shifted):
     scenarios, total_rows = demand.shape
     block_arcs = cost.shape[1] // blocks
@@ -106,8 +106,7 @@
                 new = jnp.clip(old - primal_step * gradient, 0.0, cap[:, cols])
                 flows[:, cols] = new
                 bar = (2.0 * new - old).astype(jnp.bfloat16)
-                load = load + lax.dot_general(bar, masked(block), (((1,), (1,)), ((), ())),
-                                              preferred_element_type=jnp.float32)
+                load = load + jnp.dot(bar, turned(block), preferred_element_type=jnp.float32)
             step = dual_step * (load - demand[...])
             duals[...] = jnp.maximum(step if first else duals[...] + step, 0.0)
         squares = jnp.float32(0.0)
@@ -136,7 +135,7 @@
 def plain_kernel(masked, cost, cap, mask, demand, share, slots, flows_out, duals_out, mult_out, cons_out,
                  spread_out, flows, duals, prices, centre, shifted):
     blocks, total_rows, block_arcs = masked.shape
-    rounds(lambda block: masked[block], blocks, cost, cap, mask, demand, share, slots.shape[1] * blocks,
+    rounds(lambda block: masked[block], lambda block: masked[block].T, blocks, cost, cap, mask, demand, share, slots.shape[1] * blocks,
            spread_out, flows, duals, prices, centre, shifted)
     scen, arc = lax.axis_index("scen"), lax.axis_index("arc")
     own = pl.ds(pl.multiple_of(arc * block_arcs, block_arcs), block_arcs)
@@ -148,21 +147,21 @@
 
 
 def whole_kernel(near, *refs):
-    lines, others = refs[:6], [None] * 6
-    for packed, parts in ((refs[6], (0, 1, 4)), (refs[7], (2, 3, 5))):
+    lines, others = refs[:5], [None] * 5
+    for packed, parts in ((refs[6], (0, 1, 4)), (refs[7], (2, 3))):
         first = 0
         for part in parts:
             rows = lines[part].shape[0]
             others[part] = packed.at[pl.ds(first, rows)]
             first += rows
     (slots, flows_out, duals_out, mult_out, cons_out, spread_out,
-     blocks_in, cost, cap, mask, demand_in, demand, share, flows, duals, prices, centre, shifted) = refs[8:]
+     blocks_in, turned, cost, cap, mask, demand_in, demand, share, flows, duals, prices, centre, shifted) = refs[8:]
     total_rows, block_arcs = near.shape
     scen, arc = lax.axis_index("scen"), lax.axis_index("arc")
     chip, core = scen // 2, lax.rem(scen, 2)
     chips = total_rows // TILE
     half = TILE // 2
-    tails = [lines[0][TILE + half:, :], lines[3][TILE:, :], others[3][TILE:, :], lines[5][...]]
+    tails = [lines[0][TILE + half:, :], lines[3][TILE:, :], others[3][TILE:, :], refs[5][...]]
     touch = []
     for block, tail in enumerate(tails):
         cols = slice(block * block_arcs, (block + 1) * block_arcs)
@@ -173,7 +172,7 @@
         touch.append(tail[11:11 + chips].astype(jnp.bfloat16))
     for row in range(2 * chips):
         part, source = row // 2, others if row % 2 else lines
-        tail = source[part][TILE + half:, :] if part < chips - 1 else source[5][...]
+        tail = source[part][TILE + half:, :] if part < chips - 1 else source[4][half:, :]
         tail = tail.astype(jnp.float32)
         demand_in[row:row + 1, :] = tail[7:8] + tail[8:9] + tail[9:10]
         share[row:row + 1, :] = tail[10:11, :128] + tail[10:11, 128:256] + tail[10:11, 256:384]
@@ -184,18 +183,20 @@
         for side, source in enumerate((lines, others)):
             place = jnp.where(core == side, 0, half)
             place = pl.ds(pl.multiple_of(part * TILE + place, half), half)
-            on = touch[3][chips - 1 - part:chips - part]
+            on = touch[3][part:part + 1]
             if part < chips - 1:
                 blocks_in[side, rows, :] = source[part][:TILE, :] * touch[1 + side][part:part + 1]
                 blocks_in[2, place, :] = source[part][TILE:TILE + half, :] * on
             else:
                 blocks_in[side, rows, :] = source[3][:TILE, :]
-                blocks_in[2, place, :] = source[4][...] * on
+                blocks_in[2, place, :] = source[4][:half, :] * on
 
     def masked(block):
         return near[...] if block == 0 else blocks_in[block - 1]
 
-    rounds(masked, len(tails), cost, cap, mask, demand, share, slots.shape[1] * len(tails),
+    for block in range(len(tails)):
+        turned[block] = masked(block).T
+    rounds(masked, lambda block: turned[block], len(tails), cost, cap, mask, demand, share, slots.shape[1] * len(tails),
            spread_out, flows, duals, prices, centre, shifted)
     flows_out[...] = flows[0:1, :block_arcs]
     first = pl.multiple_of(jnp.bitwise_xor(chip, arc) * TILE, TILE)
@@ -226,10 +227,10 @@
     side = swap(line, lambda scen, arc: (scen ^ 2, arc))
     front = swap(line, lambda scen, arc: (scen ^ 4, arc))
     across = swap(across, lambda scen, arc: (scen, arc ^ (1 + scen % 2)))
-    beyond = swap(narrow, lambda scen, arc: (scen ^ 6, arc))
-    extra = swap(extra, lambda scen, arc: (scen ^ 6, arc ^ 3))
-    early = jnp.concatenate([line, side, beyond], axis=0)
-    late = jnp.concatenate([front, across, extra], axis=0)
+    beyond = swap(jnp.concatenate([narrow, extra], axis=0), lambda scen, arc: (scen ^ 6, arc))
+    extra = swap(extra, lambda scen, arc: (scen, arc ^ 3))
+    early = jnp.concatenate([line, side, beyond, extra], axis=0)
+    late = jnp.concatenate([front, across], axis=0)
     other = lambda scen, arc: (scen ^ 1, arc)
     return [line, side, front, across, beyond, extra, swap(early, other), swap(late, other)]
 
@@ -285,6 +286,7 @@
             out_specs=out_specs,
             scratch_shapes=[
                 pltpu.VMEM((blocks - 1, total_rows, block_arcs), jnp.bfloat16),
+                pltpu.VMEM((blocks, block_arcs, total_rows), jnp.bfloat16),
                 pltpu.VMEM((1, arcs), jnp.float32),
                 pltpu.VMEM((1, arcs), jnp.float32),
                 pltpu.VMEM((1, arcs), jnp.float32),

time: 34.6 us -> 33.3 us (0.962)
  starting transfers between devices: 15 us -> 12.3 us
  waiting for transfers between devices: 5.7 us -> 8.17 us
  Pallas kernels: 9.58 us -> 8.53 us
    ppermute x9, starting transfers between devices: 15 us -> 12.3 us  [swap(): return lax.ppermute(value, ('scen', 'arc'), pairs)]
    ppermute x9, waiting for transfers between devices: 5.7 us -> 8.17 us  [swap(): return lax.ppermute(value, ('scen', 'arc'), pairs)]
    pallas_call x1, Pallas kernels: 8.06 us -> 7.01 us  [body(): pl.pallas_call(whole_kernel, out_shape=out_shape, in_specs=[VMEM] * (len(...]
  transfers between devices with their start and end apart: 9 -> 9, of which waited for: 3 -> 5; matrix products, arithmetic and copies ran while one was open for 0% -> 0% of each run, Pallas kernels for 4% -> 5%
where the time goes in v4:
time: 33.3 us; the launch traced here: 33 us
  starting transfers between devices  12.3 us (37%)
  Pallas kernels  8.53 us (26%)
  waiting for transfers between devices  8.17 us (25%)
  local copies, waits for them, and re-layouts  2.63 us (8%)
  between operations  1.38 us (4%)
    ppermute x9, starting transfers between devices, swap(): return lax.ppermute(value, ('scen', 'arc'), pairs)  12.3 us
    ppermute x9, waiting for transfers between devices, swap(): return lax.ppermute(value, ('scen', 'arc'), pairs)  8.17 us
    pallas_call x1, Pallas kernels, body(): pl.pallas_call(whole_kernel, out_shape=out_shape, in_specs=[VMEM] * (len(...  7.01 us
    unnamed x12, local copies, waits for them, and re-layouts  1.71 us
    pallas_call x1, Pallas kernels, body(): pl.pallas_call(pack_kernel, out_shape=(like(total_rows), like(TILE + EXTR...  1.52 us
    dynamic_slice x1, local copies, waits for them, and re-layouts, bring(): lax.dynamic_slice_in_dim(coupling, lax.shift_right_logical(scen, 1) * TIL...  0.92 us
  transfers between devices with their start and end apart: 9, of which 5 were waited for; matrix products, arithmetic and copies ran while one was open for 0% of the time, Pallas kernels for 5%

profile of v4, /device:TPU:0, one launch (start us, length us, event | category | flops | bytes accessed | tf_op | source)
XLA Modules:
  0.0 33.0 jit_solution(15903101580605994022)
XLA Ops:
  0.6 0.9 %constant_dynamic-slice_fusion.1 = bf16[128,512]{1,0:T(8,128)(2,1)S(1)} fusion(bf16[512,512]{1,0:T(8,128)(2,1)} %coupling.1, s32[]{:T(128)S(6)} %select_n.6), kind=kLoop, calls=%fused_computation.5 | loop fusion | bytes 262148 | tf_op jit(solution)/shard_map/dynamic_slice | solution.py:220
  1.6 3.1 %collective-permute-start = (bf16[128,512]{1,0:T(8,128)(2,1)S(1)}, bf16[128,512]{1,0:T(8,128)(2,1)S(1)}, u32[]{:S(2)}, u32[]{:S(2)}) collective-permute-start(bf16[128,512]{1,0:T(8,128)(2,1)S(1)} %constant_dynamic-slice_fusion.1), channel_id=1, source_target_pairs={{0,1},{1,0},{2,3},{3,2},{4,6},{5,7},{6,4},{7,5},{8,9},{9,8},{10,11... | collective-permute-start | bytes 393224 | tf_op jit(solution)/shard_map/ppermute | solution.py:214
  4.6 0.0 copy-start.3
  4.6 0.0 copy-start.4
  4.7 2.5 %collective-permute-start.1 = (bf16[64,512]{1,0:T(8,128)(2,1)S(1)}, bf16[64,512]{1,0:T(8,128)(2,1)S(1)}, u32[]{:S(2)}, u32[]{:S(2)}) collective-permute-start(bf16[64,512]{1,0:T(8,128)(2,1)S(1)} %constant_dynamic-slice_fusion), channel_id=1, source_target_pairs={{0,3},{1,2},{2,1},{3,0},{4,7},{5,6},{6,5},{7,4},{8,11},{9,10},{10,... | collective-permute-start | bytes 196616 | tf_op jit(solution)/shard_map/ppermute | solution.py:214
  7.9 0.0 copy-start.2
  7.9 0.0 copy-start.1
  7.9 0.0 copy-start.5
  7.9 0.0 copy-done.3
  7.9 0.0 copy-done.4
  7.9 0.6 %copy-done.2 = f32[512]{0:T(512)S(1)} copy-done((f32[512]{0:T(512)S(1)}, f32[512]{0:T(512)}, u32[]{:S(2)}) %copy-start.2) | copy-done | bytes 2072
  8.5 0.0 copy-done.1
  8.6 0.0 copy-done.5
  8.6 0.0 copy-start
  8.6 1.0 %copy-done = bf16[512,512]{1,0:T(8,128)(2,1)S(1)} copy-done((bf16[512,512]{1,0:T(8,128)(2,1)S(1)}, bf16[512,512]{1,0:T(8,128)(2,1)}, u32[]{:S(2)}) %copy-start) | copy-done | bytes 524312
  9.6 1.5 %pack.1 = (bf16[512,512]{1,0:T(8,128)(2,1)S(1)}, bf16[144,512]{1,0:T(8,128)(2,1)S(1)}, bf16[16,512]{1,0:T(8,128)(2,1)S(1)}) custom-call(bf16[512,512]{1,0:T(8,128)(2,1)S(1)} %copy-done, s32[4,4]{1,0:T(4,128)S(1)} %copy-done.1, f32[1,512]{1,0:T(1,128)S(1)} %bitcast.6, f32[1,512]{1,0:T(1,128)S(1)} %bitcast.7, f32[1,512]{1,0:T(1,128)S(1)} %copy-done.4, ...), custom_call_target="tpu_custom_call" | custom-call | tf_op jit(solution)/shard_map/pack/pallas_call | solution.py:269
  11.1 0.6 %collective-permute-done.1 = bf16[64,512]{1,0:T(8,128)(2,1)S(1)} collective-permute-done((bf16[64,512]{1,0:T(8,128)(2,1)S(1)}, bf16[64,512]{1,0:T(8,128)(2,1)S(1)}, u32[]{:S(2)}, u32[]{:S(2)}) %collective-permute-start.1) | collective-permute-done | bytes 65568 | tf_op jit(solution)/shard_map/ppermute | solution.py:214
  11.8 0.0 collective-permute-done
  11.8 1.6 %collective-permute-start.2 = (bf16[208,512]{1,0:T(8,128)(2,1)S(1)}, bf16[208,512]{1,0:T(8,128)(2,1)S(1)}, u32[]{:S(2)}, u32[]{:S(2)}) collective-permute-start(bf16[208,512]{1,0:T(8,128)(2,1)S(1)} %pad_maximum_fusion.2.refs_0_), channel_id=1, source_target_pairs={{0,8},{1,9},{2,10},{3,11},{4,12},{5,13},{6,14},{7,15},{8,0},{9,1},... | collective-permute-start | bytes 638984 | tf_op jit(solution)/shard_map/ppermute | solution.py:214
  13.4 1.5 %collective-permute-start.5 = (bf16[80,512]{1,0:T(8,128)(2,1)S(1)}, bf16[80,512]{1,0:T(8,128)(2,1)S(1)}, u32[]{:S(2)}, u32[]{:S(2)}) collective-permute-start(bf16[80,512]{1,0:T(8,128)(2,1)S(1)} %pad_maximum_fusion.3), channel_id=1, source_target_pairs={{0,24},{1,25},{2,26},{3,27},{4,28},{5,29},{6,30},{7,31},{8,16},{9,... | collective-permute-start | bytes 245768 | tf_op jit(solution)/shard_map/ppermute | solution.py:214
  14.9 0.5 %collective-permute-start.3 = (bf16[208,512]{1,0:T(8,128)(2,1)S(1)}, bf16[208,512]{1,0:T(8,128)(2,1)S(1)}, u32[]{:S(2)}, u32[]{:S(2)}) collective-permute-start(bf16[208,512]{1,0:T(8,128)(2,1)S(1)} %pad_maximum_fusion.2.refs_0_), channel_id=1, source_target_pairs={{0,16},{1,17},{2,18},{3,19},{4,20},{5,21},{6,22},{7,23},{8,24},{9,... | collective-permute-start | bytes 638984 | tf_op jit(solution)/shard_map/ppermute | solution.py:214
  15.4 2.3 %collective-permute-start.6 = (bf16[16,512]{1,0:T(8,128)(2,1)S(1)}, bf16[16,512]{1,0:T(8,128)(2,1)S(1)}, u32[]{:S(2)}, u32[]{:S(2)}) collective-permute-start(bf16[16,512]{1,0:T(8,128)(2,1)S(1)} %get-tuple-element.16), channel_id=1, source_target_pairs={{0,3},{1,2},{2,1},{3,0},{4,7},{5,6},{6,5},{7,4},{8,11},{9,10},{10,... | collective-permute-start | bytes 49160 | tf_op jit(solution)/shard_map/ppermute | solution.py:214
  17.7 0.6 %collective-permute-start.4 = (bf16[144,512]{1,0:T(8,128)(2,1)S(1)}, bf16[144,512]{1,0:T(8,128)(2,1)S(1)}, u32[]{:S(2)}, u32[]{:S(2)}) collective-permute-start(bf16[144,512]{1,0:T(8,128)(2,1)S(1)} %get-tuple-element.19), channel_id=1, source_target_pairs={{0,1},{1,0},{2,3},{3,2},{4,6},{5,7},{6,4},{7,5},{8,9},{9,8},{10,11... | collective-permute-start | bytes 442376 | tf_op jit(solution)/shard_map/ppermute | solution.py:214
  18.3 2.9 %collective-permute-done.6.refs_5_ = bf16[16,512]{1,0:T(8,128)(2,1)S(1)} collective-permute-done((bf16[16,512]{1,0:T(8,128)(2,1)S(1)}, bf16[16,512]{1,0:T(8,128)(2,1)S(1)}, u32[]{:S(2)}, u32[]{:S(2)}) %collective-permute-start.6) | collective-permute-done | bytes 16416 | tf_op jit(solution)/shard_map/ppermute | solution.py:214
  21.2 0.1 collective-permute-done.5.refs_4_
  21.3 0.0 collective-permute-done.2.refs_1_
  21.3 0.1 collective-permute-start.7
  21.4 2.9 %collective-permute-done.4.refs_3_ = bf16[144,512]{1,0:T(8,128)(2,1)S(1)} collective-permute-done((bf16[144,512]{1,0:T(8,128)(2,1)S(1)}, bf16[144,512]{1,0:T(8,128)(2,1)S(1)}, u32[]{:S(2)}, u32[]{:S(2)}) %collective-permute-start.4) | collective-permute-done | bytes 147488 | tf_op jit(solution)/shard_map/ppermute | solution.py:214
  24.3 0.0 collective-permute-done.3.refs_2_
  24.3 0.1 collective-permute-start.8
  24.4 1.7 %collective-permute-done.8.refs_7_ = bf16[352,512]{1,0:T(8,128)(2,1)S(1)} collective-permute-done((bf16[352,512]{1,0:T(8,128)(2,1)S(1)}, bf16[352,512]{1,0:T(8,128)(2,1)S(1)}, u32[]{:S(2)}, u32[]{:S(2)}) %collective-permute-start.8) | collective-permute-done | bytes 360480 | tf_op jit(solution)/shard_map/ppermute | solution.py:214
  26.0 0.0 collective-permute-done.7.refs_6_
  26.0 7.0 %whole.1 = (f32[1,512]{1,0:T(1,128)}, f32[1,128]{1,0:T(1,128)}, f32[1,128]{1,0:T(1,128)}, f32[1,128]{1,0:T(1,128)}, f32[2]{0:T(128)}) custom-call(bf16[512,512]{1,0:T(8,128)(2,1)S(1)} %get-tuple-element.15.near, bf16[208,512]{1,0:T(8,128)(2,1)S(1)} %pad_maximum_fusion.2.refs_0_, bf16[208,512]{1,0:T(8,128)(2,1)S(1)} %collective-permute-done.2.refs_1_, ...), custom_call_target="tpu_custom_call" | custom-call | flops 268435456 | bytes 2097152 | tf_op jit(solution)/shard_map/whole/pallas_call | solution.py:282
  (5 shorter events, 0.1 us)
Async XLA Ops:
  1.6 10.2 %collective-permute-start = (bf16[128,512]{1,0:T(8,128)(2,1)S(1)}, bf16[128,512]{1,0:T(8,128)(2,1)S(1)}, u32[]{:S(2)}, u32[]{:S(2)}) collective-permute-start(bf16[128,512]{1,0:T(8,128)(2,1)S(1)} %constant_dynamic-slice_fusion.1), channel_id=1, source_target_pairs={{0,1},{1,0},{2,3},{3,2},{4,6},{5,7},{6,4},{7,5},{8,9},{9,8},{10,11... | collective-permute-start | bytes 393224 | tf_op jit(solution)/shard_map/ppermute | solution.py:214
  4.6 3.2 %copy-start.3 = (f32[512]{0:T(512)S(1)}, f32[512]{0:T(512)}, u32[]{:S(2)}) copy-start(f32[512]{0:T(512)} %param.10) | copy-start | bytes 6148
  4.6 3.3 %copy-start.4 = (f32[1,512]{1,0:T(1,128)S(1)}, f32[1,512]{1,0:T(1,128)}, u32[]{:S(2)}) copy-start(f32[1,512]{1,0:T(1,128)} %demand.1) | copy-start | bytes 6148
  4.7 7.1 %collective-permute-start.1 = (bf16[64,512]{1,0:T(8,128)(2,1)S(1)}, bf16[64,512]{1,0:T(8,128)(2,1)S(1)}, u32[]{:S(2)}, u32[]{:S(2)}) collective-permute-start(bf16[64,512]{1,0:T(8,128)(2,1)S(1)} %constant_dynamic-slice_fusion), channel_id=1, source_target_pairs={{0,3},{1,2},{2,1},{3,0},{4,7},{5,6},{6,5},{7,4},{8,11},{9,10},{10,... | collective-permute-start | bytes 196616 | tf_op jit(solution)/shard_map/ppermute | solution.py:214
  7.9 0.7 %copy-start.2 = (f32[512]{0:T(512)S(1)}, f32[512]{0:T(512)}, u32[]{:S(2)}) copy-start(f32[512]{0:T(512)} %param.9) | copy-start | bytes 6148
  7.9 0.7 %copy-start.1 = (s32[4,4]{1,0:T(4,128)S(1)}, s32[4,4]{1,0:T(4,128)}, u32[]{:S(2)}) copy-start(s32[4,4]{1,0:T(4,128)} %incidence.1) | copy-start | bytes 196
  7.9 0.7 %copy-start.5 = (s32[128]{0:T(128)S(1)}, s32[128]{0:T(128)}, u32[]{:S(2)}) copy-start(s32[128]{0:T(128)} %param.13) | copy-start | bytes 1540
  8.6 1.0 %copy-start = (bf16[512,512]{1,0:T(8,128)(2,1)S(1)}, bf16[512,512]{1,0:T(8,128)(2,1)}, u32[]{:S(2)}) copy-start(bf16[512,512]{1,0:T(8,128)(2,1)} %coupling.1) | copy-start | bytes 1572868
  11.8 9.5 %collective-permute-start.2 = (bf16[208,512]{1,0:T(8,128)(2,1)S(1)}, bf16[208,512]{1,0:T(8,128)(2,1)S(1)}, u32[]{:S(2)}, u32[]{:S(2)}) collective-permute-start(bf16[208,512]{1,0:T(8,128)(2,1)S(1)} %pad_maximum_fusion.2.refs_0_), channel_id=1, source_target_pairs={{0,8},{1,9},{2,10},{3,11},{4,12},{5,13},{6,14},{7,15},{8,0},{9,1},... | collective-permute-start | bytes 638984 | tf_op jit(solution)/shard_map/ppermute | solution.py:214
  13.4 7.9 %collective-permute-start.5 = (bf16[80,512]{1,0:T(8,128)(2,1)S(1)}, bf16[80,512]{1,0:T(8,128)(2,1)S(1)}, u32[]{:S(2)}, u32[]{:S(2)}) collective-permute-start(bf16[80,512]{1,0:T(8,128)(2,1)S(1)} %pad_maximum_fusion.3), channel_id=1, source_target_pairs={{0,24},{1,25},{2,26},{3,27},{4,28},{5,29},{6,30},{7,31},{8,16},{9,... | collective-permute-start | bytes 245768 | tf_op jit(solution)/shard_map/ppermute | solution.py:214
  14.9 9.4 %collective-permute-start.3 = (bf16[208,512]{1,0:T(8,128)(2,1)S(1)}, bf16[208,512]{1,0:T(8,128)(2,1)S(1)}, u32[]{:S(2)}, u32[]{:S(2)}) collective-permute-start(bf16[208,512]{1,0:T(8,128)(2,1)S(1)} %pad_maximum_fusion.2.refs_0_), channel_id=1, source_target_pairs={{0,16},{1,17},{2,18},{3,19},{4,20},{5,21},{6,22},{7,23},{8,24},{9,... | collective-permute-start | bytes 638984 | tf_op jit(solution)/shard_map/ppermute | solution.py:214
  15.4 5.8 %collective-permute-start.6 = (bf16[16,512]{1,0:T(8,128)(2,1)S(1)}, bf16[16,512]{1,0:T(8,128)(2,1)S(1)}, u32[]{:S(2)}, u32[]{:S(2)}) collective-permute-start(bf16[16,512]{1,0:T(8,128)(2,1)S(1)} %get-tuple-element.16), channel_id=1, source_target_pairs={{0,3},{1,2},{2,1},{3,0},{4,7},{5,6},{6,5},{7,4},{8,11},{9,10},{10,... | collective-permute-start | bytes 49160 | tf_op jit(solution)/shard_map/ppermute | solution.py:214
  17.7 6.6 %collective-permute-start.4 = (bf16[144,512]{1,0:T(8,128)(2,1)S(1)}, bf16[144,512]{1,0:T(8,128)(2,1)S(1)}, u32[]{:S(2)}, u32[]{:S(2)}) collective-permute-start(bf16[144,512]{1,0:T(8,128)(2,1)S(1)} %get-tuple-element.19), channel_id=1, source_target_pairs={{0,1},{1,0},{2,3},{3,2},{4,6},{5,7},{6,4},{7,5},{8,9},{9,8},{10,11... | collective-permute-start | bytes 442376 | tf_op jit(solution)/shard_map/ppermute | solution.py:214
  21.3 4.7 %collective-permute-start.7 = (bf16[512,512]{1,0:T(8,128)(2,1)S(1)}, bf16[512,512]{1,0:T(8,128)(2,1)S(1)}, u32[]{:S(2)}, u32[]{:S(2)}) collective-permute-start(bf16[512,512]{1,0:T(8,128)(2,1)S(1)} %pad_maximum_fusion), channel_id=1, source_target_pairs={{0,4},{1,5},{2,6},{3,7},{4,0},{5,1},{6,2},{7,3},{8,12},{9,13},{10,... | collective-permute-start | bytes 1572872 | tf_op jit(solution)/shard_map/ppermute | solution.py:214
  24.3 1.7 %collective-permute-start.8 = (bf16[352,512]{1,0:T(8,128)(2,1)S(1)}, bf16[352,512]{1,0:T(8,128)(2,1)S(1)}, u32[]{:S(2)}, u32[]{:S(2)}) collective-permute-start(bf16[352,512]{1,0:T(8,128)(2,1)S(1)} %pad_maximum_fusion.1), channel_id=1, source_target_pairs={{0,4},{1,5},{2,6},{3,7},{4,0},{5,1},{6,2},{7,3},{8,12},{9,13},{10,... | collective-permute-start | bytes 1081352 | tf_op jit(solution)/shard_map/ppermute | solution.py:214

commit v5 on v4

--- a/solution.py
+++ b/solution.py
@@ -11,6 +11,7 @@
 ITERS = 4
 ROUNDS = 2
 EXTRA = 16
+GROUPS = ((0, 1, 2, 3, 4, 5, 6, 7),)
 
 primal_step = 0.9
 dual_step = 0.9
@@ -46,11 +47,39 @@
     return jnp.sum(jnp.where(rows == scen, value, 0.0), axis=0, keepdims=True)
 
 
-def pack_kernel(coupling, incidence, arc_cost, capacity, demand, weights, slots,
-                near, across, extra, rows_in, sems):
-    total_rows, block_arcs = rows_in.shape
+def narrow_kernel(coupling, incidence, arc_cost, capacity, demand, weights, slots, out, weight, sems):
+    half = out.shape[0] - EXTRA
+    block_arcs = out.shape[1]
+    scen = lax.axis_index("scen")
+    chip = scen // 2
+    first = pl.multiple_of(scen * half, half)
+    copies = [
+        pltpu.make_async_copy(weights, weight, sems.at[0]),
+        pltpu.make_async_copy(coupling.at[pl.ds(first, half)], out.at[pl.ds(0, half)], sems.at[1]),
+    ]
+    for copy in copies:
+        copy.start()
+    mask = fleet_mask(slots[...], block_arcs)
+    touch = []
+    for part in range(incidence.shape[0]):
+        owner = jnp.bitwise_xor(chip, part)
+        touch.append(jnp.concatenate(
+            [jnp.full((1, TILE), incidence[owner, tile].astype(jnp.float32))
+             for tile in range(block_arcs // TILE)], axis=1))
+    copies[0].wait()
+    share = jnp.full((1, 128), weight[0].astype(jnp.float32))
+    share = jnp.concatenate([*pieces(share), jnp.zeros((1, 128), jnp.bfloat16)], axis=1)
+    lines = [*pieces(arc_cost[...]), *pieces(capacity[...]), mask, *pieces(demand[...]), share, *touch]
+    lines = [line.astype(jnp.float32) for line in lines]
+    lines += [jnp.zeros((1, block_arcs), jnp.float32)] * (EXTRA - len(lines))
+    out[half:, :] = jnp.concatenate(lines, axis=0).astype(jnp.bfloat16)
+    copies[1].wait()
+
+
+def pack_kernel(coupling, narrow, near, across, rows_in, sems):
+    half = TILE // 2
     chip = lax.axis_index("scen") // 2
-    chips = total_rows // TILE
+    chips = rows_in.shape[0] // TILE
     copies = []
     for part in range(chips):
         first = pl.multiple_of(jnp.bitwise_xor(chip, part) * TILE, TILE)
@@ -58,25 +87,13 @@
             coupling.at[pl.ds(first, TILE)], rows_in.at[pl.ds(part * TILE, TILE)], sems.at[part]))
     for copy in copies:
         copy.start()
-    share = jnp.broadcast_to(weights[...].astype(jnp.float32), (1, 128))
-    share = jnp.concatenate([*pieces(share), jnp.zeros((1, 128), jnp.bfloat16)], axis=1)
-    mask = fleet_mask(slots[...], block_arcs)
-    touch = []
-    for part in range(chips):
-        owner = jnp.bitwise_xor(chip, part)
-        touch.append(jnp.concatenate(
-            [jnp.full((1, TILE), incidence[owner, tile].astype(jnp.float32))
-             for tile in range(block_arcs // TILE)], axis=1))
-    lines = [*pieces(arc_cost[...]), *pieces(capacity[...]), mask, *pieces(demand[...]), share, *touch]
-    lines = [line.astype(jnp.float32) for line in lines]
-    lines += [jnp.zeros((1, block_arcs), jnp.float32)] * (EXTRA - len(lines))
-    lines = jnp.concatenate(lines, axis=0).astype(jnp.bfloat16)
-    extra[...] = lines
-    across[TILE:, :] = lines
+    extra = narrow[half:, :]
+    across[TILE:, :] = extra
+    touch = extra.astype(jnp.float32)[11:11 + chips].astype(jnp.bfloat16)
     for part in range(chips):
         copies[part].wait()
         rows = slice(part * TILE, (part + 1) * TILE)
-        near[rows, :] = rows_in[rows, :] * touch[part].astype(jnp.bfloat16)
+        near[rows, :] = rows_in[rows, :] * touch[part:part + 1]
     across[:TILE, :] = near[(chips - 1) * TILE:, :]
 
 
@@ -146,22 +163,23 @@
     mult_out[...], cons_out[...] = pick_fleet(own_row(prices[:, own], scen), centre[:, own], slots[...])
 
 
-def whole_kernel(near, *refs):
-    lines, others = refs[:5], [None] * 5
-    for packed, parts in ((refs[6], (0, 1, 4)), (refs[7], (2, 3))):
+def whole_kernel(near, own, *refs):
+    brought, others = refs[:8], [None] * 8
+    for group, joined in zip(GROUPS, refs[8:]):
         first = 0
-        for part in parts:
-            rows = lines[part].shape[0]
-            others[part] = packed.at[pl.ds(first, rows)]
+        for part in group:
+            rows = brought[part].shape[0]
+            others[part] = joined.at[pl.ds(first, rows)]
             first += rows
+    wides, narrows = (brought[:4], others[:4]), (brought[4:], others[4:])
     (slots, flows_out, duals_out, mult_out, cons_out, spread_out,
-     blocks_in, turned, cost, cap, mask, demand_in, demand, share, flows, duals, prices, centre, shifted) = refs[8:]
+     blocks_in, turned, cost, cap, mask, demand_in, demand, share, flows, duals, prices, centre, shifted) = refs[8 + len(GROUPS):]
     total_rows, block_arcs = near.shape
     scen, arc = lax.axis_index("scen"), lax.axis_index("arc")
     chip, core = scen // 2, lax.rem(scen, 2)
     chips = total_rows // TILE
     half = TILE // 2
-    tails = [lines[0][TILE + half:, :], lines[3][TILE:, :], others[3][TILE:, :], refs[5][...]]
+    tails = [own[TILE:, :], wides[0][3][TILE:, :], wides[1][3][TILE:, :], narrows[0][0][half:, :]]
     touch = []
     for block, tail in enumerate(tails):
         cols = slice(block * block_arcs, (block + 1) * block_arcs)
@@ -171,25 +189,21 @@
         mask[:, cols] = tail[6:7]
         touch.append(tail[11:11 + chips].astype(jnp.bfloat16))
     for row in range(2 * chips):
-        part, source = row // 2, others if row % 2 else lines
-        tail = source[part][TILE + half:, :] if part < chips - 1 else source[4][half:, :]
-        tail = tail.astype(jnp.float32)
+        tail = narrows[row % 2][row // 2][half:, :].astype(jnp.float32)
         demand_in[row:row + 1, :] = tail[7:8] + tail[8:9] + tail[9:10]
         share[row:row + 1, :] = tail[10:11, :128] + tail[10:11, 128:256] + tail[10:11, 256:384]
     for part in range(chips):
         owner = jnp.bitwise_xor(chip, part)
         rows = slice(part * TILE, (part + 1) * TILE)
         demand[:, rows] = demand_in[:, pl.ds(pl.multiple_of(owner * TILE, TILE), TILE)]
-        for side, source in enumerate((lines, others)):
+        for side in range(2):
+            wide = wides[side][part][:TILE, :]
+            if part < chips - 1:
+                wide = wide * touch[1 + side][part:part + 1]
+            blocks_in[side, rows, :] = wide
             place = jnp.where(core == side, 0, half)
             place = pl.ds(pl.multiple_of(part * TILE + place, half), half)
-            on = touch[3][part:part + 1]
-            if part < chips - 1:
-                blocks_in[side, rows, :] = source[part][:TILE, :] * touch[1 + side][part:part + 1]
-                blocks_in[2, place, :] = source[part][TILE:TILE + half, :] * on
-            else:
-                blocks_in[side, rows, :] = source[3][:TILE, :]
-                blocks_in[2, place, :] = source[4][:half, :] * on
+            blocks_in[2, place, :] = narrows[side][part][:half, :] * touch[3][part:part + 1]
 
     def masked(block):
         return near[...] if block == 0 else blocks_in[block - 1]
@@ -214,25 +228,19 @@
     return lax.ppermute(value, ("scen", "arc"), pairs)
 
 
-def bring(coupling, across, extra):
+def bring(coupling, narrow, across):
     scen = lax.axis_index("scen")
-    half = TILE // 2
     wide = lax.dynamic_slice_in_dim(coupling, lax.shift_right_logical(scen, 1) * TILE, TILE, 0)
-    wide = lax.optimization_barrier(wide)
-    narrow = lax.dynamic_slice_in_dim(wide, (scen & 1) * half, half, 0)
     wide = swap(wide, lambda scen, arc: (scen, arc ^ (1 + scen % 2)))
-    narrow = swap(narrow, lambda scen, arc: (scen, arc ^ 3))
-    line = jnp.concatenate([wide, narrow, extra], axis=0)
-    line, across = lax.optimization_barrier((line, across))
-    side = swap(line, lambda scen, arc: (scen ^ 2, arc))
-    front = swap(line, lambda scen, arc: (scen ^ 4, arc))
-    across = swap(across, lambda scen, arc: (scen, arc ^ (1 + scen % 2)))
-    beyond = swap(jnp.concatenate([narrow, extra], axis=0), lambda scen, arc: (scen ^ 6, arc))
-    extra = swap(extra, lambda scen, arc: (scen, arc ^ 3))
-    early = jnp.concatenate([line, side, beyond, extra], axis=0)
-    late = jnp.concatenate([front, across], axis=0)
+    line = swap(narrow, lambda scen, arc: (scen, arc ^ 3))
+    side, front = (lambda scen, arc: (scen ^ 2, arc)), (lambda scen, arc: (scen ^ 4, arc))
+    wides = [wide, swap(wide, side), swap(wide, front)]
+    wides.append(swap(across, lambda scen, arc: (scen, arc ^ (1 + scen % 2))))
+    narrows = [line, swap(line, side), swap(line, front), swap(line, lambda scen, arc: (scen ^ 6, arc))]
     other = lambda scen, arc: (scen ^ 1, arc)
-    return [line, side, front, across, beyond, extra, swap(early, other), swap(late, other)]
+    brought = wides + narrows
+    joined = [jnp.concatenate([brought[part] for part in group], axis=0) for group in GROUPS]
+    return brought + [swap(parts, other) for parts in joined]
 
 
 def body(coupling, incidence, arc_cost, capacity, demand, weights, fleet_slots):
@@ -266,23 +274,32 @@
     fits = (scenarios, blocks) == (8, 4)
     if fits and total_rows == TILE * 4:
         like = lambda rows: jax.ShapeDtypeStruct((rows, block_arcs), jnp.bfloat16)
-        near, across, extra = pl.pallas_call(
+        narrow = pl.pallas_call(
+            narrow_kernel,
+            out_shape=like(TILE // 2 + EXTRA),
+            in_specs=[ANY, SMEM, VMEM, VMEM, VMEM, ANY, VMEM],
+            out_specs=VMEM,
+            scratch_shapes=[pltpu.SMEM((1,), jnp.int32), pltpu.SemaphoreType.DMA((2,))],
+            compiler_params=limit(56),
+            name="narrow",
+        )(coupling, incidence, row(arc_cost), row(capacity), demand, weights, slots)
+        near, across = pl.pallas_call(
             pack_kernel,
-            out_shape=(like(total_rows), like(TILE + EXTRA), like(EXTRA)),
-            in_specs=[ANY, SMEM, VMEM, VMEM, VMEM, VMEM, VMEM],
-            out_specs=(VMEM,) * 3,
+            out_shape=(like(total_rows), like(TILE + EXTRA)),
+            in_specs=[ANY, VMEM],
+            out_specs=(VMEM,) * 2,
             scratch_shapes=[
                 pltpu.VMEM((total_rows, block_arcs), jnp.bfloat16),
                 pltpu.SemaphoreType.DMA((total_rows // TILE,)),
             ],
             compiler_params=limit(8),
             name="pack",
-        )(coupling, incidence, row(arc_cost), row(capacity), demand, weights.reshape(1, 1), slots)
-        brought = bring(coupling, across, extra)
+        )(coupling, narrow)
+        brought = bring(coupling, narrow, across)
         outs = pl.pallas_call(
             whole_kernel,
             out_shape=out_shape,
-            in_specs=[VMEM] * (len(brought) + 2),
+            in_specs=[VMEM] * (len(brought) + 3),
             out_specs=out_specs,
             scratch_shapes=[
                 pltpu.VMEM((blocks - 1, total_rows, block_arcs), jnp.bfloat16),
@@ -298,7 +315,7 @@
             compiler_params=limit(16),
             cost_estimate=cost,
             name="whole",
-        )(near, *brought, slots)
+        )(near, across, *brought, slots)
     else:
         masked = (
             coupling.reshape(total_rows // TILE, TILE, block_arcs // TILE, TILE)

time: 33.3 us -> 34.6 us (1.039)
  Pallas kernels: 8.53 us -> 10.1 us
  starting transfers between devices: 12.3 us -> 13 us
  local copies, waits for them, and re-layouts: 2.63 us -> 1.95 us
    pallas_call x0 -> x1, Pallas kernels: none -> 2.33 us  [body(): pl.pallas_call(narrow_kernel, out_shape=like(TILE // 2 + EXTRA), in_specs...]
    ppermute x9, starting transfers between devices: 12.3 us -> 13 us  [swap(): return lax.ppermute(value, ('scen', 'arc'), pairs)]
    pallas_call x1, Pallas kernels: 1.52 us -> 0.74 us  [body(): pl.pallas_call(pack_kernel, out_shape=(like(total_rows), like(TILE + EXTR...]
    unnamed x12 -> x13, local copies, waits for them, and re-layouts: 1.71 us -> 0.96 us
  transfers between devices with their start and end apart: 9 -> 9, of which waited for: 5 -> 3; matrix products, arithmetic and copies ran while one was open for 0% -> 0% of each run, Pallas kernels for 5% -> 9%
where the time goes in v5:
time: 34.6 us; the launch traced here: 34.3 us
  starting transfers between devices  13 us (38%)
  Pallas kernels  10.1 us (29%)
  waiting for transfers between devices  7.84 us (23%)
  local copies, waits for them, and re-layouts  1.95 us (6%)
  between operations  1.43 us (4%)
    ppermute x9, starting transfers between devices, swap(): return lax.ppermute(value, ('scen', 'arc'), pairs)  13 us
    ppermute x9, waiting for transfers between devices, swap(): return lax.ppermute(value, ('scen', 'arc'), pairs)  7.84 us
    pallas_call x1, Pallas kernels, body(): pl.pallas_call(whole_kernel, out_shape=out_shape, in_specs=[VMEM] * (len(...  7.01 us
    pallas_call x1, Pallas kernels, body(): pl.pallas_call(narrow_kernel, out_shape=like(TILE // 2 + EXTRA), in_specs...  2.33 us
    dynamic_slice x1, local copies, waits for them, and re-layouts, bring(): lax.dynamic_slice_in_dim(coupling, lax.shift_right_logical(scen, 1) * TIL...  0.97 us
    unnamed x13, local copies, waits for them, and re-layouts  0.96 us
    pallas_call x1, Pallas kernels, body(): pl.pallas_call(pack_kernel, out_shape=(like(total_rows), like(TILE + EXTR...  0.74 us
  transfers between devices with their start and end apart: 9, of which 3 were waited for; matrix products, arithmetic and copies ran while one was open for 0% of the time, Pallas kernels for 9%

profile of v5, /device:TPU:0, one launch (start us, length us, event | category | flops | bytes accessed | tf_op | source)
XLA Modules:
  0.0 34.3 jit_solution(6352348010372219624)
XLA Ops:
  0.6 0.0 copy-start
  0.6 1.0 %constant_dynamic-slice_fusion = bf16[128,512]{1,0:T(8,128)(2,1)S(1)} fusion(bf16[512,512]{1,0:T(8,128)(2,1)} %coupling.3, s32[]{:T(128)S(6)} %select_n.3), kind=kLoop, calls=%fused_computation.8 | loop fusion | bytes 262148 | tf_op jit(solution)/shard_map/dynamic_slice | solution.py:233
  1.6 3.1 %collective-permute-start = (bf16[128,512]{1,0:T(8,128)(2,1)S(1)}, bf16[128,512]{1,0:T(8,128)(2,1)S(1)}, u32[]{:S(2)}, u32[]{:S(2)}) collective-permute-start(bf16[128,512]{1,0:T(8,128)(2,1)S(1)} %constant_dynamic-slice_fusion), channel_id=1, source_target_pairs={{0,1},{1,0},{2,3},{3,2},{4,6},{5,7},{6,4},{7,5},{8,9},{9,8},{10,11... | collective-permute-start | bytes 393224 | tf_op jit(solution)/shard_map/ppermute | solution.py:228
  5.4 2.3 %narrow.1 = bf16[80,512]{1,0:T(8,128)(2,1)} custom-call(bf16[512,512]{1,0:T(8,128)(2,1)} %coupling.3, s32[4,4]{1,0:T(4,128)} %incidence.1, f32[1,512]{1,0:T(1,128)} %bitcast.6, f32[1,512]{1,0:T(1,128)} %bitcast.7, f32[1,512]{1,0:T(1,128)} %demand.1, s32[1]{0:T(128)S(6)} %copy.19.weights, s32[1,128]{1,0:T(1,128)} %bitcast.4), custom_call_target="tpu_custom_call" | custom-call | tf_op jit(solution)/shard_map/narrow/pallas_call | solution.py:277
  7.7 2.5 %collective-permute-start.4 = (bf16[80,512]{1,0:T(8,128)(2,1)}, bf16[80,512]{1,0:T(8,128)(2,1)S(1)}, u32[]{:S(2)}, u32[]{:S(2)}) collective-permute-start(bf16[80,512]{1,0:T(8,128)(2,1)} %narrow.1), channel_id=1, source_target_pairs={{0,3},{1,2},{2,1},{3,0},{4,7},{5,6},{6,5},{7,4},{8,11},{9,10},{10,... | collective-permute-start | bytes 245768 | tf_op jit(solution)/shard_map/ppermute | solution.py:228
  10.2 0.0 collective-permute-done.refs_0_
  10.2 1.5 %collective-permute-start.1 = (bf16[128,512]{1,0:T(8,128)(2,1)S(1)}, bf16[128,512]{1,0:T(8,128)(2,1)S(1)}, u32[]{:S(2)}, u32[]{:S(2)}) collective-permute-start(bf16[128,512]{1,0:T(8,128)(2,1)S(1)} %collective-permute-done.refs_0_), channel_id=1, source_target_pairs={{0,8},{1,9},{2,10},{3,11},{4,12},{5,13},{6,14},{7,15},{8,0},{9,1},... | collective-permute-start | bytes 393224 | tf_op jit(solution)/shard_map/ppermute | solution.py:228
  11.7 0.0 copy-done
  11.7 0.0 copy-start.1
  11.7 0.9 %copy-done.1 = bf16[80,512]{1,0:T(8,128)(2,1)S(1)} copy-done((bf16[80,512]{1,0:T(8,128)(2,1)S(1)}, bf16[80,512]{1,0:T(8,128)(2,1)}, u32[]{:S(2)}) %copy-start.1) | copy-done | bytes 81944
  12.6 0.7 %pack.1 = (bf16[512,512]{1,0:T(8,128)(2,1)S(1)}, bf16[144,512]{1,0:T(8,128)(2,1)S(1)}) custom-call(bf16[512,512]{1,0:T(8,128)(2,1)S(1)} %copy-done, bf16[80,512]{1,0:T(8,128)(2,1)S(1)} %copy-done.1), custom_call_target="tpu_custom_call" | custom-call | tf_op jit(solution)/shard_map/pack/pallas_call | solution.py:286
  13.4 0.8 %collective-permute-start.3 = (bf16[144,512]{1,0:T(8,128)(2,1)S(1)}, bf16[144,512]{1,0:T(8,128)(2,1)S(1)}, u32[]{:S(2)}, u32[]{:S(2)}) collective-permute-start(bf16[144,512]{1,0:T(8,128)(2,1)S(1)} %get-tuple-element.13.own), channel_id=1, source_target_pairs={{0,1},{1,0},{2,3},{3,2},{4,6},{5,7},{6,4},{7,5},{8,9},{9,8},{10,11... | collective-permute-start | bytes 442376 | tf_op jit(solution)/shard_map/ppermute | solution.py:228
  14.2 0.6 %collective-permute-done.4.refs_4_ = bf16[80,512]{1,0:T(8,128)(2,1)S(1)} collective-permute-done((bf16[80,512]{1,0:T(8,128)(2,1)}, bf16[80,512]{1,0:T(8,128)(2,1)S(1)}, u32[]{:S(2)}, u32[]{:S(2)}) %collective-permute-start.4) | collective-permute-done | bytes 81952 | tf_op jit(solution)/shard_map/ppermute | solution.py:228
  14.8 2.4 %collective-permute-start.7 = (bf16[80,512]{1,0:T(8,128)(2,1)S(1)}, bf16[80,512]{1,0:T(8,128)(2,1)S(1)}, u32[]{:S(2)}, u32[]{:S(2)}) collective-permute-start(bf16[80,512]{1,0:T(8,128)(2,1)S(1)} %collective-permute-done.4.refs_4_), channel_id=1, source_target_pairs={{0,24},{1,25},{2,26},{3,27},{4,28},{5,29},{6,30},{7,31},{8,16},{9,... | collective-permute-start | bytes 245768 | tf_op jit(solution)/shard_map/ppermute | solution.py:228
  17.2 0.5 %collective-permute-start.6 = (bf16[80,512]{1,0:T(8,128)(2,1)S(1)}, bf16[80,512]{1,0:T(8,128)(2,1)S(1)}, u32[]{:S(2)}, u32[]{:S(2)}) collective-permute-start(bf16[80,512]{1,0:T(8,128)(2,1)S(1)} %collective-permute-done.4.refs_4_), channel_id=1, source_target_pairs={{0,16},{1,17},{2,18},{3,19},{4,20},{5,21},{6,22},{7,23},{8,24},{9,... | collective-permute-start | bytes 245768 | tf_op jit(solution)/shard_map/ppermute | solution.py:228
  17.8 1.5 %collective-permute-start.2 = (bf16[128,512]{1,0:T(8,128)(2,1)S(1)}, bf16[128,512]{1,0:T(8,128)(2,1)S(1)}, u32[]{:S(2)}, u32[]{:S(2)}) collective-permute-start(bf16[128,512]{1,0:T(8,128)(2,1)S(1)} %collective-permute-done.refs_0_), channel_id=1, source_target_pairs={{0,16},{1,17},{2,18},{3,19},{4,20},{5,21},{6,22},{7,23},{8,24},{9,... | collective-permute-start | bytes 393224 | tf_op jit(solution)/shard_map/ppermute | solution.py:228
  19.3 0.0 collective-permute-done.1.refs_1_
  19.3 0.6 %collective-permute-start.5 = (bf16[80,512]{1,0:T(8,128)(2,1)S(1)}, bf16[80,512]{1,0:T(8,128)(2,1)S(1)}, u32[]{:S(2)}, u32[]{:S(2)}) collective-permute-start(bf16[80,512]{1,0:T(8,128)(2,1)S(1)} %collective-permute-done.4.refs_4_), channel_id=1, source_target_pairs={{0,8},{1,9},{2,10},{3,11},{4,12},{5,13},{6,14},{7,15},{8,0},{9,1},... | collective-permute-start | bytes 245768 | tf_op jit(solution)/shard_map/ppermute | solution.py:228
  19.9 4.8 %collective-permute-done.2.refs_2_ = bf16[128,512]{1,0:T(8,128)(2,1)S(1)} collective-permute-done((bf16[128,512]{1,0:T(8,128)(2,1)S(1)}, bf16[128,512]{1,0:T(8,128)(2,1)S(1)}, u32[]{:S(2)}, u32[]{:S(2)}) %collective-permute-start.2) | collective-permute-done | bytes 131104 | tf_op jit(solution)/shard_map/ppermute | solution.py:228
  24.7 0.0 collective-permute-done.3.refs_3_
  24.8 0.0 collective-permute-done.5.refs_5_
  24.8 0.0 collective-permute-done.6.refs_6_
  24.8 0.0 collective-permute-done.7.refs_7_
  24.8 0.0 copy-start.2
  24.9 0.1 collective-permute-start.8
  24.9 2.4 %collective-permute-done.8.refs_8_ = bf16[848,512]{1,0:T(8,128)(2,1)S(1)} collective-permute-done((bf16[848,512]{1,0:T(8,128)(2,1)S(1)}, bf16[848,512]{1,0:T(8,128)(2,1)S(1)}, u32[]{:S(2)}, u32[]{:S(2)}) %collective-permute-start.8) | collective-permute-done | bytes 868384 | tf_op jit(solution)/shard_map/ppermute | solution.py:228
  27.3 0.0 copy-done.2
  27.3 7.0 %whole.1 = (f32[1,512]{1,0:T(1,128)}, f32[1,128]{1,0:T(1,128)}, f32[1,128]{1,0:T(1,128)}, f32[1,128]{1,0:T(1,128)}, f32[2]{0:T(128)}) custom-call(bf16[512,512]{1,0:T(8,128)(2,1)S(1)} %get-tuple-element.12.near, bf16[144,512]{1,0:T(8,128)(2,1)S(1)} %get-tuple-element.13.own, bf16[128,512]{1,0:T(8,128)(2,1)S(1)} %collective-permute-done.refs_0_, ...), custom_call_target="tpu_custom_call" | custom-call | flops 268435456 | bytes 2097152 | tf_op jit(solution)/shard_map/whole/pallas_call | solution.py:299
  (8 shorter events, 0.1 us)
Async XLA Ops:
  0.6 11.1 %copy-start = (bf16[512,512]{1,0:T(8,128)(2,1)S(1)}, bf16[512,512]{1,0:T(8,128)(2,1)}, u32[]{:S(2)}) copy-start(bf16[512,512]{1,0:T(8,128)(2,1)} %coupling.3) | copy-start | bytes 1572868
  1.6 8.6 %collective-permute-start = (bf16[128,512]{1,0:T(8,128)(2,1)S(1)}, bf16[128,512]{1,0:T(8,128)(2,1)S(1)}, u32[]{:S(2)}, u32[]{:S(2)}) collective-permute-start(bf16[128,512]{1,0:T(8,128)(2,1)S(1)} %constant_dynamic-slice_fusion), channel_id=1, source_target_pairs={{0,1},{1,0},{2,3},{3,2},{4,6},{5,7},{6,4},{7,5},{8,9},{9,8},{10,11... | collective-permute-start | bytes 393224 | tf_op jit(solution)/shard_map/ppermute | solution.py:228
  7.7 7.1 %collective-permute-start.4 = (bf16[80,512]{1,0:T(8,128)(2,1)}, bf16[80,512]{1,0:T(8,128)(2,1)S(1)}, u32[]{:S(2)}, u32[]{:S(2)}) collective-permute-start(bf16[80,512]{1,0:T(8,128)(2,1)} %narrow.1), channel_id=1, source_target_pairs={{0,3},{1,2},{2,1},{3,0},{4,7},{5,6},{6,5},{7,4},{8,11},{9,10},{10,... | collective-permute-start | bytes 245768 | tf_op jit(solution)/shard_map/ppermute | solution.py:228
  10.2 9.0 %collective-permute-start.1 = (bf16[128,512]{1,0:T(8,128)(2,1)S(1)}, bf16[128,512]{1,0:T(8,128)(2,1)S(1)}, u32[]{:S(2)}, u32[]{:S(2)}) collective-permute-start(bf16[128,512]{1,0:T(8,128)(2,1)S(1)} %collective-permute-done.refs_0_), channel_id=1, source_target_pairs={{0,8},{1,9},{2,10},{3,11},{4,12},{5,13},{6,14},{7,15},{8,0},{9,1},... | collective-permute-start | bytes 393224 | tf_op jit(solution)/shard_map/ppermute | solution.py:228
  11.7 0.9 %copy-start.1 = (bf16[80,512]{1,0:T(8,128)(2,1)S(1)}, bf16[80,512]{1,0:T(8,128)(2,1)}, u32[]{:S(2)}) copy-start(bf16[80,512]{1,0:T(8,128)(2,1)} %narrow.1) | copy-start | bytes 245764
  13.4 11.3 %collective-permute-start.3 = (bf16[144,512]{1,0:T(8,128)(2,1)S(1)}, bf16[144,512]{1,0:T(8,128)(2,1)S(1)}, u32[]{:S(2)}, u32[]{:S(2)}) collective-permute-start(bf16[144,512]{1,0:T(8,128)(2,1)S(1)} %get-tuple-element.13.own), channel_id=1, source_target_pairs={{0,1},{1,0},{2,3},{3,2},{4,6},{5,7},{6,4},{7,5},{8,9},{9,8},{10,11... | collective-permute-start | bytes 442376 | tf_op jit(solution)/shard_map/ppermute | solution.py:228
  14.8 10.0 %collective-permute-start.7 = (bf16[80,512]{1,0:T(8,128)(2,1)S(1)}, bf16[80,512]{1,0:T(8,128)(2,1)S(1)}, u32[]{:S(2)}, u32[]{:S(2)}) collective-permute-start(bf16[80,512]{1,0:T(8,128)(2,1)S(1)} %collective-permute-done.4.refs_4_), channel_id=1, source_target_pairs={{0,24},{1,25},{2,26},{3,27},{4,28},{5,29},{6,30},{7,31},{8,16},{9,... | collective-permute-start | bytes 245768 | tf_op jit(solution)/shard_map/ppermute | solution.py:228
  17.2 7.5 %collective-permute-start.6 = (bf16[80,512]{1,0:T(8,128)(2,1)S(1)}, bf16[80,512]{1,0:T(8,128)(2,1)S(1)}, u32[]{:S(2)}, u32[]{:S(2)}) collective-permute-start(bf16[80,512]{1,0:T(8,128)(2,1)S(1)} %collective-permute-done.4.refs_4_), channel_id=1, source_target_pairs={{0,16},{1,17},{2,18},{3,19},{4,20},{5,21},{6,22},{7,23},{8,24},{9,... | collective-permute-start | bytes 245768 | tf_op jit(solution)/shard_map/ppermute | solution.py:228
  17.8 7.0 %collective-permute-start.2 = (bf16[128,512]{1,0:T(8,128)(2,1)S(1)}, bf16[128,512]{1,0:T(8,128)(2,1)S(1)}, u32[]{:S(2)}, u32[]{:S(2)}) collective-permute-start(bf16[128,512]{1,0:T(8,128)(2,1)S(1)} %collective-permute-done.refs_0_), channel_id=1, source_target_pairs={{0,16},{1,17},{2,18},{3,19},{4,20},{5,21},{6,22},{7,23},{8,24},{9,... | collective-permute-start | bytes 393224 | tf_op jit(solution)/shard_map/ppermute | solution.py:228
  19.3 5.5 %collective-permute-start.5 = (bf16[80,512]{1,0:T(8,128)(2,1)S(1)}, bf16[80,512]{1,0:T(8,128)(2,1)S(1)}, u32[]{:S(2)}, u32[]{:S(2)}) collective-permute-start(bf16[80,512]{1,0:T(8,128)(2,1)S(1)} %collective-permute-done.4.refs_4_), channel_id=1, source_target_pairs={{0,8},{1,9},{2,10},{3,11},{4,12},{5,13},{6,14},{7,15},{8,0},{9,1},... | collective-permute-start | bytes 245768 | tf_op jit(solution)/shard_map/ppermute | solution.py:228
  24.8 2.5 %copy-start.2 = (s32[128]{0:T(128)S(1)}, s32[128]{0:T(128)}, u32[]{:S(2)}) copy-start(s32[128]{0:T(128)} %param.13) | copy-start | bytes 1540
  24.9 2.5 %collective-permute-start.8 = (bf16[848,512]{1,0:T(8,128)(2,1)S(1)}, bf16[848,512]{1,0:T(8,128)(2,1)S(1)}, u32[]{:S(2)}, u32[]{:S(2)}) collective-permute-start(bf16[848,512]{1,0:T(8,128)(2,1)S(1)} %constant_dynamic-update-slice_fusion), channel_id=1, source_target_pairs={{0,4},{1,5},{2,6},{3,7},{4,0},{5,1},{6,2},{7,3},{8,12},{9,13},{10,... | collective-permute-start | bytes 2605064 | tf_op jit(solution)/shard_map/ppermute | solution.py:228

commit v6 on v4

--- a/solution.py
+++ b/solution.py
@@ -11,6 +11,7 @@
 ITERS = 4
 ROUNDS = 2
 EXTRA = 16
+GROUPS = ((0, 3, 4, 5), (1, 2))
 
 primal_step = 0.9
 dual_step = 0.9
@@ -147,15 +148,15 @@
 
 
 def whole_kernel(near, *refs):
-    lines, others = refs[:5], [None] * 5
-    for packed, parts in ((refs[6], (0, 1, 4)), (refs[7], (2, 3))):
+    lines, others = refs[:6], [None] * 6
+    for group, joined in zip(GROUPS, refs[6:]):
         first = 0
-        for part in parts:
+        for part in group:
             rows = lines[part].shape[0]
-            others[part] = packed.at[pl.ds(first, rows)]
+            others[part] = joined.at[pl.ds(first, rows)]
             first += rows
     (slots, flows_out, duals_out, mult_out, cons_out, spread_out,
-     blocks_in, turned, cost, cap, mask, demand_in, demand, share, flows, duals, prices, centre, shifted) = refs[8:]
+     blocks_in, turned, cost, cap, mask, demand_in, demand, share, flows, duals, prices, centre, shifted) = refs[6 + len(GROUPS):]
     total_rows, block_arcs = near.shape
     scen, arc = lax.axis_index("scen"), lax.axis_index("arc")
     chip, core = scen // 2, lax.rem(scen, 2)
@@ -229,10 +230,9 @@
     across = swap(across, lambda scen, arc: (scen, arc ^ (1 + scen % 2)))
     beyond = swap(jnp.concatenate([narrow, extra], axis=0), lambda scen, arc: (scen ^ 6, arc))
     extra = swap(extra, lambda scen, arc: (scen, arc ^ 3))
-    early = jnp.concatenate([line, side, beyond, extra], axis=0)
-    late = jnp.concatenate([front, across], axis=0)
-    other = lambda scen, arc: (scen ^ 1, arc)
-    return [line, side, front, across, beyond, extra, swap(early, other), swap(late, other)]
+    brought = [line, side, front, across, beyond, extra]
+    joined = [jnp.concatenate([brought[part] for part in group], axis=0) for group in GROUPS]
+    return brought + [swap(parts, lambda scen, arc: (scen ^ 1, arc)) for parts in joined]
 
 
 def body(coupling, incidence, arc_cost, capacity, demand, weights, fleet_slots):

time: 33.3 us -> 31.9 us (0.958)
  waiting for transfers between devices: 8.17 us -> 5.45 us
  starting transfers between devices: 12.3 us -> 13.6 us
    ppermute x9, waiting for transfers between devices: 8.17 us -> 5.45 us  [swap(): return lax.ppermute(value, ('scen', 'arc'), pairs)]
    ppermute x9, starting transfers between devices: 12.3 us -> 13.6 us  [swap(): return lax.ppermute(value, ('scen', 'arc'), pairs)]
  transfers between devices with their start and end apart: 9 -> 9, of which waited for: 5 -> 4; matrix products, arithmetic and copies ran while one was open for 0% -> 0% of each run, Pallas kernels for 5% -> 5%
where the time goes in v6:
time: 31.9 us; the launch traced here: 31.7 us
  starting transfers between devices  13.6 us (43%)
  Pallas kernels  8.53 us (27%)
  waiting for transfers between devices  5.45 us (17%)
  local copies, waits for them, and re-layouts  2.63 us (8%)
  between operations  1.4 us (4%)
    ppermute x9, starting transfers between devices, swap(): return lax.ppermute(value, ('scen', 'arc'), pairs)  13.6 us
    pallas_call x1, Pallas kernels, body(): pl.pallas_call(whole_kernel, out_shape=out_shape, in_specs=[VMEM] * (len(...  7.01 us
    ppermute x9, waiting for transfers between devices, swap(): return lax.ppermute(value, ('scen', 'arc'), pairs)  5.45 us
    unnamed x12, local copies, waits for them, and re-layouts  1.71 us
    pallas_call x1, Pallas kernels, body(): pl.pallas_call(pack_kernel, out_shape=(like(total_rows), like(TILE + EXTR...  1.52 us
    dynamic_slice x1, local copies, waits for them, and re-layouts, bring(): lax.dynamic_slice_in_dim(coupling, lax.shift_right_logical(scen, 1) * TIL...  0.92 us
  transfers between devices with their start and end apart: 9, of which 4 were waited for; matrix products, arithmetic and copies ran while one was open for 0% of the time, Pallas kernels for 5%

profile of v6, /device:TPU:0, one launch (start us, length us, event | category | flops | bytes accessed | tf_op | source)
XLA Modules:
  0.0 31.7 jit_solution(12512549233071879895)
XLA Ops:
  0.6 0.9 %constant_dynamic-slice_fusion.1 = bf16[128,512]{1,0:T(8,128)(2,1)S(1)} fusion(bf16[512,512]{1,0:T(8,128)(2,1)} %coupling.1, s32[]{:T(128)S(6)} %select_n.6), kind=kLoop, calls=%fused_computation.5 | loop fusion | bytes 262148 | tf_op jit(solution)/shard_map/dynamic_slice | solution.py:221
  1.6 3.1 %collective-permute-start = (bf16[128,512]{1,0:T(8,128)(2,1)S(1)}, bf16[128,512]{1,0:T(8,128)(2,1)S(1)}, u32[]{:S(2)}, u32[]{:S(2)}) collective-permute-start(bf16[128,512]{1,0:T(8,128)(2,1)S(1)} %constant_dynamic-slice_fusion.1), channel_id=1, source_target_pairs={{0,1},{1,0},{2,3},{3,2},{4,6},{5,7},{6,4},{7,5},{8,9},{9,8},{10,11... | collective-permute-start | bytes 393224 | tf_op jit(solution)/shard_map/ppermute | solution.py:215
  4.6 0.0 copy-start.3
  4.6 0.0 copy-start.4
  4.7 2.5 %collective-permute-start.1 = (bf16[64,512]{1,0:T(8,128)(2,1)S(1)}, bf16[64,512]{1,0:T(8,128)(2,1)S(1)}, u32[]{:S(2)}, u32[]{:S(2)}) collective-permute-start(bf16[64,512]{1,0:T(8,128)(2,1)S(1)} %constant_dynamic-slice_fusion), channel_id=1, source_target_pairs={{0,3},{1,2},{2,1},{3,0},{4,7},{5,6},{6,5},{7,4},{8,11},{9,10},{10,... | collective-permute-start | bytes 196616 | tf_op jit(solution)/shard_map/ppermute | solution.py:215
  7.9 0.0 copy-start.2
  7.9 0.0 copy-start.1
  7.9 0.0 copy-start.5
  7.9 0.0 copy-done.3
  7.9 0.0 copy-done.4
  7.9 0.6 %copy-done.2 = f32[512]{0:T(512)S(1)} copy-done((f32[512]{0:T(512)S(1)}, f32[512]{0:T(512)}, u32[]{:S(2)}) %copy-start.2) | copy-done | bytes 2072
  8.5 0.0 copy-done.1
  8.6 0.0 copy-done.5
  8.6 0.0 copy-start
  8.6 1.0 %copy-done = bf16[512,512]{1,0:T(8,128)(2,1)S(1)} copy-done((bf16[512,512]{1,0:T(8,128)(2,1)S(1)}, bf16[512,512]{1,0:T(8,128)(2,1)}, u32[]{:S(2)}) %copy-start) | copy-done | bytes 524312
  9.6 1.5 %pack.1 = (bf16[512,512]{1,0:T(8,128)(2,1)S(1)}, bf16[144,512]{1,0:T(8,128)(2,1)S(1)}, bf16[16,512]{1,0:T(8,128)(2,1)S(1)}) custom-call(bf16[512,512]{1,0:T(8,128)(2,1)S(1)} %copy-done, s32[4,4]{1,0:T(4,128)S(1)} %copy-done.1, f32[1,512]{1,0:T(1,128)S(1)} %bitcast.6, f32[1,512]{1,0:T(1,128)S(1)} %bitcast.7, f32[1,512]{1,0:T(1,128)S(1)} %copy-done.4, ...), custom_call_target="tpu_custom_call" | custom-call | tf_op jit(solution)/shard_map/pack/pallas_call | solution.py:269
  11.1 0.6 %collective-permute-done.1 = bf16[64,512]{1,0:T(8,128)(2,1)S(1)} collective-permute-done((bf16[64,512]{1,0:T(8,128)(2,1)S(1)}, bf16[64,512]{1,0:T(8,128)(2,1)S(1)}, u32[]{:S(2)}, u32[]{:S(2)}) %collective-permute-start.1) | collective-permute-done | bytes 65568 | tf_op jit(solution)/shard_map/ppermute | solution.py:215
  11.8 0.0 collective-permute-done
  11.8 1.6 %collective-permute-start.2 = (bf16[208,512]{1,0:T(8,128)(2,1)S(1)}, bf16[208,512]{1,0:T(8,128)(2,1)S(1)}, u32[]{:S(2)}, u32[]{:S(2)}) collective-permute-start(bf16[208,512]{1,0:T(8,128)(2,1)S(1)} %pad_maximum_fusion.2.refs_0_), channel_id=1, source_target_pairs={{0,8},{1,9},{2,10},{3,11},{4,12},{5,13},{6,14},{7,15},{8,0},{9,1},... | collective-permute-start | bytes 638984 | tf_op jit(solution)/shard_map/ppermute | solution.py:215
  13.4 1.5 %collective-permute-start.3 = (bf16[208,512]{1,0:T(8,128)(2,1)S(1)}, bf16[208,512]{1,0:T(8,128)(2,1)S(1)}, u32[]{:S(2)}, u32[]{:S(2)}) collective-permute-start(bf16[208,512]{1,0:T(8,128)(2,1)S(1)} %pad_maximum_fusion.2.refs_0_), channel_id=1, source_target_pairs={{0,16},{1,17},{2,18},{3,19},{4,20},{5,21},{6,22},{7,23},{8,24},{9,... | collective-permute-start | bytes 638984 | tf_op jit(solution)/shard_map/ppermute | solution.py:215
  14.9 0.6 %collective-permute-start.4 = (bf16[144,512]{1,0:T(8,128)(2,1)S(1)}, bf16[144,512]{1,0:T(8,128)(2,1)S(1)}, u32[]{:S(2)}, u32[]{:S(2)}) collective-permute-start(bf16[144,512]{1,0:T(8,128)(2,1)S(1)} %get-tuple-element.19), channel_id=1, source_target_pairs={{0,1},{1,0},{2,3},{3,2},{4,6},{5,7},{6,4},{7,5},{8,9},{9,8},{10,11... | collective-permute-start | bytes 442376 | tf_op jit(solution)/shard_map/ppermute | solution.py:215
  15.5 0.5 %collective-permute-start.5 = (bf16[80,512]{1,0:T(8,128)(2,1)S(1)}, bf16[80,512]{1,0:T(8,128)(2,1)S(1)}, u32[]{:S(2)}, u32[]{:S(2)}) collective-permute-start(bf16[80,512]{1,0:T(8,128)(2,1)S(1)} %pad_maximum_fusion.3), channel_id=1, source_target_pairs={{0,24},{1,25},{2,26},{3,27},{4,28},{5,29},{6,30},{7,31},{8,16},{9,... | collective-permute-start | bytes 245768 | tf_op jit(solution)/shard_map/ppermute | solution.py:215
  16.0 3.2 %collective-permute-start.6 = (bf16[16,512]{1,0:T(8,128)(2,1)S(1)}, bf16[16,512]{1,0:T(8,128)(2,1)S(1)}, u32[]{:S(2)}, u32[]{:S(2)}) collective-permute-start(bf16[16,512]{1,0:T(8,128)(2,1)S(1)} %get-tuple-element.16), channel_id=1, source_target_pairs={{0,3},{1,2},{2,1},{3,0},{4,7},{5,6},{6,5},{7,4},{8,11},{9,10},{10,... | collective-permute-start | bytes 49160 | tf_op jit(solution)/shard_map/ppermute | solution.py:215
  19.2 3.0 %collective-permute-done.6.refs_5_ = bf16[16,512]{1,0:T(8,128)(2,1)S(1)} collective-permute-done((bf16[16,512]{1,0:T(8,128)(2,1)S(1)}, bf16[16,512]{1,0:T(8,128)(2,1)S(1)}, u32[]{:S(2)}, u32[]{:S(2)}) %collective-permute-start.6) | collective-permute-done | bytes 16416 | tf_op jit(solution)/shard_map/ppermute | solution.py:215
  22.2 0.0 collective-permute-done.5.refs_4_
  22.2 0.0 collective-permute-done.4.refs_3_
  22.2 0.1 collective-permute-start.7
  22.3 0.0 collective-permute-done.2.refs_1_
  22.3 0.0 collective-permute-done.3.refs_2_
  22.4 0.5 %collective-permute-start.8 = (bf16[416,512]{1,0:T(8,128)(2,1)S(1)}, bf16[416,512]{1,0:T(8,128)(2,1)S(1)}, u32[]{:S(2)}, u32[]{:S(2)}) collective-permute-start(bf16[416,512]{1,0:T(8,128)(2,1)S(1)} %pad_maximum_fusion.1), channel_id=1, source_target_pairs={{0,4},{1,5},{2,6},{3,7},{4,0},{5,1},{6,2},{7,3},{8,12},{9,13},{10,... | collective-permute-start | bytes 1277960 | tf_op jit(solution)/shard_map/ppermute | solution.py:215
  22.9 1.2 %collective-permute-done.7.refs_6_ = bf16[448,512]{1,0:T(8,128)(2,1)S(1)} collective-permute-done((bf16[448,512]{1,0:T(8,128)(2,1)S(1)}, bf16[448,512]{1,0:T(8,128)(2,1)S(1)}, u32[]{:S(2)}, u32[]{:S(2)}) %collective-permute-start.7) | collective-permute-done | bytes 458784 | tf_op jit(solution)/shard_map/ppermute | solution.py:215
  24.1 0.6 %collective-permute-done.8.refs_7_ = bf16[416,512]{1,0:T(8,128)(2,1)S(1)} collective-permute-done((bf16[416,512]{1,0:T(8,128)(2,1)S(1)}, bf16[416,512]{1,0:T(8,128)(2,1)S(1)}, u32[]{:S(2)}, u32[]{:S(2)}) %collective-permute-start.8) | collective-permute-done | bytes 426016 | tf_op jit(solution)/shard_map/ppermute | solution.py:215
  24.7 7.0 %whole.1 = (f32[1,512]{1,0:T(1,128)}, f32[1,128]{1,0:T(1,128)}, f32[1,128]{1,0:T(1,128)}, f32[1,128]{1,0:T(1,128)}, f32[2]{0:T(128)}) custom-call(bf16[512,512]{1,0:T(8,128)(2,1)S(1)} %get-tuple-element.15.near, bf16[208,512]{1,0:T(8,128)(2,1)S(1)} %pad_maximum_fusion.2.refs_0_, bf16[208,512]{1,0:T(8,128)(2,1)S(1)} %collective-permute-done.2.refs_1_, ...), custom_call_target="tpu_custom_call" | custom-call | flops 268435456 | bytes 2097152 | tf_op jit(solution)/shard_map/whole/pallas_call | solution.py:282
  (5 shorter events, 0.1 us)
Async XLA Ops:
  1.6 10.2 %collective-permute-start = (bf16[128,512]{1,0:T(8,128)(2,1)S(1)}, bf16[128,512]{1,0:T(8,128)(2,1)S(1)}, u32[]{:S(2)}, u32[]{:S(2)}) collective-permute-start(bf16[128,512]{1,0:T(8,128)(2,1)S(1)} %constant_dynamic-slice_fusion.1), channel_id=1, source_target_pairs={{0,1},{1,0},{2,3},{3,2},{4,6},{5,7},{6,4},{7,5},{8,9},{9,8},{10,11... | collective-permute-start | bytes 393224 | tf_op jit(solution)/shard_map/ppermute | solution.py:215
  4.6 3.2 %copy-start.3 = (f32[512]{0:T(512)S(1)}, f32[512]{0:T(512)}, u32[]{:S(2)}) copy-start(f32[512]{0:T(512)} %param.10) | copy-start | bytes 6148
  4.6 3.3 %copy-start.4 = (f32[1,512]{1,0:T(1,128)S(1)}, f32[1,512]{1,0:T(1,128)}, u32[]{:S(2)}) copy-start(f32[1,512]{1,0:T(1,128)} %demand.1) | copy-start | bytes 6148
  4.7 7.1 %collective-permute-start.1 = (bf16[64,512]{1,0:T(8,128)(2,1)S(1)}, bf16[64,512]{1,0:T(8,128)(2,1)S(1)}, u32[]{:S(2)}, u32[]{:S(2)}) collective-permute-start(bf16[64,512]{1,0:T(8,128)(2,1)S(1)} %constant_dynamic-slice_fusion), channel_id=1, source_target_pairs={{0,3},{1,2},{2,1},{3,0},{4,7},{5,6},{6,5},{7,4},{8,11},{9,10},{10,... | collective-permute-start | bytes 196616 | tf_op jit(solution)/shard_map/ppermute | solution.py:215
  7.9 0.7 %copy-start.2 = (f32[512]{0:T(512)S(1)}, f32[512]{0:T(512)}, u32[]{:S(2)}) copy-start(f32[512]{0:T(512)} %param.9) | copy-start | bytes 6148
  7.9 0.7 %copy-start.1 = (s32[4,4]{1,0:T(4,128)S(1)}, s32[4,4]{1,0:T(4,128)}, u32[]{:S(2)}) copy-start(s32[4,4]{1,0:T(4,128)} %incidence.1) | copy-start | bytes 196
  7.9 0.7 %copy-start.5 = (s32[128]{0:T(128)S(1)}, s32[128]{0:T(128)}, u32[]{:S(2)}) copy-start(s32[128]{0:T(128)} %param.13) | copy-start | bytes 1540
  8.6 1.0 %copy-start = (bf16[512,512]{1,0:T(8,128)(2,1)S(1)}, bf16[512,512]{1,0:T(8,128)(2,1)}, u32[]{:S(2)}) copy-start(bf16[512,512]{1,0:T(8,128)(2,1)} %coupling.1) | copy-start | bytes 1572868
  11.8 10.5 %collective-permute-start.2 = (bf16[208,512]{1,0:T(8,128)(2,1)S(1)}, bf16[208,512]{1,0:T(8,128)(2,1)S(1)}, u32[]{:S(2)}, u32[]{:S(2)}) collective-permute-start(bf16[208,512]{1,0:T(8,128)(2,1)S(1)} %pad_maximum_fusion.2.refs_0_), channel_id=1, source_target_pairs={{0,8},{1,9},{2,10},{3,11},{4,12},{5,13},{6,14},{7,15},{8,0},{9,1},... | collective-permute-start | bytes 638984 | tf_op jit(solution)/shard_map/ppermute | solution.py:215
  13.4 9.0 %collective-permute-start.3 = (bf16[208,512]{1,0:T(8,128)(2,1)S(1)}, bf16[208,512]{1,0:T(8,128)(2,1)S(1)}, u32[]{:S(2)}, u32[]{:S(2)}) collective-permute-start(bf16[208,512]{1,0:T(8,128)(2,1)S(1)} %pad_maximum_fusion.2.refs_0_), channel_id=1, source_target_pairs={{0,16},{1,17},{2,18},{3,19},{4,20},{5,21},{6,22},{7,23},{8,24},{9,... | collective-permute-start | bytes 638984 | tf_op jit(solution)/shard_map/ppermute | solution.py:215
  14.9 7.3 %collective-permute-start.4 = (bf16[144,512]{1,0:T(8,128)(2,1)S(1)}, bf16[144,512]{1,0:T(8,128)(2,1)S(1)}, u32[]{:S(2)}, u32[]{:S(2)}) collective-permute-start(bf16[144,512]{1,0:T(8,128)(2,1)S(1)} %get-tuple-element.19), channel_id=1, source_target_pairs={{0,1},{1,0},{2,3},{3,2},{4,6},{5,7},{6,4},{7,5},{8,9},{9,8},{10,11... | collective-permute-start | bytes 442376 | tf_op jit(solution)/shard_map/ppermute | solution.py:215
  15.5 6.7 %collective-permute-start.5 = (bf16[80,512]{1,0:T(8,128)(2,1)S(1)}, bf16[80,512]{1,0:T(8,128)(2,1)S(1)}, u32[]{:S(2)}, u32[]{:S(2)}) collective-permute-start(bf16[80,512]{1,0:T(8,128)(2,1)S(1)} %pad_maximum_fusion.3), channel_id=1, source_target_pairs={{0,24},{1,25},{2,26},{3,27},{4,28},{5,29},{6,30},{7,31},{8,16},{9,... | collective-permute-start | bytes 245768 | tf_op jit(solution)/shard_map/ppermute | solution.py:215
  16.0 6.2 %collective-permute-start.6 = (bf16[16,512]{1,0:T(8,128)(2,1)S(1)}, bf16[16,512]{1,0:T(8,128)(2,1)S(1)}, u32[]{:S(2)}, u32[]{:S(2)}) collective-permute-start(bf16[16,512]{1,0:T(8,128)(2,1)S(1)} %get-tuple-element.16), channel_id=1, source_target_pairs={{0,3},{1,2},{2,1},{3,0},{4,7},{5,6},{6,5},{7,4},{8,11},{9,10},{10,... | collective-permute-start | bytes 49160 | tf_op jit(solution)/shard_map/ppermute | solution.py:215
  22.2 1.9 %collective-permute-start.7 = (bf16[448,512]{1,0:T(8,128)(2,1)S(1)}, bf16[448,512]{1,0:T(8,128)(2,1)S(1)}, u32[]{:S(2)}, u32[]{:S(2)}) collective-permute-start(bf16[448,512]{1,0:T(8,128)(2,1)S(1)} %pad_maximum_fusion), channel_id=1, source_target_pairs={{0,4},{1,5},{2,6},{3,7},{4,0},{5,1},{6,2},{7,3},{8,12},{9,13},{10,... | collective-permute-start | bytes 1376264 | tf_op jit(solution)/shard_map/ppermute | solution.py:215
  22.4 2.4 %collective-permute-start.8 = (bf16[416,512]{1,0:T(8,128)(2,1)S(1)}, bf16[416,512]{1,0:T(8,128)(2,1)S(1)}, u32[]{:S(2)}, u32[]{:S(2)}) collective-permute-start(bf16[416,512]{1,0:T(8,128)(2,1)S(1)} %pad_maximum_fusion.1), channel_id=1, source_target_pairs={{0,4},{1,5},{2,6},{3,7},{4,0},{5,1},{6,2},{7,3},{8,12},{9,13},{10,... | collective-permute-start | bytes 1277960 | tf_op jit(solution)/shard_map/ppermute | solution.py:215

commit v7 on v6

--- a/solution.py
+++ b/solution.py
@@ -147,7 +147,19 @@
     mult_out[...], cons_out[...] = pick_fleet(own_row(prices[:, own], scen), centre[:, own], slots[...])
 
 
-def whole_kernel(near, *refs):
+def ready_kernel(near, line, side, front, across, near_turned, mine, mine_turned):
+    total_rows, block_arcs = near.shape
+    chips = total_rows // TILE
+    near_turned[...] = near[...].T
+    touch = across[TILE:, :].astype(jnp.float32)[11:11 + chips].astype(jnp.bfloat16)
+    for part, source in enumerate((line, side, front, across)):
+        rows = slice(part * TILE, (part + 1) * TILE)
+        wide = source[:TILE, :]
+        mine[rows, :] = wide if part == chips - 1 else wide * touch[part:part + 1]
+    mine_turned[...] = mine[...].T
+
+
+def whole_kernel(near, near_turned, mine, mine_turned, *refs):
     lines, others = refs[:6], [None] * 6
     for group, joined in zip(GROUPS, refs[6:]):
         first = 0
@@ -181,23 +193,23 @@
         owner = jnp.bitwise_xor(chip, part)
         rows = slice(part * TILE, (part + 1) * TILE)
         demand[:, rows] = demand_in[:, pl.ds(pl.multiple_of(owner * TILE, TILE), TILE)]
+        wide = others[part][:TILE, :]
+        blocks_in[0, rows, :] = wide if part == chips - 1 else wide * touch[2][part:part + 1]
         for side, source in enumerate((lines, others)):
+            narrow = source[part][TILE:TILE + half, :] if part < chips - 1 else source[4][:half, :]
             place = jnp.where(core == side, 0, half)
             place = pl.ds(pl.multiple_of(part * TILE + place, half), half)
-            on = touch[3][part:part + 1]
-            if part < chips - 1:
-                blocks_in[side, rows, :] = source[part][:TILE, :] * touch[1 + side][part:part + 1]
-                blocks_in[2, place, :] = source[part][TILE:TILE + half, :] * on
-            else:
-                blocks_in[side, rows, :] = source[3][:TILE, :]
-                blocks_in[2, place, :] = source[4][:half, :] * on
+            blocks_in[1, place, :] = narrow * touch[3][part:part + 1]
+    for block in range(2):
+        turned[block] = blocks_in[block].T
 
     def masked(block):
-        return near[...] if block == 0 else blocks_in[block - 1]
-
-    for block in range(len(tails)):
-        turned[block] = masked(block).T
-    rounds(masked, lambda block: turned[block], len(tails), cost, cap, mask, demand, share, slots.shape[1] * len(tails),
+        return (near, mine)[block][...] if block < 2 else blocks_in[block - 2]
+
+    def masked_turned(block):
+        return (near_turned, mine_turned)[block][...] if block < 2 else turned[block - 2]
+
+    rounds(masked, masked_turned, len(tails), cost, cap, mask, demand, share, slots.shape[1] * len(tails),
            spread_out, flows, duals, prices, centre, shifted)
     flows_out[...] = flows[0:1, :block_arcs]
     first = pl.multiple_of(jnp.bitwise_xor(chip, arc) * TILE, TILE)
@@ -279,14 +291,23 @@
             name="pack",
         )(coupling, incidence, row(arc_cost), row(capacity), demand, weights.reshape(1, 1), slots)
         brought = bring(coupling, across, extra)
+        square = jax.ShapeDtypeStruct((block_arcs, total_rows), jnp.bfloat16)
+        ready = pl.pallas_call(
+            ready_kernel,
+            out_shape=(square, like(total_rows), square),
+            in_specs=[VMEM] * 5,
+            out_specs=(VMEM,) * 3,
+            compiler_params=limit(8),
+            name="ready",
+        )(near, *brought[:4])
         outs = pl.pallas_call(
             whole_kernel,
             out_shape=out_shape,
-            in_specs=[VMEM] * (len(brought) + 2),
+            in_specs=[VMEM] * (len(brought) + 5),
             out_specs=out_specs,
             scratch_shapes=[
-                pltpu.VMEM((blocks - 1, total_rows, block_arcs), jnp.bfloat16),
-                pltpu.VMEM((blocks, block_arcs, total_rows), jnp.bfloat16),
+                pltpu.VMEM((blocks - 2, total_rows, block_arcs), jnp.bfloat16),
+                pltpu.VMEM((blocks - 2, block_arcs, total_rows), jnp.bfloat16),
                 pltpu.VMEM((1, arcs), jnp.float32),
                 pltpu.VMEM((1, arcs), jnp.float32),
                 pltpu.VMEM((1, arcs), jnp.float32),
@@ -298,7 +319,7 @@
             compiler_params=limit(16),
             cost_estimate=cost,
             name="whole",
-        )(near, *brought, slots)
+        )(near, *ready, *brought, slots)
     else:
         masked = (
             coupling.reshape(total_rows // TILE, TILE, block_arcs // TILE, TILE)

time: 31.9 us -> 31.7 us (level)
  waiting for transfers between devices: 5.45 us -> 5.13 us
    ppermute x9, waiting for transfers between devices: 5.45 us -> 5.13 us  [swap(): return lax.ppermute(value, ('scen', 'arc'), pairs)]
    pallas_call x0 -> x1, Pallas kernels: none -> 0.32 us  [body(): pl.pallas_call(ready_kernel, out_shape=(square, like(total_rows), square)...]
  transfers between devices with their start and end apart: 9 -> 9, of which waited for: 4 -> 4; matrix products, arithmetic and copies ran while one was open for 0% -> 0% of each run, Pallas kernels for 5% -> 6%
where the time goes in v7:
time: 31.7 us; the launch traced here: 31.5 us
  starting transfers between devices  13.6 us (43%)
  Pallas kernels  8.59 us (27%)
  waiting for transfers between devices  5.13 us (16%)
  local copies, waits for them, and re-layouts  2.63 us (8%)
  between operations  1.4 us (4%)
    ppermute x9, starting transfers between devices, swap(): return lax.ppermute(value, ('scen', 'arc'), pairs)  13.6 us
    pallas_call x1, Pallas kernels, body(): pl.pallas_call(whole_kernel, out_shape=out_shape, in_specs=[VMEM] * (len(...  6.75 us
    ppermute x9, waiting for transfers between devices, swap(): return lax.ppermute(value, ('scen', 'arc'), pairs)  5.13 us
    unnamed x12, local copies, waits for them, and re-layouts  1.71 us
    pallas_call x1, Pallas kernels, body(): pl.pallas_call(pack_kernel, out_shape=(like(total_rows), like(TILE + EXTR...  1.52 us
    dynamic_slice x1, local copies, waits for them, and re-layouts, bring(): lax.dynamic_slice_in_dim(coupling, lax.shift_right_logical(scen, 1) * TIL...  0.92 us
  transfers between devices with their start and end apart: 9, of which 4 were waited for; matrix products, arithmetic and copies ran while one was open for 0% of the time, Pallas kernels for 6%

profile of v7, /device:TPU:0, one launch (start us, length us, event | category | flops | bytes accessed | tf_op | source)
XLA Modules:
  0.0 31.5 jit_solution(5048773722787859018)
XLA Ops:
  0.6 0.9 %constant_dynamic-slice_fusion.1 = bf16[128,512]{1,0:T(8,128)(2,1)S(1)} fusion(bf16[512,512]{1,0:T(8,128)(2,1)} %coupling.1, s32[]{:T(128)S(6)} %select_n.6), kind=kLoop, calls=%fused_computation.5 | loop fusion | bytes 262148 | tf_op jit(solution)/shard_map/dynamic_slice | solution.py:233
  1.6 3.1 %collective-permute-start = (bf16[128,512]{1,0:T(8,128)(2,1)S(1)}, bf16[128,512]{1,0:T(8,128)(2,1)S(1)}, u32[]{:S(2)}, u32[]{:S(2)}) collective-permute-start(bf16[128,512]{1,0:T(8,128)(2,1)S(1)} %constant_dynamic-slice_fusion.1), channel_id=1, source_target_pairs={{0,1},{1,0},{2,3},{3,2},{4,6},{5,7},{6,4},{7,5},{8,9},{9,8},{10,11... | collective-permute-start | bytes 393224 | tf_op jit(solution)/shard_map/ppermute | solution.py:227
  4.6 0.0 copy-start.3
  4.6 0.0 copy-start.4
  4.7 2.5 %collective-permute-start.1 = (bf16[64,512]{1,0:T(8,128)(2,1)S(1)}, bf16[64,512]{1,0:T(8,128)(2,1)S(1)}, u32[]{:S(2)}, u32[]{:S(2)}) collective-permute-start(bf16[64,512]{1,0:T(8,128)(2,1)S(1)} %constant_dynamic-slice_fusion), channel_id=1, source_target_pairs={{0,3},{1,2},{2,1},{3,0},{4,7},{5,6},{6,5},{7,4},{8,11},{9,10},{10,... | collective-permute-start | bytes 196616 | tf_op jit(solution)/shard_map/ppermute | solution.py:227
  7.9 0.0 copy-start.2
  7.9 0.0 copy-start.1
  7.9 0.0 copy-start.5
  7.9 0.0 copy-done.3
  7.9 0.0 copy-done.4
  7.9 0.6 %copy-done.2 = f32[512]{0:T(512)S(1)} copy-done((f32[512]{0:T(512)S(1)}, f32[512]{0:T(512)}, u32[]{:S(2)}) %copy-start.2) | copy-done | bytes 2072
  8.5 0.0 copy-done.1
  8.6 0.0 copy-done.5
  8.6 0.0 copy-start
  8.6 1.0 %copy-done = bf16[512,512]{1,0:T(8,128)(2,1)S(1)} copy-done((bf16[512,512]{1,0:T(8,128)(2,1)S(1)}, bf16[512,512]{1,0:T(8,128)(2,1)}, u32[]{:S(2)}) %copy-start) | copy-done | bytes 524312
  9.6 1.5 %pack.1 = (bf16[512,512]{1,0:T(8,128)(2,1)S(1)}, bf16[144,512]{1,0:T(8,128)(2,1)S(1)}, bf16[16,512]{1,0:T(8,128)(2,1)S(1)}) custom-call(bf16[512,512]{1,0:T(8,128)(2,1)S(1)} %copy-done, s32[4,4]{1,0:T(4,128)S(1)} %copy-done.1, f32[1,512]{1,0:T(1,128)S(1)} %bitcast.6, f32[1,512]{1,0:T(1,128)S(1)} %bitcast.7, f32[1,512]{1,0:T(1,128)S(1)} %copy-done.4, ...), custom_call_target="tpu_custom_call" | custom-call | tf_op jit(solution)/shard_map/pack/pallas_call | solution.py:281
  11.1 0.6 %collective-permute-done.1 = bf16[64,512]{1,0:T(8,128)(2,1)S(1)} collective-permute-done((bf16[64,512]{1,0:T(8,128)(2,1)S(1)}, bf16[64,512]{1,0:T(8,128)(2,1)S(1)}, u32[]{:S(2)}, u32[]{:S(2)}) %collective-permute-start.1) | collective-permute-done | bytes 65568 | tf_op jit(solution)/shard_map/ppermute | solution.py:227
  11.8 0.0 collective-permute-done
  11.8 1.6 %collective-permute-start.3 = (bf16[208,512]{1,0:T(8,128)(2,1)S(1)}, bf16[208,512]{1,0:T(8,128)(2,1)S(1)}, u32[]{:S(2)}, u32[]{:S(2)}) collective-permute-start(bf16[208,512]{1,0:T(8,128)(2,1)S(1)} %pad_maximum_fusion.2.line.refs_0_), channel_id=1, source_target_pairs={{0,16},{1,17},{2,18},{3,19},{4,20},{5,21},{6,22},{7,23},{8,24},{9,... | collective-permute-start | bytes 638984 | tf_op jit(solution)/shard_map/ppermute | solution.py:227
  13.4 1.5 %collective-permute-start.2 = (bf16[208,512]{1,0:T(8,128)(2,1)S(1)}, bf16[208,512]{1,0:T(8,128)(2,1)S(1)}, u32[]{:S(2)}, u32[]{:S(2)}) collective-permute-start(bf16[208,512]{1,0:T(8,128)(2,1)S(1)} %pad_maximum_fusion.2.line.refs_0_), channel_id=1, source_target_pairs={{0,8},{1,9},{2,10},{3,11},{4,12},{5,13},{6,14},{7,15},{8,0},{9,1},... | collective-permute-start | bytes 638984 | tf_op jit(solution)/shard_map/ppermute | solution.py:227
  14.9 0.6 %collective-permute-start.4 = (bf16[144,512]{1,0:T(8,128)(2,1)S(1)}, bf16[144,512]{1,0:T(8,128)(2,1)S(1)}, u32[]{:S(2)}, u32[]{:S(2)}) collective-permute-start(bf16[144,512]{1,0:T(8,128)(2,1)S(1)} %get-tuple-element.22), channel_id=1, source_target_pairs={{0,1},{1,0},{2,3},{3,2},{4,6},{5,7},{6,4},{7,5},{8,9},{9,8},{10,11... | collective-permute-start | bytes 442376 | tf_op jit(solution)/shard_map/ppermute | solution.py:227
  15.5 0.5 %collective-permute-start.5 = (bf16[80,512]{1,0:T(8,128)(2,1)S(1)}, bf16[80,512]{1,0:T(8,128)(2,1)S(1)}, u32[]{:S(2)}, u32[]{:S(2)}) collective-permute-start(bf16[80,512]{1,0:T(8,128)(2,1)S(1)} %pad_maximum_fusion.3), channel_id=1, source_target_pairs={{0,24},{1,25},{2,26},{3,27},{4,28},{5,29},{6,30},{7,31},{8,16},{9,... | collective-permute-start | bytes 245768 | tf_op jit(solution)/shard_map/ppermute | solution.py:227
  16.0 3.2 %collective-permute-start.6 = (bf16[16,512]{1,0:T(8,128)(2,1)S(1)}, bf16[16,512]{1,0:T(8,128)(2,1)S(1)}, u32[]{:S(2)}, u32[]{:S(2)}) collective-permute-start(bf16[16,512]{1,0:T(8,128)(2,1)S(1)} %get-tuple-element.19), channel_id=1, source_target_pairs={{0,3},{1,2},{2,1},{3,0},{4,7},{5,6},{6,5},{7,4},{8,11},{9,10},{10,... | collective-permute-start | bytes 49160 | tf_op jit(solution)/shard_map/ppermute | solution.py:227
  19.2 3.0 %collective-permute-done.6.refs_5_ = bf16[16,512]{1,0:T(8,128)(2,1)S(1)} collective-permute-done((bf16[16,512]{1,0:T(8,128)(2,1)S(1)}, bf16[16,512]{1,0:T(8,128)(2,1)S(1)}, u32[]{:S(2)}, u32[]{:S(2)}) %collective-permute-start.6) | collective-permute-done | bytes 16416 | tf_op jit(solution)/shard_map/ppermute | solution.py:227
  22.2 0.0 collective-permute-done.5.refs_4_
  22.2 0.0 collective-permute-done.4.across.refs_3_
  22.2 0.1 collective-permute-start.7
  22.3 0.0 collective-permute-done.3.front.refs_2_
  22.3 0.0 collective-permute-done.2.side.refs_1_
  22.4 0.5 %collective-permute-start.8 = (bf16[416,512]{1,0:T(8,128)(2,1)S(1)}, bf16[416,512]{1,0:T(8,128)(2,1)S(1)}, u32[]{:S(2)}, u32[]{:S(2)}) collective-permute-start(bf16[416,512]{1,0:T(8,128)(2,1)S(1)} %pad_maximum_fusion.1), channel_id=1, source_target_pairs={{0,4},{1,5},{2,6},{3,7},{4,0},{5,1},{6,2},{7,3},{8,12},{9,13},{10,... | collective-permute-start | bytes 1277960 | tf_op jit(solution)/shard_map/ppermute | solution.py:227
  22.9 0.3 %ready.1 = (bf16[512,512]{1,0:T(8,128)(2,1)S(1)}, bf16[512,512]{1,0:T(8,128)(2,1)S(1)}, bf16[512,512]{1,0:T(8,128)(2,1)S(1)}) custom-call(bf16[512,512]{1,0:T(8,128)(2,1)S(1)} %get-tuple-element.18.near, bf16[208,512]{1,0:T(8,128)(2,1)S(1)} %pad_maximum_fusion.2.line.refs_0_, bf16[208,512]{1,0:T(8,128)(2,1)S(1)} %collective-permute-done.2.side.refs_1_, ...), custom_call_target="tpu_custom_call" | custom-call | tf_op jit(solution)/shard_map/ready/pallas_call | solution.py:295
  23.2 0.9 %collective-permute-done.7.refs_6_ = bf16[448,512]{1,0:T(8,128)(2,1)S(1)} collective-permute-done((bf16[448,512]{1,0:T(8,128)(2,1)S(1)}, bf16[448,512]{1,0:T(8,128)(2,1)S(1)}, u32[]{:S(2)}, u32[]{:S(2)}) %collective-permute-start.7) | collective-permute-done | bytes 458784 | tf_op jit(solution)/shard_map/ppermute | solution.py:227
  24.1 0.6 %collective-permute-done.8.refs_7_ = bf16[416,512]{1,0:T(8,128)(2,1)S(1)} collective-permute-done((bf16[416,512]{1,0:T(8,128)(2,1)S(1)}, bf16[416,512]{1,0:T(8,128)(2,1)S(1)}, u32[]{:S(2)}, u32[]{:S(2)}) %collective-permute-start.8) | collective-permute-done | bytes 426016 | tf_op jit(solution)/shard_map/ppermute | solution.py:227
  24.7 6.8 %whole.1 = (f32[1,512]{1,0:T(1,128)}, f32[1,128]{1,0:T(1,128)}, f32[1,128]{1,0:T(1,128)}, f32[1,128]{1,0:T(1,128)}, f32[2]{0:T(128)}) custom-call(bf16[512,512]{1,0:T(8,128)(2,1)S(1)} %get-tuple-element.18.near, bf16[512,512]{1,0:T(8,128)(2,1)S(1)} %get-tuple-element.23.near_turned, bf16[512,512]{1,0:T(8,128)(2,1)S(1)} %get-tuple-element.24.mine, ...), custom_call_target="tpu_custom_call" | custom-call | flops 268435456 | bytes 2097152 | tf_op jit(solution)/shard_map/whole/pallas_call | solution.py:303
  (5 shorter events, 0.1 us)
Async XLA Ops:
  1.6 10.2 %collective-permute-start = (bf16[128,512]{1,0:T(8,128)(2,1)S(1)}, bf16[128,512]{1,0:T(8,128)(2,1)S(1)}, u32[]{:S(2)}, u32[]{:S(2)}) collective-permute-start(bf16[128,512]{1,0:T(8,128)(2,1)S(1)} %constant_dynamic-slice_fusion.1), channel_id=1, source_target_pairs={{0,1},{1,0},{2,3},{3,2},{4,6},{5,7},{6,4},{7,5},{8,9},{9,8},{10,11... | collective-permute-start | bytes 393224 | tf_op jit(solution)/shard_map/ppermute | solution.py:227
  4.6 3.2 %copy-start.3 = (f32[512]{0:T(512)S(1)}, f32[512]{0:T(512)}, u32[]{:S(2)}) copy-start(f32[512]{0:T(512)} %param.10) | copy-start | bytes 6148
  4.6 3.3 %copy-start.4 = (f32[1,512]{1,0:T(1,128)S(1)}, f32[1,512]{1,0:T(1,128)}, u32[]{:S(2)}) copy-start(f32[1,512]{1,0:T(1,128)} %demand.1) | copy-start | bytes 6148
  4.7 7.1 %collective-permute-start.1 = (bf16[64,512]{1,0:T(8,128)(2,1)S(1)}, bf16[64,512]{1,0:T(8,128)(2,1)S(1)}, u32[]{:S(2)}, u32[]{:S(2)}) collective-permute-start(bf16[64,512]{1,0:T(8,128)(2,1)S(1)} %constant_dynamic-slice_fusion), channel_id=1, source_target_pairs={{0,3},{1,2},{2,1},{3,0},{4,7},{5,6},{6,5},{7,4},{8,11},{9,10},{10,... | collective-permute-start | bytes 196616 | tf_op jit(solution)/shard_map/ppermute | solution.py:227
  7.9 0.7 %copy-start.2 = (f32[512]{0:T(512)S(1)}, f32[512]{0:T(512)}, u32[]{:S(2)}) copy-start(f32[512]{0:T(512)} %param.9) | copy-start | bytes 6148
  7.9 0.7 %copy-start.1 = (s32[4,4]{1,0:T(4,128)S(1)}, s32[4,4]{1,0:T(4,128)}, u32[]{:S(2)}) copy-start(s32[4,4]{1,0:T(4,128)} %incidence.1) | copy-start | bytes 196
  7.9 0.7 %copy-start.5 = (s32[128]{0:T(128)S(1)}, s32[128]{0:T(128)}, u32[]{:S(2)}) copy-start(s32[128]{0:T(128)} %param.13) | copy-start | bytes 1540
  8.6 1.0 %copy-start = (bf16[512,512]{1,0:T(8,128)(2,1)S(1)}, bf16[512,512]{1,0:T(8,128)(2,1)}, u32[]{:S(2)}) copy-start(bf16[512,512]{1,0:T(8,128)(2,1)} %coupling.1) | copy-start | bytes 1572868
  11.8 10.5 %collective-permute-start.3 = (bf16[208,512]{1,0:T(8,128)(2,1)S(1)}, bf16[208,512]{1,0:T(8,128)(2,1)S(1)}, u32[]{:S(2)}, u32[]{:S(2)}) collective-permute-start(bf16[208,512]{1,0:T(8,128)(2,1)S(1)} %pad_maximum_fusion.2.line.refs_0_), channel_id=1, source_target_pairs={{0,16},{1,17},{2,18},{3,19},{4,20},{5,21},{6,22},{7,23},{8,24},{9,... | collective-permute-start | bytes 638984 | tf_op jit(solution)/shard_map/ppermute | solution.py:227
  13.4 8.9 %collective-permute-start.2 = (bf16[208,512]{1,0:T(8,128)(2,1)S(1)}, bf16[208,512]{1,0:T(8,128)(2,1)S(1)}, u32[]{:S(2)}, u32[]{:S(2)}) collective-permute-start(bf16[208,512]{1,0:T(8,128)(2,1)S(1)} %pad_maximum_fusion.2.line.refs_0_), channel_id=1, source_target_pairs={{0,8},{1,9},{2,10},{3,11},{4,12},{5,13},{6,14},{7,15},{8,0},{9,1},... | collective-permute-start | bytes 638984 | tf_op jit(solution)/shard_map/ppermute | solution.py:227
  14.9 7.3 %collective-permute-start.4 = (bf16[144,512]{1,0:T(8,128)(2,1)S(1)}, bf16[144,512]{1,0:T(8,128)(2,1)S(1)}, u32[]{:S(2)}, u32[]{:S(2)}) collective-permute-start(bf16[144,512]{1,0:T(8,128)(2,1)S(1)} %get-tuple-element.22), channel_id=1, source_target_pairs={{0,1},{1,0},{2,3},{3,2},{4,6},{5,7},{6,4},{7,5},{8,9},{9,8},{10,11... | collective-permute-start | bytes 442376 | tf_op jit(solution)/shard_map/ppermute | solution.py:227
  15.5 6.7 %collective-permute-start.5 = (bf16[80,512]{1,0:T(8,128)(2,1)S(1)}, bf16[80,512]{1,0:T(8,128)(2,1)S(1)}, u32[]{:S(2)}, u32[]{:S(2)}) collective-permute-start(bf16[80,512]{1,0:T(8,128)(2,1)S(1)} %pad_maximum_fusion.3), channel_id=1, source_target_pairs={{0,24},{1,25},{2,26},{3,27},{4,28},{5,29},{6,30},{7,31},{8,16},{9,... | collective-permute-start | bytes 245768 | tf_op jit(solution)/shard_map/ppermute | solution.py:227
  16.0 6.2 %collective-permute-start.6 = (bf16[16,512]{1,0:T(8,128)(2,1)S(1)}, bf16[16,512]{1,0:T(8,128)(2,1)S(1)}, u32[]{:S(2)}, u32[]{:S(2)}) collective-permute-start(bf16[16,512]{1,0:T(8,128)(2,1)S(1)} %get-tuple-element.19), channel_id=1, source_target_pairs={{0,3},{1,2},{2,1},{3,0},{4,7},{5,6},{6,5},{7,4},{8,11},{9,10},{10,... | collective-permute-start | bytes 49160 | tf_op jit(solution)/shard_map/ppermute | solution.py:227
  22.2 1.9 %collective-permute-start.7 = (bf16[448,512]{1,0:T(8,128)(2,1)S(1)}, bf16[448,512]{1,0:T(8,128)(2,1)S(1)}, u32[]{:S(2)}, u32[]{:S(2)}) collective-permute-start(bf16[448,512]{1,0:T(8,128)(2,1)S(1)} %pad_maximum_fusion), channel_id=1, source_target_pairs={{0,4},{1,5},{2,6},{3,7},{4,0},{5,1},{6,2},{7,3},{8,12},{9,13},{10,... | collective-permute-start | bytes 1376264 | tf_op jit(solution)/shard_map/ppermute | solution.py:227
  22.4 2.4 %collective-permute-start.8 = (bf16[416,512]{1,0:T(8,128)(2,1)S(1)}, bf16[416,512]{1,0:T(8,128)(2,1)S(1)}, u32[]{:S(2)}, u32[]{:S(2)}) collective-permute-start(bf16[416,512]{1,0:T(8,128)(2,1)S(1)} %pad_maximum_fusion.1), channel_id=1, source_target_pairs={{0,4},{1,5},{2,6},{3,7},{4,0},{5,1},{6,2},{7,3},{8,12},{9,13},{10,... | collective-permute-start | bytes 1277960 | tf_op jit(solution)/shard_map/ppermute | solution.py:227

commit v8 on v7

--- a/solution.py
+++ b/solution.py
@@ -81,7 +81,7 @@
     across[:TILE, :] = near[(chips - 1) * TILE:, :]
 
 
-def rounds(masked, turned, blocks, cost, cap, mask, demand, share, fleet_count, spread_out,
+def rounds(masked, turned, blocks, joined, cost, cap, mask, demand, share, fleet_count, spread_out,
            flows, duals, prices, centre, shifted):
     scenarios, total_rows = demand.shape
     block_arcs = cost.shape[1] // blocks
@@ -92,22 +92,29 @@
             load = jnp.zeros((scenarios, total_rows), jnp.float32)
             if not first:
                 duals_low = duals[...].astype(jnp.bfloat16)
-            for block in range(blocks):
-                cols = slice(block * block_arcs, (block + 1) * block_arcs)
-                if first:
-                    gradient = jnp.broadcast_to(cost[:, cols], (scenarios, block_arcs))
-                    old = jnp.zeros((scenarios, block_arcs), jnp.float32)
-                else:
-                    old = flows[:, cols]
-                    pull = jnp.dot(duals_low, masked(block), preferred_element_type=jnp.float32)
-                    push = penalty * mask[:, cols] * old
-                    if round_index > 0:
-                        push = push + shifted[:, cols]
-                    gradient = cost[:, cols] + pull + push
-                new = jnp.clip(old - primal_step * gradient, 0.0, cap[:, cols])
-                flows[:, cols] = new
-                bar = (2.0 * new - old).astype(jnp.bfloat16)
-                load = load + jnp.dot(bar, turned(block), preferred_element_type=jnp.float32)
+            for start in range(0, blocks, joined):
+                group = range(start, start + joined)
+                if not first:
+                    weights = jnp.concatenate([masked(block) for block in group], axis=1)
+                    pulls = jnp.dot(duals_low, weights, preferred_element_type=jnp.float32)
+                bars = []
+                for block in group:
+                    cols = slice(block * block_arcs, (block + 1) * block_arcs)
+                    if first:
+                        gradient = jnp.broadcast_to(cost[:, cols], (scenarios, block_arcs))
+                        old = jnp.zeros((scenarios, block_arcs), jnp.float32)
+                    else:
+                        old = flows[:, cols]
+                        pull = pulls[:, (block - start) * block_arcs:(block - start + 1) * block_arcs]
+                        push = penalty * mask[:, cols] * old
+                        if round_index > 0:
+                            push = push + shifted[:, cols]
+                        gradient = cost[:, cols] + pull + push
+                    new = jnp.clip(old - primal_step * gradient, 0.0, cap[:, cols])
+                    flows[:, cols] = new
+                    bars.append((2.0 * new - old).astype(jnp.bfloat16))
+                weights = jnp.concatenate([turned(block) for block in group], axis=0)
+                load = load + jnp.dot(jnp.concatenate(bars, axis=1), weights, preferred_element_type=jnp.float32)
             step = dual_step * (load - demand[...])
             duals[...] = jnp.maximum(step if first else duals[...] + step, 0.0)
         squares = jnp.float32(0.0)
@@ -136,7 +143,7 @@
 def plain_kernel(masked, cost, cap, mask, demand, share, slots, flows_out, duals_out, mult_out, cons_out,
                  spread_out, flows, duals, prices, centre, shifted):
     blocks, total_rows, block_arcs = masked.shape
-    rounds(lambda block: masked[block], lambda block: masked[block].T, blocks, cost, cap, mask, demand, share, slots.shape[1] * blocks,
+    rounds(lambda block: masked[block], lambda block: masked[block].T, blocks, 1, cost, cap, mask, demand, share, slots.shape[1] * blocks,
            spread_out, flows, duals, prices, centre, shifted)
     scen, arc = lax.axis_index("scen"), lax.axis_index("arc")
     own = pl.ds(pl.multiple_of(arc * block_arcs, block_arcs), block_arcs)
@@ -209,7 +216,7 @@
     def masked_turned(block):
         return (near_turned, mine_turned)[block][...] if block < 2 else turned[block - 2]
 
-    rounds(masked, masked_turned, len(tails), cost, cap, mask, demand, share, slots.shape[1] * len(tails),
+    rounds(masked, masked_turned, len(tails), len(tails), cost, cap, mask, demand, share, slots.shape[1] * len(tails),
            spread_out, flows, duals, prices, centre, shifted)
     flows_out[...] = flows[0:1, :block_arcs]
     first = pl.multiple_of(jnp.bitwise_xor(chip, arc) * TILE, TILE)

time: 31.7 us -> 30.5 us (0.962)
  Pallas kernels: 8.59 us -> 7.41 us
    pallas_call x1, Pallas kernels: 6.75 us -> 5.57 us  [body(): pl.pallas_call(whole_kernel, out_shape=out_shape, in_specs=[VMEM] * (len(...]
where the time goes in v8:
time: 30.5 us; the launch traced here: 30.3 us
  starting transfers between devices  13.6 us (45%)
  Pallas kernels  7.41 us (24%)
  waiting for transfers between devices  5.13 us (17%)
  local copies, waits for them, and re-layouts  2.63 us (9%)
  between operations  1.4 us (5%)
    ppermute x9, starting transfers between devices, swap(): return lax.ppermute(value, ('scen', 'arc'), pairs)  13.6 us
    pallas_call x1, Pallas kernels, body(): pl.pallas_call(whole_kernel, out_shape=out_shape, in_specs=[VMEM] * (len(...  5.57 us
    ppermute x9, waiting for transfers between devices, swap(): return lax.ppermute(value, ('scen', 'arc'), pairs)  5.13 us
    unnamed x12, local copies, waits for them, and re-layouts  1.71 us
    pallas_call x1, Pallas kernels, body(): pl.pallas_call(pack_kernel, out_shape=(like(total_rows), like(TILE + EXTR...  1.52 us
    dynamic_slice x1, local copies, waits for them, and re-layouts, bring(): lax.dynamic_slice_in_dim(coupling, lax.shift_right_logical(scen, 1) * TIL...  0.92 us
  transfers between devices with their start and end apart: 9, of which 4 were waited for; matrix products, arithmetic and copies ran while one was open for 0% of the time, Pallas kernels for 6%

profile of v8, /device:TPU:0, one launch (start us, length us, event | category | flops | bytes accessed | tf_op | source)
XLA Modules:
  0.0 30.3 jit_solution(6959092522068526877)
XLA Ops:
  0.6 0.9 %constant_dynamic-slice_fusion.1 = bf16[128,512]{1,0:T(8,128)(2,1)S(1)} fusion(bf16[512,512]{1,0:T(8,128)(2,1)} %coupling.1, s32[]{:T(128)S(6)} %select_n.6), kind=kLoop, calls=%fused_computation.5 | loop fusion | bytes 262148 | tf_op jit(solution)/shard_map/dynamic_slice | solution.py:240
  1.6 3.1 %collective-permute-start = (bf16[128,512]{1,0:T(8,128)(2,1)S(1)}, bf16[128,512]{1,0:T(8,128)(2,1)S(1)}, u32[]{:S(2)}, u32[]{:S(2)}) collective-permute-start(bf16[128,512]{1,0:T(8,128)(2,1)S(1)} %constant_dynamic-slice_fusion.1), channel_id=1, source_target_pairs={{0,1},{1,0},{2,3},{3,2},{4,6},{5,7},{6,4},{7,5},{8,9},{9,8},{10,11... | collective-permute-start | bytes 393224 | tf_op jit(solution)/shard_map/ppermute | solution.py:234
  4.6 0.0 copy-start.3
  4.6 0.0 copy-start.4
  4.7 2.5 %collective-permute-start.1 = (bf16[64,512]{1,0:T(8,128)(2,1)S(1)}, bf16[64,512]{1,0:T(8,128)(2,1)S(1)}, u32[]{:S(2)}, u32[]{:S(2)}) collective-permute-start(bf16[64,512]{1,0:T(8,128)(2,1)S(1)} %constant_dynamic-slice_fusion), channel_id=1, source_target_pairs={{0,3},{1,2},{2,1},{3,0},{4,7},{5,6},{6,5},{7,4},{8,11},{9,10},{10,... | collective-permute-start | bytes 196616 | tf_op jit(solution)/shard_map/ppermute | solution.py:234
  7.9 0.0 copy-start.2
  7.9 0.0 copy-start.1
  7.9 0.0 copy-start.5
  7.9 0.0 copy-done.3
  7.9 0.0 copy-done.4
  7.9 0.6 %copy-done.2 = f32[512]{0:T(512)S(1)} copy-done((f32[512]{0:T(512)S(1)}, f32[512]{0:T(512)}, u32[]{:S(2)}) %copy-start.2) | copy-done | bytes 2072
  8.5 0.0 copy-done.1
  8.6 0.0 copy-done.5
  8.6 0.0 copy-start
  8.6 1.0 %copy-done = bf16[512,512]{1,0:T(8,128)(2,1)S(1)} copy-done((bf16[512,512]{1,0:T(8,128)(2,1)S(1)}, bf16[512,512]{1,0:T(8,128)(2,1)}, u32[]{:S(2)}) %copy-start) | copy-done | bytes 524312
  9.6 1.5 %pack.1 = (bf16[512,512]{1,0:T(8,128)(2,1)S(1)}, bf16[144,512]{1,0:T(8,128)(2,1)S(1)}, bf16[16,512]{1,0:T(8,128)(2,1)S(1)}) custom-call(bf16[512,512]{1,0:T(8,128)(2,1)S(1)} %copy-done, s32[4,4]{1,0:T(4,128)S(1)} %copy-done.1, f32[1,512]{1,0:T(1,128)S(1)} %bitcast.6, f32[1,512]{1,0:T(1,128)S(1)} %bitcast.7, f32[1,512]{1,0:T(1,128)S(1)} %copy-done.4, ...), custom_call_target="tpu_custom_call" | custom-call | tf_op jit(solution)/shard_map/pack/pallas_call | solution.py:288
  11.1 0.6 %collective-permute-done.1 = bf16[64,512]{1,0:T(8,128)(2,1)S(1)} collective-permute-done((bf16[64,512]{1,0:T(8,128)(2,1)S(1)}, bf16[64,512]{1,0:T(8,128)(2,1)S(1)}, u32[]{:S(2)}, u32[]{:S(2)}) %collective-permute-start.1) | collective-permute-done | bytes 65568 | tf_op jit(solution)/shard_map/ppermute | solution.py:234
  11.8 0.0 collective-permute-done
  11.8 1.6 %collective-permute-start.3 = (bf16[208,512]{1,0:T(8,128)(2,1)S(1)}, bf16[208,512]{1,0:T(8,128)(2,1)S(1)}, u32[]{:S(2)}, u32[]{:S(2)}) collective-permute-start(bf16[208,512]{1,0:T(8,128)(2,1)S(1)} %pad_maximum_fusion.2.line.refs_0_), channel_id=1, source_target_pairs={{0,16},{1,17},{2,18},{3,19},{4,20},{5,21},{6,22},{7,23},{8,24},{9,... | collective-permute-start | bytes 638984 | tf_op jit(solution)/shard_map/ppermute | solution.py:234
  13.4 1.5 %collective-permute-start.2 = (bf16[208,512]{1,0:T(8,128)(2,1)S(1)}, bf16[208,512]{1,0:T(8,128)(2,1)S(1)}, u32[]{:S(2)}, u32[]{:S(2)}) collective-permute-start(bf16[208,512]{1,0:T(8,128)(2,1)S(1)} %pad_maximum_fusion.2.line.refs_0_), channel_id=1, source_target_pairs={{0,8},{1,9},{2,10},{3,11},{4,12},{5,13},{6,14},{7,15},{8,0},{9,1},... | collective-permute-start | bytes 638984 | tf_op jit(solution)/shard_map/ppermute | solution.py:234
  14.9 0.6 %collective-permute-start.4 = (bf16[144,512]{1,0:T(8,128)(2,1)S(1)}, bf16[144,512]{1,0:T(8,128)(2,1)S(1)}, u32[]{:S(2)}, u32[]{:S(2)}) collective-permute-start(bf16[144,512]{1,0:T(8,128)(2,1)S(1)} %get-tuple-element.22), channel_id=1, source_target_pairs={{0,1},{1,0},{2,3},{3,2},{4,6},{5,7},{6,4},{7,5},{8,9},{9,8},{10,11... | collective-permute-start | bytes 442376 | tf_op jit(solution)/shard_map/ppermute | solution.py:234
  15.5 0.5 %collective-permute-start.5 = (bf16[80,512]{1,0:T(8,128)(2,1)S(1)}, bf16[80,512]{1,0:T(8,128)(2,1)S(1)}, u32[]{:S(2)}, u32[]{:S(2)}) collective-permute-start(bf16[80,512]{1,0:T(8,128)(2,1)S(1)} %pad_maximum_fusion.3), channel_id=1, source_target_pairs={{0,24},{1,25},{2,26},{3,27},{4,28},{5,29},{6,30},{7,31},{8,16},{9,... | collective-permute-start | bytes 245768 | tf_op jit(solution)/shard_map/ppermute | solution.py:234
  16.0 3.2 %collective-permute-start.6 = (bf16[16,512]{1,0:T(8,128)(2,1)S(1)}, bf16[16,512]{1,0:T(8,128)(2,1)S(1)}, u32[]{:S(2)}, u32[]{:S(2)}) collective-permute-start(bf16[16,512]{1,0:T(8,128)(2,1)S(1)} %get-tuple-element.19), channel_id=1, source_target_pairs={{0,3},{1,2},{2,1},{3,0},{4,7},{5,6},{6,5},{7,4},{8,11},{9,10},{10,... | collective-permute-start | bytes 49160 | tf_op jit(solution)/shard_map/ppermute | solution.py:234
  19.2 3.0 %collective-permute-done.6.refs_5_ = bf16[16,512]{1,0:T(8,128)(2,1)S(1)} collective-permute-done((bf16[16,512]{1,0:T(8,128)(2,1)S(1)}, bf16[16,512]{1,0:T(8,128)(2,1)S(1)}, u32[]{:S(2)}, u32[]{:S(2)}) %collective-permute-start.6) | collective-permute-done | bytes 16416 | tf_op jit(solution)/shard_map/ppermute | solution.py:234
  22.2 0.0 collective-permute-done.5.refs_4_
  22.2 0.0 collective-permute-done.4.across.refs_3_
  22.2 0.1 collective-permute-start.7
  22.3 0.0 collective-permute-done.3.front.refs_2_
  22.3 0.0 collective-permute-done.2.side.refs_1_
  22.4 0.5 %collective-permute-start.8 = (bf16[416,512]{1,0:T(8,128)(2,1)S(1)}, bf16[416,512]{1,0:T(8,128)(2,1)S(1)}, u32[]{:S(2)}, u32[]{:S(2)}) collective-permute-start(bf16[416,512]{1,0:T(8,128)(2,1)S(1)} %pad_maximum_fusion.1), channel_id=1, source_target_pairs={{0,4},{1,5},{2,6},{3,7},{4,0},{5,1},{6,2},{7,3},{8,12},{9,13},{10,... | collective-permute-start | bytes 1277960 | tf_op jit(solution)/shard_map/ppermute | solution.py:234
  22.9 0.3 %ready.1 = (bf16[512,512]{1,0:T(8,128)(2,1)S(1)}, bf16[512,512]{1,0:T(8,128)(2,1)S(1)}, bf16[512,512]{1,0:T(8,128)(2,1)S(1)}) custom-call(bf16[512,512]{1,0:T(8,128)(2,1)S(1)} %get-tuple-element.18.near, bf16[208,512]{1,0:T(8,128)(2,1)S(1)} %pad_maximum_fusion.2.line.refs_0_, bf16[208,512]{1,0:T(8,128)(2,1)S(1)} %collective-permute-done.2.side.refs_1_, ...), custom_call_target="tpu_custom_call" | custom-call | tf_op jit(solution)/shard_map/ready/pallas_call | solution.py:302
  23.2 0.9 %collective-permute-done.7.refs_6_ = bf16[448,512]{1,0:T(8,128)(2,1)S(1)} collective-permute-done((bf16[448,512]{1,0:T(8,128)(2,1)S(1)}, bf16[448,512]{1,0:T(8,128)(2,1)S(1)}, u32[]{:S(2)}, u32[]{:S(2)}) %collective-permute-start.7) | collective-permute-done | bytes 458784 | tf_op jit(solution)/shard_map/ppermute | solution.py:234
  24.1 0.6 %collective-permute-done.8.refs_7_ = bf16[416,512]{1,0:T(8,128)(2,1)S(1)} collective-permute-done((bf16[416,512]{1,0:T(8,128)(2,1)S(1)}, bf16[416,512]{1,0:T(8,128)(2,1)S(1)}, u32[]{:S(2)}, u32[]{:S(2)}) %collective-permute-start.8) | collective-permute-done | bytes 426016 | tf_op jit(solution)/shard_map/ppermute | solution.py:234
  24.7 5.6 %whole.1 = (f32[1,512]{1,0:T(1,128)}, f32[1,128]{1,0:T(1,128)}, f32[1,128]{1,0:T(1,128)}, f32[1,128]{1,0:T(1,128)}, f32[2]{0:T(128)}) custom-call(bf16[512,512]{1,0:T(8,128)(2,1)S(1)} %get-tuple-element.18.near, bf16[512,512]{1,0:T(8,128)(2,1)S(1)} %get-tuple-element.23.near_turned, bf16[512,512]{1,0:T(8,128)(2,1)S(1)} %get-tuple-element.24.mine, ...), custom_call_target="tpu_custom_call" | custom-call | flops 268435456 | bytes 2097152 | tf_op jit(solution)/shard_map/whole/pallas_call | solution.py:310
  (5 shorter events, 0.1 us)
Async XLA Ops:
  1.6 10.2 %collective-permute-start = (bf16[128,512]{1,0:T(8,128)(2,1)S(1)}, bf16[128,512]{1,0:T(8,128)(2,1)S(1)}, u32[]{:S(2)}, u32[]{:S(2)}) collective-permute-start(bf16[128,512]{1,0:T(8,128)(2,1)S(1)} %constant_dynamic-slice_fusion.1), channel_id=1, source_target_pairs={{0,1},{1,0},{2,3},{3,2},{4,6},{5,7},{6,4},{7,5},{8,9},{9,8},{10,11... | collective-permute-start | bytes 393224 | tf_op jit(solution)/shard_map/ppermute | solution.py:234
  4.6 3.2 %copy-start.3 = (f32[512]{0:T(512)S(1)}, f32[512]{0:T(512)}, u32[]{:S(2)}) copy-start(f32[512]{0:T(512)} %param.10) | copy-start | bytes 6148
  4.6 3.3 %copy-start.4 = (f32[1,512]{1,0:T(1,128)S(1)}, f32[1,512]{1,0:T(1,128)}, u32[]{:S(2)}) copy-start(f32[1,512]{1,0:T(1,128)} %demand.1) | copy-start | bytes 6148
  4.7 7.1 %collective-permute-start.1 = (bf16[64,512]{1,0:T(8,128)(2,1)S(1)}, bf16[64,512]{1,0:T(8,128)(2,1)S(1)}, u32[]{:S(2)}, u32[]{:S(2)}) collective-permute-start(bf16[64,512]{1,0:T(8,128)(2,1)S(1)} %constant_dynamic-slice_fusion), channel_id=1, source_target_pairs={{0,3},{1,2},{2,1},{3,0},{4,7},{5,6},{6,5},{7,4},{8,11},{9,10},{10,... | collective-permute-start | bytes 196616 | tf_op jit(solution)/shard_map/ppermute | solution.py:234
  7.9 0.7 %copy-start.2 = (f32[512]{0:T(512)S(1)}, f32[512]{0:T(512)}, u32[]{:S(2)}) copy-start(f32[512]{0:T(512)} %param.9) | copy-start | bytes 6148
  7.9 0.7 %copy-start.1 = (s32[4,4]{1,0:T(4,128)S(1)}, s32[4,4]{1,0:T(4,128)}, u32[]{:S(2)}) copy-start(s32[4,4]{1,0:T(4,128)} %incidence.1) | copy-start | bytes 196
  7.9 0.7 %copy-start.5 = (s32[128]{0:T(128)S(1)}, s32[128]{0:T(128)}, u32[]{:S(2)}) copy-start(s32[128]{0:T(128)} %param.13) | copy-start | bytes 1540
  8.6 1.0 %copy-start = (bf16[512,512]{1,0:T(8,128)(2,1)S(1)}, bf16[512,512]{1,0:T(8,128)(2,1)}, u32[]{:S(2)}) copy-start(bf16[512,512]{1,0:T(8,128)(2,1)} %coupling.1) | copy-start | bytes 1572868
  11.8 10.5 %collective-permute-start.3 = (bf16[208,512]{1,0:T(8,128)(2,1)S(1)}, bf16[208,512]{1,0:T(8,128)(2,1)S(1)}, u32[]{:S(2)}, u32[]{:S(2)}) collective-permute-start(bf16[208,512]{1,0:T(8,128)(2,1)S(1)} %pad_maximum_fusion.2.line.refs_0_), channel_id=1, source_target_pairs={{0,16},{1,17},{2,18},{3,19},{4,20},{5,21},{6,22},{7,23},{8,24},{9,... | collective-permute-start | bytes 638984 | tf_op jit(solution)/shard_map/ppermute | solution.py:234
  13.4 8.9 %collective-permute-start.2 = (bf16[208,512]{1,0:T(8,128)(2,1)S(1)}, bf16[208,512]{1,0:T(8,128)(2,1)S(1)}, u32[]{:S(2)}, u32[]{:S(2)}) collective-permute-start(bf16[208,512]{1,0:T(8,128)(2,1)S(1)} %pad_maximum_fusion.2.line.refs_0_), channel_id=1, source_target_pairs={{0,8},{1,9},{2,10},{3,11},{4,12},{5,13},{6,14},{7,15},{8,0},{9,1},... | collective-permute-start | bytes 638984 | tf_op jit(solution)/shard_map/ppermute | solution.py:234
  14.9 7.3 %collective-permute-start.4 = (bf16[144,512]{1,0:T(8,128)(2,1)S(1)}, bf16[144,512]{1,0:T(8,128)(2,1)S(1)}, u32[]{:S(2)}, u32[]{:S(2)}) collective-permute-start(bf16[144,512]{1,0:T(8,128)(2,1)S(1)} %get-tuple-element.22), channel_id=1, source_target_pairs={{0,1},{1,0},{2,3},{3,2},{4,6},{5,7},{6,4},{7,5},{8,9},{9,8},{10,11... | collective-permute-start | bytes 442376 | tf_op jit(solution)/shard_map/ppermute | solution.py:234
  15.5 6.7 %collective-permute-start.5 = (bf16[80,512]{1,0:T(8,128)(2,1)S(1)}, bf16[80,512]{1,0:T(8,128)(2,1)S(1)}, u32[]{:S(2)}, u32[]{:S(2)}) collective-permute-start(bf16[80,512]{1,0:T(8,128)(2,1)S(1)} %pad_maximum_fusion.3), channel_id=1, source_target_pairs={{0,24},{1,25},{2,26},{3,27},{4,28},{5,29},{6,30},{7,31},{8,16},{9,... | collective-permute-start | bytes 245768 | tf_op jit(solution)/shard_map/ppermute | solution.py:234
  16.0 6.2 %collective-permute-start.6 = (bf16[16,512]{1,0:T(8,128)(2,1)S(1)}, bf16[16,512]{1,0:T(8,128)(2,1)S(1)}, u32[]{:S(2)}, u32[]{:S(2)}) collective-permute-start(bf16[16,512]{1,0:T(8,128)(2,1)S(1)} %get-tuple-element.19), channel_id=1, source_target_pairs={{0,3},{1,2},{2,1},{3,0},{4,7},{5,6},{6,5},{7,4},{8,11},{9,10},{10,... | collective-permute-start | bytes 49160 | tf_op jit(solution)/shard_map/ppermute | solution.py:234
  22.2 1.9 %collective-permute-start.7 = (bf16[448,512]{1,0:T(8,128)(2,1)S(1)}, bf16[448,512]{1,0:T(8,128)(2,1)S(1)}, u32[]{:S(2)}, u32[]{:S(2)}) collective-permute-start(bf16[448,512]{1,0:T(8,128)(2,1)S(1)} %pad_maximum_fusion), channel_id=1, source_target_pairs={{0,4},{1,5},{2,6},{3,7},{4,0},{5,1},{6,2},{7,3},{8,12},{9,13},{10,... | collective-permute-start | bytes 1376264 | tf_op jit(solution)/shard_map/ppermute | solution.py:234
  22.4 2.4 %collective-permute-start.8 = (bf16[416,512]{1,0:T(8,128)(2,1)S(1)}, bf16[416,512]{1,0:T(8,128)(2,1)S(1)}, u32[]{:S(2)}, u32[]{:S(2)}) collective-permute-start(bf16[416,512]{1,0:T(8,128)(2,1)S(1)} %pad_maximum_fusion.1), channel_id=1, source_target_pairs={{0,4},{1,5},{2,6},{3,7},{4,0},{5,1},{6,2},{7,3},{8,12},{9,13},{10,... | collective-permute-start | bytes 1277960 | tf_op jit(solution)/shard_map/ppermute | solution.py:234

commit v9 on v8

--- a/solution.py
+++ b/solution.py
@@ -11,7 +11,7 @@
 ITERS = 4
 ROUNDS = 2
 EXTRA = 16
-GROUPS = ((0, 3, 4, 5), (1, 2))
+GROUPS = ((0, 3, 5), (1, 2, 4))
 
 primal_step = 0.9
 dual_step = 0.9

time: 30.5 us -> 30.2 us (level)
  starting transfers between devices: 13.6 us -> 13.2 us
    ppermute x9, starting transfers between devices: 13.6 us -> 13.2 us  [swap(): return lax.ppermute(value, ('scen', 'arc'), pairs)]
where the time goes in v9:
time: 30.2 us; the launch traced here: 30 us
  starting transfers between devices  13.2 us (44%)
  Pallas kernels  7.41 us (25%)
  waiting for transfers between devices  5.36 us (18%)
  local copies, waits for them, and re-layouts  2.63 us (9%)
  between operations  1.39 us (5%)
    ppermute x9, starting transfers between devices, swap(): return lax.ppermute(value, ('scen', 'arc'), pairs)  13.2 us
    pallas_call x1, Pallas kernels, body(): pl.pallas_call(whole_kernel, out_shape=out_shape, in_specs=[VMEM] * (len(...  5.57 us
    ppermute x9, waiting for transfers between devices, swap(): return lax.ppermute(value, ('scen', 'arc'), pairs)  5.36 us
    unnamed x12, local copies, waits for them, and re-layouts  1.71 us
    pallas_call x1, Pallas kernels, body(): pl.pallas_call(pack_kernel, out_shape=(like(total_rows), like(TILE + EXTR...  1.52 us
    dynamic_slice x1, local copies, waits for them, and re-layouts, bring(): lax.dynamic_slice_in_dim(coupling, lax.shift_right_logical(scen, 1) * TIL...  0.92 us
  transfers between devices with their start and end apart: 9, of which 4 were waited for; matrix products, arithmetic and copies ran while one was open for 0% of the time, Pallas kernels for 6%

profile of v9, /device:TPU:0, one launch (start us, length us, event | category | flops | bytes accessed | tf_op | source)
XLA Modules:
  0.0 30.0 jit_solution(11423280732755303195)
XLA Ops:
  0.6 0.9 %constant_dynamic-slice_fusion.1 = bf16[128,512]{1,0:T(8,128)(2,1)S(1)} fusion(bf16[512,512]{1,0:T(8,128)(2,1)} %coupling.1, s32[]{:T(128)S(6)} %select_n.6), kind=kLoop, calls=%fused_computation.5 | loop fusion | bytes 262148 | tf_op jit(solution)/shard_map/dynamic_slice | solution.py:240
  1.6 3.1 %collective-permute-start = (bf16[128,512]{1,0:T(8,128)(2,1)S(1)}, bf16[128,512]{1,0:T(8,128)(2,1)S(1)}, u32[]{:S(2)}, u32[]{:S(2)}) collective-permute-start(bf16[128,512]{1,0:T(8,128)(2,1)S(1)} %constant_dynamic-slice_fusion.1), channel_id=1, source_target_pairs={{0,1},{1,0},{2,3},{3,2},{4,6},{5,7},{6,4},{7,5},{8,9},{9,8},{10,11... | collective-permute-start | bytes 393224 | tf_op jit(solution)/shard_map/ppermute | solution.py:234
  4.6 0.0 copy-start.3
  4.6 0.0 copy-start.4
  4.7 2.5 %collective-permute-start.1 = (bf16[64,512]{1,0:T(8,128)(2,1)S(1)}, bf16[64,512]{1,0:T(8,128)(2,1)S(1)}, u32[]{:S(2)}, u32[]{:S(2)}) collective-permute-start(bf16[64,512]{1,0:T(8,128)(2,1)S(1)} %constant_dynamic-slice_fusion), channel_id=1, source_target_pairs={{0,3},{1,2},{2,1},{3,0},{4,7},{5,6},{6,5},{7,4},{8,11},{9,10},{10,... | collective-permute-start | bytes 196616 | tf_op jit(solution)/shard_map/ppermute | solution.py:234
  7.9 0.0 copy-start.2
  7.9 0.0 copy-start.1
  7.9 0.0 copy-start.5
  7.9 0.0 copy-done.3
  7.9 0.0 copy-done.4
  7.9 0.6 %copy-done.2 = f32[512]{0:T(512)S(1)} copy-done((f32[512]{0:T(512)S(1)}, f32[512]{0:T(512)}, u32[]{:S(2)}) %copy-start.2) | copy-done | bytes 2072
  8.5 0.0 copy-done.1
  8.6 0.0 copy-done.5
  8.6 0.0 copy-start
  8.6 1.0 %copy-done = bf16[512,512]{1,0:T(8,128)(2,1)S(1)} copy-done((bf16[512,512]{1,0:T(8,128)(2,1)S(1)}, bf16[512,512]{1,0:T(8,128)(2,1)}, u32[]{:S(2)}) %copy-start) | copy-done | bytes 524312
  9.6 1.5 %pack.1 = (bf16[512,512]{1,0:T(8,128)(2,1)S(1)}, bf16[144,512]{1,0:T(8,128)(2,1)S(1)}, bf16[16,512]{1,0:T(8,128)(2,1)S(1)}) custom-call(bf16[512,512]{1,0:T(8,128)(2,1)S(1)} %copy-done, s32[4,4]{1,0:T(4,128)S(1)} %copy-done.1, f32[1,512]{1,0:T(1,128)S(1)} %bitcast.6, f32[1,512]{1,0:T(1,128)S(1)} %bitcast.7, f32[1,512]{1,0:T(1,128)S(1)} %copy-done.4, ...), custom_call_target="tpu_custom_call" | custom-call | tf_op jit(solution)/shard_map/pack/pallas_call | solution.py:288
  11.1 0.6 %collective-permute-done.1 = bf16[64,512]{1,0:T(8,128)(2,1)S(1)} collective-permute-done((bf16[64,512]{1,0:T(8,128)(2,1)S(1)}, bf16[64,512]{1,0:T(8,128)(2,1)S(1)}, u32[]{:S(2)}, u32[]{:S(2)}) %collective-permute-start.1) | collective-permute-done | bytes 65568 | tf_op jit(solution)/shard_map/ppermute | solution.py:234
  11.8 0.0 collective-permute-done
  11.8 1.6 %collective-permute-start.3 = (bf16[208,512]{1,0:T(8,128)(2,1)S(1)}, bf16[208,512]{1,0:T(8,128)(2,1)S(1)}, u32[]{:S(2)}, u32[]{:S(2)}) collective-permute-start(bf16[208,512]{1,0:T(8,128)(2,1)S(1)} %pad_maximum_fusion.2.line.refs_0_), channel_id=1, source_target_pairs={{0,16},{1,17},{2,18},{3,19},{4,20},{5,21},{6,22},{7,23},{8,24},{9,... | collective-permute-start | bytes 638984 | tf_op jit(solution)/shard_map/ppermute | solution.py:234
  13.4 1.5 %collective-permute-start.2 = (bf16[208,512]{1,0:T(8,128)(2,1)S(1)}, bf16[208,512]{1,0:T(8,128)(2,1)S(1)}, u32[]{:S(2)}, u32[]{:S(2)}) collective-permute-start(bf16[208,512]{1,0:T(8,128)(2,1)S(1)} %pad_maximum_fusion.2.line.refs_0_), channel_id=1, source_target_pairs={{0,8},{1,9},{2,10},{3,11},{4,12},{5,13},{6,14},{7,15},{8,0},{9,1},... | collective-permute-start | bytes 638984 | tf_op jit(solution)/shard_map/ppermute | solution.py:234
  14.9 0.5 %collective-permute-start.5 = (bf16[80,512]{1,0:T(8,128)(2,1)S(1)}, bf16[80,512]{1,0:T(8,128)(2,1)S(1)}, u32[]{:S(2)}, u32[]{:S(2)}) collective-permute-start(bf16[80,512]{1,0:T(8,128)(2,1)S(1)} %pad_maximum_fusion.3), channel_id=1, source_target_pairs={{0,24},{1,25},{2,26},{3,27},{4,28},{5,29},{6,30},{7,31},{8,16},{9,... | collective-permute-start | bytes 245768 | tf_op jit(solution)/shard_map/ppermute | solution.py:234
  15.4 0.6 %collective-permute-start.4 = (bf16[144,512]{1,0:T(8,128)(2,1)S(1)}, bf16[144,512]{1,0:T(8,128)(2,1)S(1)}, u32[]{:S(2)}, u32[]{:S(2)}) collective-permute-start(bf16[144,512]{1,0:T(8,128)(2,1)S(1)} %get-tuple-element.22), channel_id=1, source_target_pairs={{0,1},{1,0},{2,3},{3,2},{4,6},{5,7},{6,4},{7,5},{8,9},{9,8},{10,11... | collective-permute-start | bytes 442376 | tf_op jit(solution)/shard_map/ppermute | solution.py:234
  16.0 3.2 %collective-permute-start.6 = (bf16[16,512]{1,0:T(8,128)(2,1)S(1)}, bf16[16,512]{1,0:T(8,128)(2,1)S(1)}, u32[]{:S(2)}, u32[]{:S(2)}) collective-permute-start(bf16[16,512]{1,0:T(8,128)(2,1)S(1)} %get-tuple-element.19), channel_id=1, source_target_pairs={{0,3},{1,2},{2,1},{3,0},{4,7},{5,6},{6,5},{7,4},{8,11},{9,10},{10,... | collective-permute-start | bytes 49160 | tf_op jit(solution)/shard_map/ppermute | solution.py:234
  19.2 2.2 %collective-permute-done.5.refs_4_ = bf16[80,512]{1,0:T(8,128)(2,1)S(1)} collective-permute-done((bf16[80,512]{1,0:T(8,128)(2,1)S(1)}, bf16[80,512]{1,0:T(8,128)(2,1)S(1)}, u32[]{:S(2)}, u32[]{:S(2)}) %collective-permute-start.5) | collective-permute-done | bytes 81952 | tf_op jit(solution)/shard_map/ppermute | solution.py:234
  21.4 0.0 collective-permute-done.3.front.refs_2_
  21.4 0.0 collective-permute-done.2.side.refs_1_
  21.4 0.1 collective-permute-start.8
  21.5 1.1 %collective-permute-done.6.refs_5_ = bf16[16,512]{1,0:T(8,128)(2,1)S(1)} collective-permute-done((bf16[16,512]{1,0:T(8,128)(2,1)S(1)}, bf16[16,512]{1,0:T(8,128)(2,1)S(1)}, u32[]{:S(2)}, u32[]{:S(2)}) %collective-permute-start.6) | collective-permute-done | bytes 16416 | tf_op jit(solution)/shard_map/ppermute | solution.py:234
  22.7 0.0 collective-permute-done.4.across.refs_3_
  22.7 0.1 collective-permute-start.7
  22.8 0.3 %ready.1 = (bf16[512,512]{1,0:T(8,128)(2,1)S(1)}, bf16[512,512]{1,0:T(8,128)(2,1)S(1)}, bf16[512,512]{1,0:T(8,128)(2,1)S(1)}) custom-call(bf16[512,512]{1,0:T(8,128)(2,1)S(1)} %get-tuple-element.18.near, bf16[208,512]{1,0:T(8,128)(2,1)S(1)} %pad_maximum_fusion.2.line.refs_0_, bf16[208,512]{1,0:T(8,128)(2,1)S(1)} %collective-permute-done.2.side.refs_1_, ...), custom_call_target="tpu_custom_call" | custom-call | tf_op jit(solution)/shard_map/ready/pallas_call | solution.py:302
  23.1 1.4 %collective-permute-done.7.refs_6_ = bf16[368,512]{1,0:T(8,128)(2,1)S(1)} collective-permute-done((bf16[368,512]{1,0:T(8,128)(2,1)S(1)}, bf16[368,512]{1,0:T(8,128)(2,1)S(1)}, u32[]{:S(2)}, u32[]{:S(2)}) %collective-permute-start.7) | collective-permute-done | bytes 376864 | tf_op jit(solution)/shard_map/ppermute | solution.py:234
  24.5 0.0 collective-permute-done.8.refs_7_
  24.5 5.6 %whole.1 = (f32[1,512]{1,0:T(1,128)}, f32[1,128]{1,0:T(1,128)}, f32[1,128]{1,0:T(1,128)}, f32[1,128]{1,0:T(1,128)}, f32[2]{0:T(128)}) custom-call(bf16[512,512]{1,0:T(8,128)(2,1)S(1)} %get-tuple-element.18.near, bf16[512,512]{1,0:T(8,128)(2,1)S(1)} %get-tuple-element.23.near_turned, bf16[512,512]{1,0:T(8,128)(2,1)S(1)} %get-tuple-element.24.mine, ...), custom_call_target="tpu_custom_call" | custom-call | flops 268435456 | bytes 2097152 | tf_op jit(solution)/shard_map/whole/pallas_call | solution.py:310
  (5 shorter events, 0.1 us)
Async XLA Ops:
  1.6 10.2 %collective-permute-start = (bf16[128,512]{1,0:T(8,128)(2,1)S(1)}, bf16[128,512]{1,0:T(8,128)(2,1)S(1)}, u32[]{:S(2)}, u32[]{:S(2)}) collective-permute-start(bf16[128,512]{1,0:T(8,128)(2,1)S(1)} %constant_dynamic-slice_fusion.1), channel_id=1, source_target_pairs={{0,1},{1,0},{2,3},{3,2},{4,6},{5,7},{6,4},{7,5},{8,9},{9,8},{10,11... | collective-permute-start | bytes 393224 | tf_op jit(solution)/shard_map/ppermute | solution.py:234
  4.6 3.2 %copy-start.3 = (f32[512]{0:T(512)S(1)}, f32[512]{0:T(512)}, u32[]{:S(2)}) copy-start(f32[512]{0:T(512)} %param.10) | copy-start | bytes 6148
  4.6 3.3 %copy-start.4 = (f32[1,512]{1,0:T(1,128)S(1)}, f32[1,512]{1,0:T(1,128)}, u32[]{:S(2)}) copy-start(f32[1,512]{1,0:T(1,128)} %demand.1) | copy-start | bytes 6148
  4.7 7.1 %collective-permute-start.1 = (bf16[64,512]{1,0:T(8,128)(2,1)S(1)}, bf16[64,512]{1,0:T(8,128)(2,1)S(1)}, u32[]{:S(2)}, u32[]{:S(2)}) collective-permute-start(bf16[64,512]{1,0:T(8,128)(2,1)S(1)} %constant_dynamic-slice_fusion), channel_id=1, source_target_pairs={{0,3},{1,2},{2,1},{3,0},{4,7},{5,6},{6,5},{7,4},{8,11},{9,10},{10,... | collective-permute-start | bytes 196616 | tf_op jit(solution)/shard_map/ppermute | solution.py:234
  7.9 0.7 %copy-start.2 = (f32[512]{0:T(512)S(1)}, f32[512]{0:T(512)}, u32[]{:S(2)}) copy-start(f32[512]{0:T(512)} %param.9) | copy-start | bytes 6148
  7.9 0.7 %copy-start.1 = (s32[4,4]{1,0:T(4,128)S(1)}, s32[4,4]{1,0:T(4,128)}, u32[]{:S(2)}) copy-start(s32[4,4]{1,0:T(4,128)} %incidence.1) | copy-start | bytes 196
  7.9 0.7 %copy-start.5 = (s32[128]{0:T(128)S(1)}, s32[128]{0:T(128)}, u32[]{:S(2)}) copy-start(s32[128]{0:T(128)} %param.13) | copy-start | bytes 1540
  8.6 1.0 %copy-start = (bf16[512,512]{1,0:T(8,128)(2,1)S(1)}, bf16[512,512]{1,0:T(8,128)(2,1)}, u32[]{:S(2)}) copy-start(bf16[512,512]{1,0:T(8,128)(2,1)} %coupling.1) | copy-start | bytes 1572868
  11.8 9.6 %collective-permute-start.3 = (bf16[208,512]{1,0:T(8,128)(2,1)S(1)}, bf16[208,512]{1,0:T(8,128)(2,1)S(1)}, u32[]{:S(2)}, u32[]{:S(2)}) collective-permute-start(bf16[208,512]{1,0:T(8,128)(2,1)S(1)} %pad_maximum_fusion.2.line.refs_0_), channel_id=1, source_target_pairs={{0,16},{1,17},{2,18},{3,19},{4,20},{5,21},{6,22},{7,23},{8,24},{9,... | collective-permute-start | bytes 638984 | tf_op jit(solution)/shard_map/ppermute | solution.py:234
  13.4 8.0 %collective-permute-start.2 = (bf16[208,512]{1,0:T(8,128)(2,1)S(1)}, bf16[208,512]{1,0:T(8,128)(2,1)S(1)}, u32[]{:S(2)}, u32[]{:S(2)}) collective-permute-start(bf16[208,512]{1,0:T(8,128)(2,1)S(1)} %pad_maximum_fusion.2.line.refs_0_), channel_id=1, source_target_pairs={{0,8},{1,9},{2,10},{3,11},{4,12},{5,13},{6,14},{7,15},{8,0},{9,1},... | collective-permute-start | bytes 638984 | tf_op jit(solution)/shard_map/ppermute | solution.py:234
  14.9 6.5 %collective-permute-start.5 = (bf16[80,512]{1,0:T(8,128)(2,1)S(1)}, bf16[80,512]{1,0:T(8,128)(2,1)S(1)}, u32[]{:S(2)}, u32[]{:S(2)}) collective-permute-start(bf16[80,512]{1,0:T(8,128)(2,1)S(1)} %pad_maximum_fusion.3), channel_id=1, source_target_pairs={{0,24},{1,25},{2,26},{3,27},{4,28},{5,29},{6,30},{7,31},{8,16},{9,... | collective-permute-start | bytes 245768 | tf_op jit(solution)/shard_map/ppermute | solution.py:234
  15.4 7.3 %collective-permute-start.4 = (bf16[144,512]{1,0:T(8,128)(2,1)S(1)}, bf16[144,512]{1,0:T(8,128)(2,1)S(1)}, u32[]{:S(2)}, u32[]{:S(2)}) collective-permute-start(bf16[144,512]{1,0:T(8,128)(2,1)S(1)} %get-tuple-element.22), channel_id=1, source_target_pairs={{0,1},{1,0},{2,3},{3,2},{4,6},{5,7},{6,4},{7,5},{8,9},{9,8},{10,11... | collective-permute-start | bytes 442376 | tf_op jit(solution)/shard_map/ppermute | solution.py:234
  16.0 6.7 %collective-permute-start.6 = (bf16[16,512]{1,0:T(8,128)(2,1)S(1)}, bf16[16,512]{1,0:T(8,128)(2,1)S(1)}, u32[]{:S(2)}, u32[]{:S(2)}) collective-permute-start(bf16[16,512]{1,0:T(8,128)(2,1)S(1)} %get-tuple-element.19), channel_id=1, source_target_pairs={{0,3},{1,2},{2,1},{3,0},{4,7},{5,6},{6,5},{7,4},{8,11},{9,10},{10,... | collective-permute-start | bytes 49160 | tf_op jit(solution)/shard_map/ppermute | solution.py:234
  21.4 3.0 %collective-permute-start.8 = (bf16[496,512]{1,0:T(8,128)(2,1)S(1)}, bf16[496,512]{1,0:T(8,128)(2,1)S(1)}, u32[]{:S(2)}, u32[]{:S(2)}) collective-permute-start(bf16[496,512]{1,0:T(8,128)(2,1)S(1)} %pad_maximum_fusion), channel_id=1, source_target_pairs={{0,4},{1,5},{2,6},{3,7},{4,0},{5,1},{6,2},{7,3},{8,12},{9,13},{10,... | collective-permute-start | bytes 1523720 | tf_op jit(solution)/shard_map/ppermute | solution.py:234
  22.7 1.8 %collective-permute-start.7 = (bf16[368,512]{1,0:T(8,128)(2,1)S(1)}, bf16[368,512]{1,0:T(8,128)(2,1)S(1)}, u32[]{:S(2)}, u32[]{:S(2)}) collective-permute-start(bf16[368,512]{1,0:T(8,128)(2,1)S(1)} %pad_maximum_fusion.1), channel_id=1, source_target_pairs={{0,4},{1,5},{2,6},{3,7},{4,0},{5,1},{6,2},{7,3},{8,12},{9,13},{10,... | collective-permute-start | bytes 1130504 | tf_op jit(solution)/shard_map/ppermute | solution.py:234

commit v10 on v9

--- a/solution.py
+++ b/solution.py
@@ -85,7 +85,8 @@
            flows, duals, prices, centre, shifted):
     scenarios, total_rows = demand.shape
     block_arcs = cost.shape[1] // blocks
-    weight_sum = jnp.sum(share[:, :1])
+    weight_sum = jnp.sum(share[:, :1], axis=0, keepdims=True)
+    spreads = []
     for round_index in range(ROUNDS):
         for step_index in range(ITERS):
             first = round_index == 0 and step_index == 0
@@ -117,19 +118,25 @@
                 load = load + jnp.dot(jnp.concatenate(bars, axis=1), weights, preferred_element_type=jnp.float32)
             step = dual_step * (load - demand[...])
             duals[...] = jnp.maximum(step if first else duals[...] + step, 0.0)
-        squares = jnp.float32(0.0)
+        squares = jnp.zeros((1, block_arcs), jnp.float32)
         for block in range(blocks):
             cols = slice(block * block_arcs, (block + 1) * block_arcs)
             fleet = flows[:, cols] * mask[:, cols]
             share_col = share[:, :1]
             mean = jnp.sum(share_col * fleet, axis=0, keepdims=True) / weight_sum
             gap = fleet - mean
-            squares = squares + jnp.sum(share_col * gap * gap)
+            squares = squares + jnp.sum(share_col * gap * gap, axis=0, keepdims=True)
             total = penalty * gap if round_index == 0 else prices[:, cols] + penalty * gap
             prices[:, cols] = total
             centre[:, cols] = mean
             shifted[:, cols] = total - penalty * mean
-        spread_out[round_index] = jnp.sqrt(squares / (weight_sum * fleet_count) + 1e-06)
+        squares = jnp.sum(squares, axis=1, keepdims=True)
+        spreads.append(jnp.sqrt(squares / (weight_sum * fleet_count) + 1e-06))
+    lanes = lax.broadcasted_iota(jnp.int32, spread_out.shape, 1)
+    spread = jnp.broadcast_to(spreads[0], spread_out.shape)
+    for round_index in range(1, ROUNDS):
+        spread = jnp.where(lanes == round_index, spreads[round_index], spread)
+    spread_out[...] = spread
 
 
 def pick_fleet(price, mean, slots):
@@ -266,9 +273,9 @@
         jax.ShapeDtypeStruct((1, total_rows // blocks), jnp.float32),
         jax.ShapeDtypeStruct((1, fleet_block), jnp.float32),
         jax.ShapeDtypeStruct((1, fleet_block), jnp.float32),
-        jax.ShapeDtypeStruct((ROUNDS,), jnp.float32),
+        jax.ShapeDtypeStruct((1, ROUNDS), jnp.float32),
     )
-    out_specs = (VMEM, VMEM, VMEM, VMEM, SMEM)
+    out_specs = (VMEM,) * 5
     state = [
         pltpu.VMEM((scenarios, arcs), jnp.float32),
         pltpu.VMEM((scenarios, total_rows), jnp.float32),
@@ -349,7 +356,7 @@
         )(masked, per_arc[0:1], per_arc[1:2], per_arc[2:3], per_scen[:, :total_rows],
           per_scen[:, total_rows:], slots)
     flows, duals, multipliers, consensus, spread = outs
-    return flows, duals, multipliers, consensus.reshape(-1), spread
+    return flows, duals, multipliers, consensus.reshape(-1), spread.reshape(-1)
 
 
 def solution(mesh):

time: 30.2 us -> 30.2 us (level)
  no operation moved by 1% of the time
where the time goes in v10:
time: 30.2 us; the launch traced here: 30 us
  starting transfers between devices  13.2 us (44%)
  Pallas kernels  7.38 us (24%)
  waiting for transfers between devices  5.36 us (18%)
  local copies, waits for them, and re-layouts  2.63 us (9%)
  between operations  1.39 us (5%)
    ppermute x9, starting transfers between devices, swap(): return lax.ppermute(value, ('scen', 'arc'), pairs)  13.2 us
    pallas_call x1, Pallas kernels, body(): pl.pallas_call(whole_kernel, out_shape=out_shape, in_specs=[VMEM] * (len(...  5.54 us
    ppermute x9, waiting for transfers between devices, swap(): return lax.ppermute(value, ('scen', 'arc'), pairs)  5.36 us
    unnamed x12, local copies, waits for them, and re-layouts  1.71 us
    pallas_call x1, Pallas kernels, body(): pl.pallas_call(pack_kernel, out_shape=(like(total_rows), like(TILE + EXTR...  1.52 us
    dynamic_slice x1, local copies, waits for them, and re-layouts, bring(): lax.dynamic_slice_in_dim(coupling, lax.shift_right_logical(scen, 1) * TIL...  0.92 us
  transfers between devices with their start and end apart: 9, of which 4 were waited for; matrix products, arithmetic and copies ran while one was open for 0% of the time, Pallas kernels for 6%

profile of v10, /device:TPU:0, one launch (start us, length us, event | category | flops | bytes accessed | tf_op | source)
XLA Modules:
  0.0 30.0 jit_solution(14475067712304463100)
XLA Ops:
  0.6 0.9 %constant_dynamic-slice_fusion.1 = bf16[128,512]{1,0:T(8,128)(2,1)S(1)} fusion(bf16[512,512]{1,0:T(8,128)(2,1)} %coupling.1, s32[]{:T(128)S(6)} %select_n.6), kind=kLoop, calls=%fused_computation.5 | loop fusion | bytes 262148 | tf_op jit(solution)/shard_map/dynamic_slice | solution.py:247
  1.6 3.1 %collective-permute-start = (bf16[128,512]{1,0:T(8,128)(2,1)S(1)}, bf16[128,512]{1,0:T(8,128)(2,1)S(1)}, u32[]{:S(2)}, u32[]{:S(2)}) collective-permute-start(bf16[128,512]{1,0:T(8,128)(2,1)S(1)} %constant_dynamic-slice_fusion.1), channel_id=1, source_target_pairs={{0,1},{1,0},{2,3},{3,2},{4,6},{5,7},{6,4},{7,5},{8,9},{9,8},{10,11... | collective-permute-start | bytes 393224 | tf_op jit(solution)/shard_map/ppermute | solution.py:241
  4.6 0.0 copy-start.3
  4.6 0.0 copy-start.4
  4.7 2.5 %collective-permute-start.1 = (bf16[64,512]{1,0:T(8,128)(2,1)S(1)}, bf16[64,512]{1,0:T(8,128)(2,1)S(1)}, u32[]{:S(2)}, u32[]{:S(2)}) collective-permute-start(bf16[64,512]{1,0:T(8,128)(2,1)S(1)} %constant_dynamic-slice_fusion), channel_id=1, source_target_pairs={{0,3},{1,2},{2,1},{3,0},{4,7},{5,6},{6,5},{7,4},{8,11},{9,10},{10,... | collective-permute-start | bytes 196616 | tf_op jit(solution)/shard_map/ppermute | solution.py:241
  7.9 0.0 copy-start.2
  7.9 0.0 copy-start.1
  7.9 0.0 copy-start.5
  7.9 0.0 copy-done.3
  7.9 0.0 copy-done.4
  7.9 0.6 %copy-done.2 = f32[512]{0:T(512)S(1)} copy-done((f32[512]{0:T(512)S(1)}, f32[512]{0:T(512)}, u32[]{:S(2)}) %copy-start.2) | copy-done | bytes 2072
  8.5 0.0 copy-done.1
  8.6 0.0 copy-done.5
  8.6 0.0 copy-start
  8.6 1.0 %copy-done = bf16[512,512]{1,0:T(8,128)(2,1)S(1)} copy-done((bf16[512,512]{1,0:T(8,128)(2,1)S(1)}, bf16[512,512]{1,0:T(8,128)(2,1)}, u32[]{:S(2)}) %copy-start) | copy-done | bytes 524312
  9.6 1.5 %pack.1 = (bf16[512,512]{1,0:T(8,128)(2,1)S(1)}, bf16[144,512]{1,0:T(8,128)(2,1)S(1)}, bf16[16,512]{1,0:T(8,128)(2,1)S(1)}) custom-call(bf16[512,512]{1,0:T(8,128)(2,1)S(1)} %copy-done, s32[4,4]{1,0:T(4,128)S(1)} %copy-done.1, f32[1,512]{1,0:T(1,128)S(1)} %bitcast.7, f32[1,512]{1,0:T(1,128)S(1)} %bitcast.8, f32[1,512]{1,0:T(1,128)S(1)} %copy-done.4, ...), custom_call_target="tpu_custom_call" | custom-call | tf_op jit(solution)/shard_map/pack/pallas_call | solution.py:295
  11.1 0.6 %collective-permute-done.1 = bf16[64,512]{1,0:T(8,128)(2,1)S(1)} collective-permute-done((bf16[64,512]{1,0:T(8,128)(2,1)S(1)}, bf16[64,512]{1,0:T(8,128)(2,1)S(1)}, u32[]{:S(2)}, u32[]{:S(2)}) %collective-permute-start.1) | collective-permute-done | bytes 65568 | tf_op jit(solution)/shard_map/ppermute | solution.py:241
  11.8 0.0 collective-permute-done
  11.8 1.6 %collective-permute-start.3 = (bf16[208,512]{1,0:T(8,128)(2,1)S(1)}, bf16[208,512]{1,0:T(8,128)(2,1)S(1)}, u32[]{:S(2)}, u32[]{:S(2)}) collective-permute-start(bf16[208,512]{1,0:T(8,128)(2,1)S(1)} %pad_maximum_fusion.2.line.refs_0_), channel_id=1, source_target_pairs={{0,16},{1,17},{2,18},{3,19},{4,20},{5,21},{6,22},{7,23},{8,24},{9,... | collective-permute-start | bytes 638984 | tf_op jit(solution)/shard_map/ppermute | solution.py:241
  13.4 1.5 %collective-permute-start.2 = (bf16[208,512]{1,0:T(8,128)(2,1)S(1)}, bf16[208,512]{1,0:T(8,128)(2,1)S(1)}, u32[]{:S(2)}, u32[]{:S(2)}) collective-permute-start(bf16[208,512]{1,0:T(8,128)(2,1)S(1)} %pad_maximum_fusion.2.line.refs_0_), channel_id=1, source_target_pairs={{0,8},{1,9},{2,10},{3,11},{4,12},{5,13},{6,14},{7,15},{8,0},{9,1},... | collective-permute-start | bytes 638984 | tf_op jit(solution)/shard_map/ppermute | solution.py:241
  14.9 0.5 %collective-permute-start.5 = (bf16[80,512]{1,0:T(8,128)(2,1)S(1)}, bf16[80,512]{1,0:T(8,128)(2,1)S(1)}, u32[]{:S(2)}, u32[]{:S(2)}) collective-permute-start(bf16[80,512]{1,0:T(8,128)(2,1)S(1)} %pad_maximum_fusion.3), channel_id=1, source_target_pairs={{0,24},{1,25},{2,26},{3,27},{4,28},{5,29},{6,30},{7,31},{8,16},{9,... | collective-permute-start | bytes 245768 | tf_op jit(solution)/shard_map/ppermute | solution.py:241
  15.4 0.6 %collective-permute-start.4 = (bf16[144,512]{1,0:T(8,128)(2,1)S(1)}, bf16[144,512]{1,0:T(8,128)(2,1)S(1)}, u32[]{:S(2)}, u32[]{:S(2)}) collective-permute-start(bf16[144,512]{1,0:T(8,128)(2,1)S(1)} %get-tuple-element.22), channel_id=1, source_target_pairs={{0,1},{1,0},{2,3},{3,2},{4,6},{5,7},{6,4},{7,5},{8,9},{9,8},{10,11... | collective-permute-start | bytes 442376 | tf_op jit(solution)/shard_map/ppermute | solution.py:241
  16.0 3.2 %collective-permute-start.6 = (bf16[16,512]{1,0:T(8,128)(2,1)S(1)}, bf16[16,512]{1,0:T(8,128)(2,1)S(1)}, u32[]{:S(2)}, u32[]{:S(2)}) collective-permute-start(bf16[16,512]{1,0:T(8,128)(2,1)S(1)} %get-tuple-element.19), channel_id=1, source_target_pairs={{0,3},{1,2},{2,1},{3,0},{4,7},{5,6},{6,5},{7,4},{8,11},{9,10},{10,... | collective-permute-start | bytes 49160 | tf_op jit(solution)/shard_map/ppermute | solution.py:241
  19.2 2.2 %collective-permute-done.5.refs_4_ = bf16[80,512]{1,0:T(8,128)(2,1)S(1)} collective-permute-done((bf16[80,512]{1,0:T(8,128)(2,1)S(1)}, bf16[80,512]{1,0:T(8,128)(2,1)S(1)}, u32[]{:S(2)}, u32[]{:S(2)}) %collective-permute-start.5) | collective-permute-done | bytes 81952 | tf_op jit(solution)/shard_map/ppermute | solution.py:241
  21.4 0.0 collective-permute-done.3.front.refs_2_
  21.4 0.0 collective-permute-done.2.side.refs_1_
  21.4 0.1 collective-permute-start.8
  21.5 1.1 %collective-permute-done.6.refs_5_ = bf16[16,512]{1,0:T(8,128)(2,1)S(1)} collective-permute-done((bf16[16,512]{1,0:T(8,128)(2,1)S(1)}, bf16[16,512]{1,0:T(8,128)(2,1)S(1)}, u32[]{:S(2)}, u32[]{:S(2)}) %collective-permute-start.6) | collective-permute-done | bytes 16416 | tf_op jit(solution)/shard_map/ppermute | solution.py:241
  22.7 0.0 collective-permute-done.4.across.refs_3_
  22.7 0.1 collective-permute-start.7
  22.8 0.3 %ready.1 = (bf16[512,512]{1,0:T(8,128)(2,1)S(1)}, bf16[512,512]{1,0:T(8,128)(2,1)S(1)}, bf16[512,512]{1,0:T(8,128)(2,1)S(1)}) custom-call(bf16[512,512]{1,0:T(8,128)(2,1)S(1)} %get-tuple-element.18.near, bf16[208,512]{1,0:T(8,128)(2,1)S(1)} %pad_maximum_fusion.2.line.refs_0_, bf16[208,512]{1,0:T(8,128)(2,1)S(1)} %collective-permute-done.2.side.refs_1_, ...), custom_call_target="tpu_custom_call" | custom-call | tf_op jit(solution)/shard_map/ready/pallas_call | solution.py:309
  23.1 1.4 %collective-permute-done.7.refs_6_ = bf16[368,512]{1,0:T(8,128)(2,1)S(1)} collective-permute-done((bf16[368,512]{1,0:T(8,128)(2,1)S(1)}, bf16[368,512]{1,0:T(8,128)(2,1)S(1)}, u32[]{:S(2)}, u32[]{:S(2)}) %collective-permute-start.7) | collective-permute-done | bytes 376864 | tf_op jit(solution)/shard_map/ppermute | solution.py:241
  24.5 0.0 collective-permute-done.8.refs_7_
  24.5 5.5 %whole.1 = (f32[1,512]{1,0:T(1,128)}, f32[1,128]{1,0:T(1,128)}, f32[1,128]{1,0:T(1,128)}, f32[1,128]{1,0:T(1,128)}, f32[1,2]{1,0:T(1,128)}) custom-call(bf16[512,512]{1,0:T(8,128)(2,1)S(1)} %get-tuple-element.18.near, bf16[512,512]{1,0:T(8,128)(2,1)S(1)} %get-tuple-element.23.near_turned, bf16[512,512]{1,0:T(8,128)(2,1)S(1)} %get-tuple-element.24.mine, ...), custom_call_target="tpu_custom_call" | custom-call | flops 268435456 | bytes 2097152 | tf_op jit(solution)/shard_map/whole/pallas_call | solution.py:317
  (5 shorter events, 0.1 us)
Async XLA Ops:
  1.6 10.2 %collective-permute-start = (bf16[128,512]{1,0:T(8,128)(2,1)S(1)}, bf16[128,512]{1,0:T(8,128)(2,1)S(1)}, u32[]{:S(2)}, u32[]{:S(2)}) collective-permute-start(bf16[128,512]{1,0:T(8,128)(2,1)S(1)} %constant_dynamic-slice_fusion.1), channel_id=1, source_target_pairs={{0,1},{1,0},{2,3},{3,2},{4,6},{5,7},{6,4},{7,5},{8,9},{9,8},{10,11... | collective-permute-start | bytes 393224 | tf_op jit(solution)/shard_map/ppermute | solution.py:241
  4.6 3.2 %copy-start.3 = (f32[512]{0:T(512)S(1)}, f32[512]{0:T(512)}, u32[]{:S(2)}) copy-start(f32[512]{0:T(512)} %param.10) | copy-start | bytes 6148
  4.6 3.3 %copy-start.4 = (f32[1,512]{1,0:T(1,128)S(1)}, f32[1,512]{1,0:T(1,128)}, u32[]{:S(2)}) copy-start(f32[1,512]{1,0:T(1,128)} %demand.1) | copy-start | bytes 6148
  4.7 7.1 %collective-permute-start.1 = (bf16[64,512]{1,0:T(8,128)(2,1)S(1)}, bf16[64,512]{1,0:T(8,128)(2,1)S(1)}, u32[]{:S(2)}, u32[]{:S(2)}) collective-permute-start(bf16[64,512]{1,0:T(8,128)(2,1)S(1)} %constant_dynamic-slice_fusion), channel_id=1, source_target_pairs={{0,3},{1,2},{2,1},{3,0},{4,7},{5,6},{6,5},{7,4},{8,11},{9,10},{10,... | collective-permute-start | bytes 196616 | tf_op jit(solution)/shard_map/ppermute | solution.py:241
  7.9 0.7 %copy-start.2 = (f32[512]{0:T(512)S(1)}, f32[512]{0:T(512)}, u32[]{:S(2)}) copy-start(f32[512]{0:T(512)} %param.9) | copy-start | bytes 6148
  7.9 0.7 %copy-start.1 = (s32[4,4]{1,0:T(4,128)S(1)}, s32[4,4]{1,0:T(4,128)}, u32[]{:S(2)}) copy-start(s32[4,4]{1,0:T(4,128)} %incidence.1) | copy-start | bytes 196
  7.9 0.7 %copy-start.5 = (s32[128]{0:T(128)S(1)}, s32[128]{0:T(128)}, u32[]{:S(2)}) copy-start(s32[128]{0:T(128)} %param.13) | copy-start | bytes 1540
  8.6 1.0 %copy-start = (bf16[512,512]{1,0:T(8,128)(2,1)S(1)}, bf16[512,512]{1,0:T(8,128)(2,1)}, u32[]{:S(2)}) copy-start(bf16[512,512]{1,0:T(8,128)(2,1)} %coupling.1) | copy-start | bytes 1572868
  11.8 9.6 %collective-permute-start.3 = (bf16[208,512]{1,0:T(8,128)(2,1)S(1)}, bf16[208,512]{1,0:T(8,128)(2,1)S(1)}, u32[]{:S(2)}, u32[]{:S(2)}) collective-permute-start(bf16[208,512]{1,0:T(8,128)(2,1)S(1)} %pad_maximum_fusion.2.line.refs_0_), channel_id=1, source_target_pairs={{0,16},{1,17},{2,18},{3,19},{4,20},{5,21},{6,22},{7,23},{8,24},{9,... | collective-permute-start | bytes 638984 | tf_op jit(solution)/shard_map/ppermute | solution.py:241
  13.4 8.0 %collective-permute-start.2 = (bf16[208,512]{1,0:T(8,128)(2,1)S(1)}, bf16[208,512]{1,0:T(8,128)(2,1)S(1)}, u32[]{:S(2)}, u32[]{:S(2)}) collective-permute-start(bf16[208,512]{1,0:T(8,128)(2,1)S(1)} %pad_maximum_fusion.2.line.refs_0_), channel_id=1, source_target_pairs={{0,8},{1,9},{2,10},{3,11},{4,12},{5,13},{6,14},{7,15},{8,0},{9,1},... | collective-permute-start | bytes 638984 | tf_op jit(solution)/shard_map/ppermute | solution.py:241
  14.9 6.5 %collective-permute-start.5 = (bf16[80,512]{1,0:T(8,128)(2,1)S(1)}, bf16[80,512]{1,0:T(8,128)(2,1)S(1)}, u32[]{:S(2)}, u32[]{:S(2)}) collective-permute-start(bf16[80,512]{1,0:T(8,128)(2,1)S(1)} %pad_maximum_fusion.3), channel_id=1, source_target_pairs={{0,24},{1,25},{2,26},{3,27},{4,28},{5,29},{6,30},{7,31},{8,16},{9,... | collective-permute-start | bytes 245768 | tf_op jit(solution)/shard_map/ppermute | solution.py:241
  15.4 7.3 %collective-permute-start.4 = (bf16[144,512]{1,0:T(8,128)(2,1)S(1)}, bf16[144,512]{1,0:T(8,128)(2,1)S(1)}, u32[]{:S(2)}, u32[]{:S(2)}) collective-permute-start(bf16[144,512]{1,0:T(8,128)(2,1)S(1)} %get-tuple-element.22), channel_id=1, source_target_pairs={{0,1},{1,0},{2,3},{3,2},{4,6},{5,7},{6,4},{7,5},{8,9},{9,8},{10,11... | collective-permute-start | bytes 442376 | tf_op jit(solution)/shard_map/ppermute | solution.py:241
  16.0 6.7 %collective-permute-start.6 = (bf16[16,512]{1,0:T(8,128)(2,1)S(1)}, bf16[16,512]{1,0:T(8,128)(2,1)S(1)}, u32[]{:S(2)}, u32[]{:S(2)}) collective-permute-start(bf16[16,512]{1,0:T(8,128)(2,1)S(1)} %get-tuple-element.19), channel_id=1, source_target_pairs={{0,3},{1,2},{2,1},{3,0},{4,7},{5,6},{6,5},{7,4},{8,11},{9,10},{10,... | collective-permute-start | bytes 49160 | tf_op jit(solution)/shard_map/ppermute | solution.py:241
  21.4 3.0 %collective-permute-start.8 = (bf16[496,512]{1,0:T(8,128)(2,1)S(1)}, bf16[496,512]{1,0:T(8,128)(2,1)S(1)}, u32[]{:S(2)}, u32[]{:S(2)}) collective-permute-start(bf16[496,512]{1,0:T(8,128)(2,1)S(1)} %pad_maximum_fusion), channel_id=1, source_target_pairs={{0,4},{1,5},{2,6},{3,7},{4,0},{5,1},{6,2},{7,3},{8,12},{9,13},{10,... | collective-permute-start | bytes 1523720 | tf_op jit(solution)/shard_map/ppermute | solution.py:241
  22.7 1.8 %collective-permute-start.7 = (bf16[368,512]{1,0:T(8,128)(2,1)S(1)}, bf16[368,512]{1,0:T(8,128)(2,1)S(1)}, u32[]{:S(2)}, u32[]{:S(2)}) collective-permute-start(bf16[368,512]{1,0:T(8,128)(2,1)S(1)} %pad_maximum_fusion.1), channel_id=1, source_target_pairs={{0,4},{1,5},{2,6},{3,7},{4,0},{5,1},{6,2},{7,3},{8,12},{9,13},{10,... | collective-permute-start | bytes 1130504 | tf_op jit(solution)/shard_map/ppermute | solution.py:241

commit v11 on v10

--- a/solution.py
+++ b/solution.py
@@ -87,12 +87,24 @@
     block_arcs = cost.shape[1] // blocks
     weight_sum = jnp.sum(share[:, :1], axis=0, keepdims=True)
     spreads = []
+    held = {}
+
+    def load_state(name, ref, cols):
+        return held[name, cols.start] if joined > 1 else ref[:, cols]
+
+    def store_state(name, ref, cols, value):
+        if joined > 1:
+            held[name, cols.start] = value
+        else:
+            ref[:, cols] = value
+
+    rows = slice(0, total_rows)
     for round_index in range(ROUNDS):
         for step_index in range(ITERS):
             first = round_index == 0 and step_index == 0
             load = jnp.zeros((scenarios, total_rows), jnp.float32)
             if not first:
-                duals_low = duals[...].astype(jnp.bfloat16)
+                duals_low = load_state("duals", duals, rows).astype(jnp.bfloat16)
             for start in range(0, blocks, joined):
                 group = range(start, start + joined)
                 if not first:
@@ -105,33 +117,40 @@
                         gradient = jnp.broadcast_to(cost[:, cols], (scenarios, block_arcs))
                         old = jnp.zeros((scenarios, block_arcs), jnp.float32)
                     else:
-                        old = flows[:, cols]
+                        old = load_state("flows", flows, cols)
                         pull = pulls[:, (block - start) * block_arcs:(block - start + 1) * block_arcs]
                         push = penalty * mask[:, cols] * old
                         if round_index > 0:
-                            push = push + shifted[:, cols]
+                            push = push + load_state("shifted", shifted, cols)
                         gradient = cost[:, cols] + pull + push
                     new = jnp.clip(old - primal_step * gradient, 0.0, cap[:, cols])
-                    flows[:, cols] = new
+                    store_state("flows", flows, cols, new)
                     bars.append((2.0 * new - old).astype(jnp.bfloat16))
                 weights = jnp.concatenate([turned(block) for block in group], axis=0)
                 load = load + jnp.dot(jnp.concatenate(bars, axis=1), weights, preferred_element_type=jnp.float32)
             step = dual_step * (load - demand[...])
-            duals[...] = jnp.maximum(step if first else duals[...] + step, 0.0)
+            if not first:
+                step = load_state("duals", duals, rows) + step
+            store_state("duals", duals, rows, jnp.maximum(step, 0.0))
         squares = jnp.zeros((1, block_arcs), jnp.float32)
         for block in range(blocks):
             cols = slice(block * block_arcs, (block + 1) * block_arcs)
-            fleet = flows[:, cols] * mask[:, cols]
+            fleet = load_state("flows", flows, cols) * mask[:, cols]
             share_col = share[:, :1]
             mean = jnp.sum(share_col * fleet, axis=0, keepdims=True) / weight_sum
             gap = fleet - mean
             squares = squares + jnp.sum(share_col * gap * gap, axis=0, keepdims=True)
-            total = penalty * gap if round_index == 0 else prices[:, cols] + penalty * gap
-            prices[:, cols] = total
+            total = penalty * gap
+            if round_index > 0:
+                total = load_state("prices", prices, cols) + total
+            store_state("prices", prices, cols, total)
             centre[:, cols] = mean
-            shifted[:, cols] = total - penalty * mean
+            store_state("shifted", shifted, cols, total - penalty * mean)
         squares = jnp.sum(squares, axis=1, keepdims=True)
         spreads.append(jnp.sqrt(squares / (weight_sum * fleet_count) + 1e-06))
+    refs = {"flows": flows, "duals": duals, "prices": prices, "shifted": shifted}
+    for (name, start), value in held.items():
+        refs[name][:, start:start + value.shape[1]] = value
     lanes = lax.broadcasted_iota(jnp.int32, spread_out.shape, 1)
     spread = jnp.broadcast_to(spreads[0], spread_out.shape)
     for round_index in range(1, ROUNDS):

time: 30.2 us -> 30.2 us (level)
  no operation moved by 1% of the time
where the time goes in v11:
time: 30.2 us; the launch traced here: 30 us
  starting transfers between devices  13.2 us (44%)
  Pallas kernels  7.35 us (24%)
  waiting for transfers between devices  5.36 us (18%)
  local copies, waits for them, and re-layouts  2.63 us (9%)
  between operations  1.39 us (5%)
    ppermute x9, starting transfers between devices, swap(): return lax.ppermute(value, ('scen', 'arc'), pairs)  13.2 us
    pallas_call x1, Pallas kernels, body(): pl.pallas_call(whole_kernel, out_shape=out_shape, in_specs=[VMEM] * (len(...  5.5 us
    ppermute x9, waiting for transfers between devices, swap(): return lax.ppermute(value, ('scen', 'arc'), pairs)  5.36 us
    unnamed x12, local copies, waits for them, and re-layouts  1.71 us
    pallas_call x1, Pallas kernels, body(): pl.pallas_call(pack_kernel, out_shape=(like(total_rows), like(TILE + EXTR...  1.52 us
    dynamic_slice x1, local copies, waits for them, and re-layouts, bring(): lax.dynamic_slice_in_dim(coupling, lax.shift_right_logical(scen, 1) * TIL...  0.92 us
  transfers between devices with their start and end apart: 9, of which 4 were waited for; matrix products, arithmetic and copies ran while one was open for 0% of the time, Pallas kernels for 6%

profile of v11, /device:TPU:0, one launch (start us, length us, event | category | flops | bytes accessed | tf_op | source)
XLA Modules:
  0.0 30.0 jit_solution(17832271562031379620)
XLA Ops:
  0.6 0.9 %constant_dynamic-slice_fusion.1 = bf16[128,512]{1,0:T(8,128)(2,1)S(1)} fusion(bf16[512,512]{1,0:T(8,128)(2,1)} %coupling.1, s32[]{:T(128)S(6)} %select_n.6), kind=kLoop, calls=%fused_computation.5 | loop fusion | bytes 262148 | tf_op jit(solution)/shard_map/dynamic_slice | solution.py:266
  1.6 3.1 %collective-permute-start = (bf16[128,512]{1,0:T(8,128)(2,1)S(1)}, bf16[128,512]{1,0:T(8,128)(2,1)S(1)}, u32[]{:S(2)}, u32[]{:S(2)}) collective-permute-start(bf16[128,512]{1,0:T(8,128)(2,1)S(1)} %constant_dynamic-slice_fusion.1), channel_id=1, source_target_pairs={{0,1},{1,0},{2,3},{3,2},{4,6},{5,7},{6,4},{7,5},{8,9},{9,8},{10,11... | collective-permute-start | bytes 393224 | tf_op jit(solution)/shard_map/ppermute | solution.py:260
  4.6 0.0 copy-start.3
  4.6 0.0 copy-start.4
  4.7 2.5 %collective-permute-start.1 = (bf16[64,512]{1,0:T(8,128)(2,1)S(1)}, bf16[64,512]{1,0:T(8,128)(2,1)S(1)}, u32[]{:S(2)}, u32[]{:S(2)}) collective-permute-start(bf16[64,512]{1,0:T(8,128)(2,1)S(1)} %constant_dynamic-slice_fusion), channel_id=1, source_target_pairs={{0,3},{1,2},{2,1},{3,0},{4,7},{5,6},{6,5},{7,4},{8,11},{9,10},{10,... | collective-permute-start | bytes 196616 | tf_op jit(solution)/shard_map/ppermute | solution.py:260
  7.9 0.0 copy-start.2
  7.9 0.0 copy-start.1
  7.9 0.0 copy-start.5
  7.9 0.0 copy-done.3
  7.9 0.0 copy-done.4
  7.9 0.6 %copy-done.2 = f32[512]{0:T(512)S(1)} copy-done((f32[512]{0:T(512)S(1)}, f32[512]{0:T(512)}, u32[]{:S(2)}) %copy-start.2) | copy-done | bytes 2072
  8.5 0.0 copy-done.1
  8.6 0.0 copy-done.5
  8.6 0.0 copy-start
  8.6 1.0 %copy-done = bf16[512,512]{1,0:T(8,128)(2,1)S(1)} copy-done((bf16[512,512]{1,0:T(8,128)(2,1)S(1)}, bf16[512,512]{1,0:T(8,128)(2,1)}, u32[]{:S(2)}) %copy-start) | copy-done | bytes 524312
  9.6 1.5 %pack.1 = (bf16[512,512]{1,0:T(8,128)(2,1)S(1)}, bf16[144,512]{1,0:T(8,128)(2,1)S(1)}, bf16[16,512]{1,0:T(8,128)(2,1)S(1)}) custom-call(bf16[512,512]{1,0:T(8,128)(2,1)S(1)} %copy-done, s32[4,4]{1,0:T(4,128)S(1)} %copy-done.1, f32[1,512]{1,0:T(1,128)S(1)} %bitcast.7, f32[1,512]{1,0:T(1,128)S(1)} %bitcast.8, f32[1,512]{1,0:T(1,128)S(1)} %copy-done.4, ...), custom_call_target="tpu_custom_call" | custom-call | tf_op jit(solution)/shard_map/pack/pallas_call | solution.py:314
  11.1 0.6 %collective-permute-done.1 = bf16[64,512]{1,0:T(8,128)(2,1)S(1)} collective-permute-done((bf16[64,512]{1,0:T(8,128)(2,1)S(1)}, bf16[64,512]{1,0:T(8,128)(2,1)S(1)}, u32[]{:S(2)}, u32[]{:S(2)}) %collective-permute-start.1) | collective-permute-done | bytes 65568 | tf_op jit(solution)/shard_map/ppermute | solution.py:260
  11.8 0.0 collective-permute-done
  11.8 1.6 %collective-permute-start.3 = (bf16[208,512]{1,0:T(8,128)(2,1)S(1)}, bf16[208,512]{1,0:T(8,128)(2,1)S(1)}, u32[]{:S(2)}, u32[]{:S(2)}) collective-permute-start(bf16[208,512]{1,0:T(8,128)(2,1)S(1)} %pad_maximum_fusion.2.line.refs_0_), channel_id=1, source_target_pairs={{0,16},{1,17},{2,18},{3,19},{4,20},{5,21},{6,22},{7,23},{8,24},{9,... | collective-permute-start | bytes 638984 | tf_op jit(solution)/shard_map/ppermute | solution.py:260
  13.4 1.5 %collective-permute-start.2 = (bf16[208,512]{1,0:T(8,128)(2,1)S(1)}, bf16[208,512]{1,0:T(8,128)(2,1)S(1)}, u32[]{:S(2)}, u32[]{:S(2)}) collective-permute-start(bf16[208,512]{1,0:T(8,128)(2,1)S(1)} %pad_maximum_fusion.2.line.refs_0_), channel_id=1, source_target_pairs={{0,8},{1,9},{2,10},{3,11},{4,12},{5,13},{6,14},{7,15},{8,0},{9,1},... | collective-permute-start | bytes 638984 | tf_op jit(solution)/shard_map/ppermute | solution.py:260
  14.9 0.5 %collective-permute-start.5 = (bf16[80,512]{1,0:T(8,128)(2,1)S(1)}, bf16[80,512]{1,0:T(8,128)(2,1)S(1)}, u32[]{:S(2)}, u32[]{:S(2)}) collective-permute-start(bf16[80,512]{1,0:T(8,128)(2,1)S(1)} %pad_maximum_fusion.3), channel_id=1, source_target_pairs={{0,24},{1,25},{2,26},{3,27},{4,28},{5,29},{6,30},{7,31},{8,16},{9,... | collective-permute-start | bytes 245768 | tf_op jit(solution)/shard_map/ppermute | solution.py:260
  15.4 0.6 %collective-permute-start.4 = (bf16[144,512]{1,0:T(8,128)(2,1)S(1)}, bf16[144,512]{1,0:T(8,128)(2,1)S(1)}, u32[]{:S(2)}, u32[]{:S(2)}) collective-permute-start(bf16[144,512]{1,0:T(8,128)(2,1)S(1)} %get-tuple-element.22), channel_id=1, source_target_pairs={{0,1},{1,0},{2,3},{3,2},{4,6},{5,7},{6,4},{7,5},{8,9},{9,8},{10,11... | collective-permute-start | bytes 442376 | tf_op jit(solution)/shard_map/ppermute | solution.py:260
  16.0 3.2 %collective-permute-start.6 = (bf16[16,512]{1,0:T(8,128)(2,1)S(1)}, bf16[16,512]{1,0:T(8,128)(2,1)S(1)}, u32[]{:S(2)}, u32[]{:S(2)}) collective-permute-start(bf16[16,512]{1,0:T(8,128)(2,1)S(1)} %get-tuple-element.19), channel_id=1, source_target_pairs={{0,3},{1,2},{2,1},{3,0},{4,7},{5,6},{6,5},{7,4},{8,11},{9,10},{10,... | collective-permute-start | bytes 49160 | tf_op jit(solution)/shard_map/ppermute | solution.py:260
  19.2 2.2 %collective-permute-done.5.refs_4_ = bf16[80,512]{1,0:T(8,128)(2,1)S(1)} collective-permute-done((bf16[80,512]{1,0:T(8,128)(2,1)S(1)}, bf16[80,512]{1,0:T(8,128)(2,1)S(1)}, u32[]{:S(2)}, u32[]{:S(2)}) %collective-permute-start.5) | collective-permute-done | bytes 81952 | tf_op jit(solution)/shard_map/ppermute | solution.py:260
  21.4 0.0 collective-permute-done.3.front.refs_2_
  21.4 0.0 collective-permute-done.2.side.refs_1_
  21.4 0.1 collective-permute-start.8
  21.5 1.1 %collective-permute-done.6.refs_5_ = bf16[16,512]{1,0:T(8,128)(2,1)S(1)} collective-permute-done((bf16[16,512]{1,0:T(8,128)(2,1)S(1)}, bf16[16,512]{1,0:T(8,128)(2,1)S(1)}, u32[]{:S(2)}, u32[]{:S(2)}) %collective-permute-start.6) | collective-permute-done | bytes 16416 | tf_op jit(solution)/shard_map/ppermute | solution.py:260
  22.7 0.0 collective-permute-done.4.across.refs_3_
  22.7 0.1 collective-permute-start.7
  22.8 0.3 %ready.1 = (bf16[512,512]{1,0:T(8,128)(2,1)S(1)}, bf16[512,512]{1,0:T(8,128)(2,1)S(1)}, bf16[512,512]{1,0:T(8,128)(2,1)S(1)}) custom-call(bf16[512,512]{1,0:T(8,128)(2,1)S(1)} %get-tuple-element.18.near, bf16[208,512]{1,0:T(8,128)(2,1)S(1)} %pad_maximum_fusion.2.line.refs_0_, bf16[208,512]{1,0:T(8,128)(2,1)S(1)} %collective-permute-done.2.side.refs_1_, ...), custom_call_target="tpu_custom_call" | custom-call | tf_op jit(solution)/shard_map/ready/pallas_call | solution.py:328
  23.1 1.4 %collective-permute-done.7.refs_6_ = bf16[368,512]{1,0:T(8,128)(2,1)S(1)} collective-permute-done((bf16[368,512]{1,0:T(8,128)(2,1)S(1)}, bf16[368,512]{1,0:T(8,128)(2,1)S(1)}, u32[]{:S(2)}, u32[]{:S(2)}) %collective-permute-start.7) | collective-permute-done | bytes 376864 | tf_op jit(solution)/shard_map/ppermute | solution.py:260
  24.5 0.0 collective-permute-done.8.refs_7_
  24.5 5.5 %whole.1 = (f32[1,512]{1,0:T(1,128)}, f32[1,128]{1,0:T(1,128)}, f32[1,128]{1,0:T(1,128)}, f32[1,128]{1,0:T(1,128)}, f32[1,2]{1,0:T(1,128)}) custom-call(bf16[512,512]{1,0:T(8,128)(2,1)S(1)} %get-tuple-element.18.near, bf16[512,512]{1,0:T(8,128)(2,1)S(1)} %get-tuple-element.23.near_turned, bf16[512,512]{1,0:T(8,128)(2,1)S(1)} %get-tuple-element.24.mine, ...), custom_call_target="tpu_custom_call" | custom-call | flops 268435456 | bytes 2097152 | tf_op jit(solution)/shard_map/whole/pallas_call | solution.py:336
  (5 shorter events, 0.1 us)
Async XLA Ops:
  1.6 10.2 %collective-permute-start = (bf16[128,512]{1,0:T(8,128)(2,1)S(1)}, bf16[128,512]{1,0:T(8,128)(2,1)S(1)}, u32[]{:S(2)}, u32[]{:S(2)}) collective-permute-start(bf16[128,512]{1,0:T(8,128)(2,1)S(1)} %constant_dynamic-slice_fusion.1), channel_id=1, source_target_pairs={{0,1},{1,0},{2,3},{3,2},{4,6},{5,7},{6,4},{7,5},{8,9},{9,8},{10,11... | collective-permute-start | bytes 393224 | tf_op jit(solution)/shard_map/ppermute | solution.py:260
  4.6 3.2 %copy-start.3 = (f32[512]{0:T(512)S(1)}, f32[512]{0:T(512)}, u32[]{:S(2)}) copy-start(f32[512]{0:T(512)} %param.10) | copy-start | bytes 6148
  4.6 3.3 %copy-start.4 = (f32[1,512]{1,0:T(1,128)S(1)}, f32[1,512]{1,0:T(1,128)}, u32[]{:S(2)}) copy-start(f32[1,512]{1,0:T(1,128)} %demand.1) | copy-start | bytes 6148
  4.7 7.1 %collective-permute-start.1 = (bf16[64,512]{1,0:T(8,128)(2,1)S(1)}, bf16[64,512]{1,0:T(8,128)(2,1)S(1)}, u32[]{:S(2)}, u32[]{:S(2)}) collective-permute-start(bf16[64,512]{1,0:T(8,128)(2,1)S(1)} %constant_dynamic-slice_fusion), channel_id=1, source_target_pairs={{0,3},{1,2},{2,1},{3,0},{4,7},{5,6},{6,5},{7,4},{8,11},{9,10},{10,... | collective-permute-start | bytes 196616 | tf_op jit(solution)/shard_map/ppermute | solution.py:260
  7.9 0.7 %copy-start.2 = (f32[512]{0:T(512)S(1)}, f32[512]{0:T(512)}, u32[]{:S(2)}) copy-start(f32[512]{0:T(512)} %param.9) | copy-start | bytes 6148
  7.9 0.7 %copy-start.1 = (s32[4,4]{1,0:T(4,128)S(1)}, s32[4,4]{1,0:T(4,128)}, u32[]{:S(2)}) copy-start(s32[4,4]{1,0:T(4,128)} %incidence.1) | copy-start | bytes 196
  7.9 0.7 %copy-start.5 = (s32[128]{0:T(128)S(1)}, s32[128]{0:T(128)}, u32[]{:S(2)}) copy-start(s32[128]{0:T(128)} %param.13) | copy-start | bytes 1540
  8.6 1.0 %copy-start = (bf16[512,512]{1,0:T(8,128)(2,1)S(1)}, bf16[512,512]{1,0:T(8,128)(2,1)}, u32[]{:S(2)}) copy-start(bf16[512,512]{1,0:T(8,128)(2,1)} %coupling.1) | copy-start | bytes 1572868
  11.8 9.6 %collective-permute-start.3 = (bf16[208,512]{1,0:T(8,128)(2,1)S(1)}, bf16[208,512]{1,0:T(8,128)(2,1)S(1)}, u32[]{:S(2)}, u32[]{:S(2)}) collective-permute-start(bf16[208,512]{1,0:T(8,128)(2,1)S(1)} %pad_maximum_fusion.2.line.refs_0_), channel_id=1, source_target_pairs={{0,16},{1,17},{2,18},{3,19},{4,20},{5,21},{6,22},{7,23},{8,24},{9,... | collective-permute-start | bytes 638984 | tf_op jit(solution)/shard_map/ppermute | solution.py:260
  13.4 8.0 %collective-permute-start.2 = (bf16[208,512]{1,0:T(8,128)(2,1)S(1)}, bf16[208,512]{1,0:T(8,128)(2,1)S(1)}, u32[]{:S(2)}, u32[]{:S(2)}) collective-permute-start(bf16[208,512]{1,0:T(8,128)(2,1)S(1)} %pad_maximum_fusion.2.line.refs_0_), channel_id=1, source_target_pairs={{0,8},{1,9},{2,10},{3,11},{4,12},{5,13},{6,14},{7,15},{8,0},{9,1},... | collective-permute-start | bytes 638984 | tf_op jit(solution)/shard_map/ppermute | solution.py:260
  14.9 6.5 %collective-permute-start.5 = (bf16[80,512]{1,0:T(8,128)(2,1)S(1)}, bf16[80,512]{1,0:T(8,128)(2,1)S(1)}, u32[]{:S(2)}, u32[]{:S(2)}) collective-permute-start(bf16[80,512]{1,0:T(8,128)(2,1)S(1)} %pad_maximum_fusion.3), channel_id=1, source_target_pairs={{0,24},{1,25},{2,26},{3,27},{4,28},{5,29},{6,30},{7,31},{8,16},{9,... | collective-permute-start | bytes 245768 | tf_op jit(solution)/shard_map/ppermute | solution.py:260
  15.4 7.3 %collective-permute-start.4 = (bf16[144,512]{1,0:T(8,128)(2,1)S(1)}, bf16[144,512]{1,0:T(8,128)(2,1)S(1)}, u32[]{:S(2)}, u32[]{:S(2)}) collective-permute-start(bf16[144,512]{1,0:T(8,128)(2,1)S(1)} %get-tuple-element.22), channel_id=1, source_target_pairs={{0,1},{1,0},{2,3},{3,2},{4,6},{5,7},{6,4},{7,5},{8,9},{9,8},{10,11... | collective-permute-start | bytes 442376 | tf_op jit(solution)/shard_map/ppermute | solution.py:260
  16.0 6.7 %collective-permute-start.6 = (bf16[16,512]{1,0:T(8,128)(2,1)S(1)}, bf16[16,512]{1,0:T(8,128)(2,1)S(1)}, u32[]{:S(2)}, u32[]{:S(2)}) collective-permute-start(bf16[16,512]{1,0:T(8,128)(2,1)S(1)} %get-tuple-element.19), channel_id=1, source_target_pairs={{0,3},{1,2},{2,1},{3,0},{4,7},{5,6},{6,5},{7,4},{8,11},{9,10},{10,... | collective-permute-start | bytes 49160 | tf_op jit(solution)/shard_map/ppermute | solution.py:260
  21.4 3.0 %collective-permute-start.8 = (bf16[496,512]{1,0:T(8,128)(2,1)S(1)}, bf16[496,512]{1,0:T(8,128)(2,1)S(1)}, u32[]{:S(2)}, u32[]{:S(2)}) collective-permute-start(bf16[496,512]{1,0:T(8,128)(2,1)S(1)} %pad_maximum_fusion), channel_id=1, source_target_pairs={{0,4},{1,5},{2,6},{3,7},{4,0},{5,1},{6,2},{7,3},{8,12},{9,13},{10,... | collective-permute-start | bytes 1523720 | tf_op jit(solution)/shard_map/ppermute | solution.py:260
  22.7 1.8 %collective-permute-start.7 = (bf16[368,512]{1,0:T(8,128)(2,1)S(1)}, bf16[368,512]{1,0:T(8,128)(2,1)S(1)}, u32[]{:S(2)}, u32[]{:S(2)}) collective-permute-start(bf16[368,512]{1,0:T(8,128)(2,1)S(1)} %pad_maximum_fusion.1), channel_id=1, source_target_pairs={{0,4},{1,5},{2,6},{3,7},{4,0},{5,1},{6,2},{7,3},{8,12},{9,13},{10,... | collective-permute-start | bytes 1130504 | tf_op jit(solution)/shard_map/ppermute | solution.py:260
